TPU v7x, 1024 devices: a whole 4x8x16 slice. The times are simulated.
1024 devices in a mesh: replica: 32 (over x, y_hi, core), mp: 32 (over z, y_lo).
Axes of the slice: x: 4, y: 8 (y_hi: 4, y_lo: 2; y = y_hi * 2 + y_lo), z: 16, core: 2. Of those that a mesh axis runs over, the one named last changes fastest.
Arguments:
- table: float32 [32768, 256], P('mp'), may hold values from -0.6 to 0.6
- row_ids: int32 [32, 128], P('mp'), may hold values from 0 to 1023, as said below
- pool_counts: int32 [131072, 4096], P('replica', 'mp'), may hold values from 0 to 3
- table_of: int32 [32], replicated, may hold values from 0 to 7, as said below
- dense_feat: bfloat16 [13, 131072], P(None, ('replica', 'mp')), may hold values from -6 to 6
- labels: int32 [131072], P(('replica', 'mp')), may hold values 0 or 1
- w_bottom1: bfloat16 [13, 512], replicated, may hold values from -1.75 to 1.75
- w_bottom2: bfloat16 [512, 256], replicated, may hold values from -0.25 to 0.25
- cross_down: bfloat16 [2304, 256], replicated, may hold values from -0.125 to 0.125
- cross_up: bfloat16 [256, 2304], replicated, may hold values from -0.375 to 0.375
- w_top1: bfloat16 [2304, 512], replicated, may hold values from -0.125 to 0.125
- w_top2: bfloat16 [512, 512], replicated, may hold values from -0.25 to 0.25
- w_out: float32 [512], replicated, may hold values from -0.25 to 0.25
Outputs:
- row_grads: float32 [128, 8192], P('replica', 'mp')
- logits: float32 [131072], P(('replica', 'mp'))
Inputs may be any that keep to these rules, and one draw needn't show every extreme that they name: `row_ids`: the 128 entries of each row are distinct. `table_of`: each table number appears exactly 4 times.
All inputs are finite; a program needn't handle non-finite values. No bound on the sum of `labels` on one device may be relied on, other than what follows from the above.
Results may differ from a plain program's by a relative error of at most 0.0084.
Values may be sent and summed in bfloat16 or wider, within the bound.
No kernel may reach another device: no remote copies, remote signals or barrier semaphores. Data moves between devices by JAX's collectives and lax.ppermute only.
A program may use at most 32 MiB of HBM per device.

v0:
```python
import jax
import jax.numpy as jnp
from jax import lax
from jax.sharding import PartitionSpec as P


def silu_slope(value):
    sig = jax.nn.sigmoid(value)
    return sig + value * sig * (1.0 - sig)


def row_terms(counts_bf, pooled_grad):
    return lax.dot_general(
        counts_bf, pooled_grad, (((0,), (0,)), ((), ())), preferred_element_type=jnp.float32
    )


def shards(
    table,
    row_ids,
    pool_counts,
    table_of,
    dense_feat,
    labels,
    w_bottom1,
    w_bottom2,
    cross_down,
    cross_up,
    w_top1,
    w_top2,
    w_out,
):
    mp_count = lax.axis_size("mp")
    group_count = lax.axis_size("replica")
    emb_width = table.shape[1]
    samples = dense_feat.shape[1]
    shard_count = max(1, mp_count // 8)
    table_count = mp_count // shard_count
    looked = jnp.take(table, row_ids[0], axis=0)
    counts_f = pool_counts.astype(jnp.float32)
    pooled_part = jnp.dot(
        counts_f, looked, precision=lax.Precision.HIGHEST, preferred_element_type=jnp.float32
    )
    pooled_part = pooled_part.astype(jnp.bfloat16).reshape(mp_count, samples, emb_width)
    onehot = (table_of[:, None] == jnp.arange(table_count, dtype=jnp.int32)[None, :]).astype(
        jnp.bfloat16
    )
    pooled_emb = jnp.einsum(
        "mbe,mt->bte",
        lax.all_to_all(pooled_part, "mp", split_axis=0, concat_axis=0, tiled=True),
        onehot,
        preferred_element_type=jnp.float32,
    ).astype(jnp.bfloat16)
    hidden = lax.dot_general(
        dense_feat, w_bottom1, (((0,), (0,)), ((), ())), preferred_element_type=jnp.float32
    )
    hidden = jax.nn.relu(hidden).astype(jnp.bfloat16)
    bottom = jax.nn.relu(jnp.dot(hidden, w_bottom2, preferred_element_type=jnp.float32)).astype(
        jnp.bfloat16
    )
    features = jnp.concatenate(
        [bottom, pooled_emb.reshape(samples, table_count * emb_width)], axis=1
    )
    low_rank = jnp.dot(features, cross_down, preferred_element_type=jnp.float32).astype(
        jnp.bfloat16
    )
    cross_scale = jnp.dot(low_rank, cross_up, preferred_element_type=jnp.float32)
    feat_f = features.astype(jnp.float32)
    crossed = (feat_f * cross_scale + feat_f).astype(jnp.bfloat16)
    pre_one = jnp.dot(crossed, w_top1, preferred_element_type=jnp.float32)
    act_one = jax.nn.silu(pre_one).astype(jnp.bfloat16)
    pre_two = jnp.dot(act_one, w_top2, preferred_element_type=jnp.float32)
    logits = jnp.sum(jax.nn.silu(pre_two) * w_out[None, :], axis=1)
    logit_grad = (jax.nn.sigmoid(logits) - labels.astype(jnp.float32)) / group_count
    grad_two = (logit_grad[:, None] * w_out[None, :] * silu_slope(pre_two)).astype(jnp.bfloat16)
    grad_act = lax.dot_general(
        grad_two, w_top2, (((1,), (1,)), ((), ())), preferred_element_type=jnp.float32
    )
    grad_one = (grad_act * silu_slope(pre_one)).astype(jnp.bfloat16)
    crossed_grad = lax.dot_general(
        grad_one, w_top1, (((1,), (1,)), ((), ())), preferred_element_type=jnp.float32
    )
    scale_grad = (crossed_grad * feat_f).astype(jnp.bfloat16)
    low_grad = lax.dot_general(
        scale_grad, cross_up, (((1,), (1,)), ((), ())), preferred_element_type=jnp.float32
    ).astype(jnp.bfloat16)
    back_proj = lax.dot_general(
        low_grad,
        cross_down[emb_width:],
        (((1,), (1,)), ((), ())),
        preferred_element_type=jnp.float32,
    )
    emb_grad = crossed_grad[:, emb_width:] * (cross_scale[:, emb_width:] + 1.0) + back_proj
    emb_grad = emb_grad.astype(jnp.bfloat16).reshape(samples, table_count, emb_width)
    grad_blocks = jnp.einsum(
        "bte,mt->mbe", emb_grad, onehot, preferred_element_type=jnp.float32
    ).astype(jnp.bfloat16)
    counts_bf = pool_counts.astype(jnp.bfloat16)
    pooled_grad = lax.all_to_all(
        grad_blocks, "mp", split_axis=0, concat_axis=0, tiled=True
    ).reshape(mp_count * samples, emb_width)
    row_grads = lax.psum_scatter(
        row_terms(counts_bf, pooled_grad), "replica", scatter_dimension=0, tiled=True
    )
    return (row_grads, logits)


def solution(mesh):
    return jax.shard_map(
        shards,
        mesh=mesh,
        in_specs=(
            P("mp", None),
            P("mp", None),
            P("replica", "mp"),
            P(),
            P(None, ("replica", "mp")),
            P(("replica", "mp")),
            P(),
            P(),
            P(),
            P(),
            P(),
            P(),
            P(),
        ),
        out_specs=(P("replica", "mp"), P(("replica", "mp"))),
        check_vma=False,
    )
```

profile of v0, /device:TPU:8, one launch (start us, length us, event | category | flops | bytes accessed | tf_op | source)
XLA Modules:
  0.0 543.0 jit_solution(13606410428135349024)
XLA Ops:
  7.2 0.0 copy-start
  7.2 0.8 fusion.49
  8.0 0.7 compare_and_fusion
  8.7 2.0 gather_fusion
  10.6 6.6 %fusion = bf16[4096,256]{0,1:T(8,128)(2,1)} fusion(s32[4096,128]{1,0:T(8,128)} %param.15, f32[128,256]{1,0:T(8,128)S(1)} %gather_fusion, pred[128]{0:T(512)(128)(4,1)S(1)} %compare_and_fusion), kind=kOutput, calls=%fused_computation.2 | convolution fusion | flops 1612218368 | bytes 4325504 | tf_op jit(solution)/shard_map/dot_general | solution.py:41
  17.3 4.1 copy.24
  21.4 20.6 %all-to-all-start = ((bf16[32,128,256]{2,1,0:T(8,128)(2,1)}), bf16[32,128,256]{2,1,0:T(8,128)(2,1)}, u32[]{:S(2)}, u32[]{:S(2)}) async-start(bf16[32,128,256]{2,1,0:T(8,128)(2,1)} %bitcast.36), calls=%async_computation | async-start | bytes 4194304 | tf_op jit(solution)/shard_map/all_to_all | solution.py:50
  41.9 0.0 all-reduce.3.cloned.1.call-start
  42.0 1.0 fusion.15
  43.0 98.2 %all-to-all-done = bf16[32,128,256]{2,1,0:T(8,128)(2,1)} async-done(((bf16[32,128,256]{2,1,0:T(8,128)(2,1)}), bf16[32,128,256]{2,1,0:T(8,128)(2,1)}, u32[]{:S(2)}, u32[]{:S(2)}) %all-to-all-start) | async-done | bytes 2097184 | tf_op jit(solution)/shard_map/all_to_all | solution.py:50
  141.2 0.0 copy-done.6
  141.2 2.8 fusion.5
  144.0 0.9 copy.27
  144.9 2.7 fusion.16
  147.6 0.0 copy-start.7
  147.6 0.0 copy-start.8
  147.6 1.6 fusion.20
  149.2 0.0 copy-start.9
  149.3 1.0 multiply_reduce_fusion
  150.3 3.3 fusion.14
  153.5 4.6 fusion.1
  158.2 1.1 copy.28
  159.3 0.7 convolution_convert_fusion.1
  160.1 1.2 copy.22
  161.3 0.0 copy-start.1
  161.3 102.3 %all_to_all.10 = bf16[32,128,256]{2,1,0:T(8,128)(2,1)S(1)} all-to-all(bf16[32,128,256]{2,1,0:T(8,128)(2,1)S(1)} %copy.22), channel_id=1, replica_groups=mesh['replica'=32,'mp'=32] {'mp'}, dimensions={0} | all-to-all | bytes 4194304 | tf_op jit(solution)/shard_map/all_to_all | solution.py:99
  263.6 1.4 convolution_bitcast_fusion
  265.0 0.0 all-reduce.3.cloned.1.call-update
  265.0 1.3 dynamic-slice
  266.9 267.6 %all-reduce.3.cloned.1.call-done = f32[128,256]{0,1:T(8,128)} async-done(((f32[128,256]{0,1:T(8,128)}), f32[128,256]{0,1:T(8,128)}) %all-reduce.3.cloned.1.call-update) | async-done | bytes 131088
  534.5 1.0 constant_dynamic-slice_fusion
  535.5 0.7 copy.23
  (18 shorter events, 0.0 us)
Async XLA Ops:
  7.2 140.4 %copy-start = (bf16[2304,512]{1,0:T(8,128)(2,1)S(1)}, bf16[2304,512]{1,0:T(8,128)(2,1)}, u32[]{:S(2)}) copy-start(bf16[2304,512]{1,0:T(8,128)(2,1)} %param.23) | copy-start | bytes 7077892
  21.3 20.6 %copy-start.3 = (bf16[512,256]{1,0:T(8,128)(2,1)S(1)}, bf16[512,256]{1,0:T(8,128)(2,1)}, u32[]{:S(2)}) copy-start(bf16[512,256]{1,0:T(8,128)(2,1)} %param.20) | copy-start | bytes 786436
  21.3 20.7 %copy-start.4 = (bf16[13,512]{1,0:T(8,128)(2,1)S(1)}, bf16[13,512]{1,0:T(8,128)(2,1)}, u32[]{:S(2)}) copy-start(bf16[13,512]{1,0:T(8,128)(2,1)} %param.19) | copy-start | bytes 39940
  21.3 20.7 %copy-start.5 = (bf16[13,128]{1,0:T(8,128)(2,1)S(1)}, bf16[13,128]{1,0:T(8,128)(2,1)}, u32[]{:S(2)}) copy-start(bf16[13,128]{1,0:T(8,128)(2,1)} %param.17) | copy-start | bytes 9988
  21.3 119.8 %copy-start.6 = (s32[32]{0:T(128)S(1)}, s32[32]{0:T(128)}, u32[]{:S(2)}) copy-start(s32[32]{0:T(128)} %param.16) | copy-start | bytes 388
  21.4 119.8 %all-to-all-start = ((bf16[32,128,256]{2,1,0:T(8,128)(2,1)}), bf16[32,128,256]{2,1,0:T(8,128)(2,1)}, u32[]{:S(2)}, u32[]{:S(2)}) async-start(bf16[32,128,256]{2,1,0:T(8,128)(2,1)} %bitcast.36), calls=%async_computation | async-start | bytes 4194304 | tf_op jit(solution)/shard_map/all_to_all | solution.py:50
  41.9 492.6 %all-reduce.3.cloned.1.call-start = ((), (), s32[]{:S(2)}) async-start(), calls=%async_computation.2 | async-start | bytes 262144
  147.6 1.6 copy-start.7
  147.6 1.6 copy-start.8
  149.2 1.0 copy-start.2
  149.2 1.0 copy-start.9
  150.2 3.3 copy-start.10
  161.3 102.3 %copy-start.1 = (s32[4096,128]{1,0:T(8,128)S(1)}, s32[4096,128]{1,0:T(8,128)}, u32[]{:S(2)}) copy-start(s32[4096,128]{1,0:T(8,128)} %param.15) | copy-start | bytes 6291460
Sparse Core Ops, SparseCore 0:
  265.1 269.3 all-reduce.2
where the time goes:
time: 544 us; the launch traced here: 543 us
  waiting for transfers between devices  366 us (67%)
  blocking collectives  102 us (19%)
  matrix products  25.7 us (5%)
  starting transfers between devices  20.6 us (4%)
  between operations  14.9 us (3%)
  local copies, waits for them, and re-layouts  12.3 us (2%)
    unnamed x2, waiting for transfers between devices  268 us
    all_to_all x1, blocking collectives, shards(): lax.all_to_all(grad_blocks, 'mp', split_axis=0, concat_axis=0, tiled=True)  102 us
    all_to_all x1, waiting for transfers between devices, shards(): lax.all_to_all(pooled_part, 'mp', split_axis=0, concat_axis=0, tiled=True)  98.2 us
    all_to_all x1, starting transfers between devices, shards(): lax.all_to_all(pooled_part, 'mp', split_axis=0, concat_axis=0, tiled=True)  20.6 us
  transfers between devices with their start and end apart: 2, of which 2 were waited for; matrix products, arithmetic and copies ran while one was open for 0% of the time, Pallas kernels for 0%

commit v1 on v0

v1 whole, which is shorter than its diff:
```python
import functools

import jax
import jax.numpy as jnp
from jax import lax
from jax.experimental import pallas as pl
from jax.experimental.pallas import tpu as pltpu
from jax.sharding import Mesh
from jax.sharding import PartitionSpec as P

X, YH, CORES, Z, YL = 4, 4, 2, 16, 2
REP = ("x", "yh", "c")
MP = ("z", "yl")
SHARDS = Z * YL
TABLES = 8
PER = SHARDS // TABLES
E = 256
N = 128
LOOK = 128
BF = jnp.bfloat16
F32 = jnp.float32


def silu_slope(value, sig):
    return sig + value * sig * (1.0 - sig)


def dot(a, b):
    return jnp.dot(a, b, preferred_element_type=F32)


def dot_nt(a, b):
    return lax.dot_general(a, b, (((1,), (1,)), ((), ())), preferred_element_type=F32)


def dot_tn(a, b):
    return lax.dot_general(a, b, (((0,), (0,)), ((), ())), preferred_element_type=F32)


def step_kernel(
    place,
    table_of,
    counts,
    looked,
    bottom,
    labels,
    cross_down,
    cross_up,
    w_top1,
    w_top2,
    w_out,
    grads,
    logits_out,
    feats,
    scaled,
    emb_grad,
    order,
    filled,
):
    my_x, my_c = place[0], place[1]
    for t in range(TABLES):
        filled[t] = 0
    for m in range(SHARDS):
        t = table_of[m]
        k = filled[t]
        order[t * PER + k] = m
        filled[t] = k + 1

    def cols(k):
        return slice(k * E, (k + 1) * E)

    feats[:, cols(0)] = bottom[...]
    for t in range(TABLES):
        acc = None
        for k in range(PER):
            m = order[t * PER + k]
            rows = jnp.concatenate(
                [
                    looked[lax.bitwise_xor(my_c, c), lax.rem(my_x + X - x, X), m]
                    for c in range(CORES)
                    for x in range(X)
                ],
                axis=0,
            )
            term = dot(counts[m], rows)
            acc = term if acc is None else acc + term
        feats[:, cols(t + 1)] = acc.astype(BF)

    low = dot(feats[...], cross_down[...]).astype(BF)
    pre_one = None
    for k in range(TABLES + 1):
        scale = dot(low, cross_up[:, cols(k)])
        scaled[:, cols(k)] = scale
        feat = feats[:, cols(k)].astype(F32)
        term = dot((feat * scale + feat).astype(BF), w_top1[cols(k), :])
        pre_one = term if pre_one is None else pre_one + term
    sig_one = jax.nn.sigmoid(pre_one)
    pre_two = dot((pre_one * sig_one).astype(BF), w_top2[...])
    sig_two = jax.nn.sigmoid(pre_two)
    head = w_out[...]
    logits = jnp.sum(pre_two * sig_two * head, axis=1, keepdims=True)
    logits_out[...] = logits
    logit_grad = (jax.nn.sigmoid(logits) - labels[...].astype(F32)) * (1.0 / 32.0)
    grad_two = (logit_grad * head * silu_slope(pre_two, sig_two)).astype(BF)
    grad_one = (dot_nt(grad_two, w_top2[...]) * silu_slope(pre_one, sig_one)).astype(BF)
    low_grad = None
    for k in range(TABLES + 1):
        part = dot_nt(grad_one, w_top1[cols(k), :])
        feat = feats[:, cols(k)].astype(F32)
        term = dot_nt((part * feat).astype(BF), cross_up[:, cols(k)])
        low_grad = term if low_grad is None else low_grad + term
        if k > 0:
            scaled[:, cols(k)] = part * (scaled[:, cols(k)] + 1.0)
    low_grad = low_grad.astype(BF)
    for t in range(TABLES):
        back = dot_nt(low_grad, cross_down[cols(t + 1), :])
        emb_grad[t] = (scaled[:, cols(t + 1)] + back).astype(BF)

    def one_shard(m, carry):
        terms = dot_tn(counts[m], emb_grad[table_of[m]]).astype(BF)
        for c in range(CORES):
            for x in range(X):
                at = (c * X + x) * 16
                grads[c, x, m] = terms[at : at + 16]
        return carry

    lax.fori_loop(0, SHARDS, one_shard, 0, unroll=4)


def run_step(place, table_of, *arrays):
    smem = pl.BlockSpec(memory_space=pltpu.SMEM)
    vmem = pl.BlockSpec(memory_space=pltpu.VMEM)
    return pl.pallas_call(
        step_kernel,
        out_shape=(
            jax.ShapeDtypeStruct((CORES, X, SHARDS, 16, E), BF),
            jax.ShapeDtypeStruct((N, 1), F32),
        ),
        in_specs=[smem, smem] + [vmem] * len(arrays),
        out_specs=(vmem, vmem),
        scratch_shapes=[
            pltpu.VMEM((N, (TABLES + 1) * E), BF),
            pltpu.VMEM((N, (TABLES + 1) * E), F32),
            pltpu.VMEM((TABLES, N, E), BF),
            pltpu.SMEM((SHARDS,), jnp.int32),
            pltpu.SMEM((TABLES,), jnp.int32),
        ],
        compiler_params=pltpu.CompilerParams(vmem_limit_bytes=40 * 2**20),
        cost_estimate=pl.CostEstimate(
            flops=3 * 10**9, bytes_accessed=12 * 2**20, transcendentals=2 * 10**5
        ),
    )(place, table_of, *arrays)


def swap(value, axes):
    return lax.all_to_all(value, axes, split_axis=0, concat_axis=0, tiled=True)


def add_up(value):
    return jnp.sum(value.astype(F32), axis=0)


def turn(value, axis, size, shift):
    return lax.ppermute(value, axis, [(i, (i + shift) % size) for i in range(size)])


def shards(
    table,
    row_ids,
    pool_counts,
    table_of,
    dense_feat,
    labels,
    w_bottom1,
    w_bottom2,
    cross_down,
    cross_up,
    w_top1,
    w_top2,
    w_out,
):
    my_x, my_c = lax.axis_index("x"), lax.axis_index("c")
    ids = row_ids[0].reshape(X, YH, CORES, 4).transpose(2, 0, 1, 3)
    ids = lax.dynamic_index_in_dim(ids.reshape(CORES * X, 16), my_c * X + my_x, 0, keepdims=False)
    mine = jnp.take(table, ids, axis=0).astype(BF)
    looked = swap(jnp.broadcast_to(mine, (SHARDS, 16, E)), MP)
    counts = pool_counts.astype(BF).reshape(SHARDS * N, X, YH, CORES, 4)
    counts = counts.transpose(0, 3, 1, 2, 4).reshape(SHARDS, N, LOOK)
    counts, looked = lax.optimization_barrier((counts, looked))
    counts = swap(counts, MP)
    looked = jnp.stack([looked] + [turn(looked, "x", X, k) for k in range(1, X)])
    looked = jnp.stack([looked, turn(looked, "c", CORES, 1)])

    hidden = lax.dot_general(
        dense_feat, w_bottom1, (((0,), (0,)), ((), ())), preferred_element_type=F32
    )
    hidden = jax.nn.relu(hidden).astype(BF)
    bottom = jax.nn.relu(dot(hidden, w_bottom2)).astype(BF)

    place = jnp.stack([my_x, my_c]).astype(jnp.int32)
    grads, logits = run_step(
        place,
        table_of,
        counts,
        looked,
        bottom,
        labels.reshape(N, 1),
        cross_down,
        cross_up,
        w_top1,
        w_top2,
        w_out.reshape(1, -1),
    )
    grads = add_up(swap(grads, "c")).astype(BF)
    grads = add_up(swap(grads, "x")).astype(BF)
    grads = grads.reshape(SHARDS, YH, 4, E).transpose(1, 0, 2, 3)
    grads = add_up(swap(grads, "yh")).astype(BF)
    grads = add_up(swap(grads, MP))
    return grads, logits.reshape(N)


def solution(mesh):
    fine = Mesh(mesh.devices.reshape(X, YH, CORES, Z, YL), REP + MP)
    both = REP + MP
    return jax.shard_map(
        shards,
        mesh=fine,
        in_specs=(
            P(MP, None),
            P(MP, None),
            P(REP, MP),
            P(),
            P(None, both),
            P(both),
            P(),
            P(),
            P(),
            P(),
            P(),
            P(),
            P(),
        ),
        out_specs=(P(REP, MP), P(both)),
        check_vma=False,
    )
```

time: 544 us -> 183 us (0.34)
  waiting for transfers between devices: 366 us -> 66.2 us
  blocking collectives: 102 us -> 41.1 us
  matrix products: 25.7 us -> 1.3 us
  starting transfers between devices: 20.6 us -> 42 us
  between operations: 14.9 us -> 0.85 us
  other arithmetic: 1.49 us -> 9.9 us
  Pallas kernels: 0 us -> 7.74 us
    unnamed x2 -> x0, waiting for transfers between devices: 268 us -> none
    all_to_all x1 -> x3, blocking collectives: 102 us -> 41.1 us  [swap(): return lax.all_to_all(value, axes, split_axis=0, concat_axis=0, tiled=True)]
    all_to_all x1 -> x3, waiting for transfers between devices: 98.2 us -> 55.7 us  [swap(): return lax.all_to_all(value, axes, split_axis=0, concat_axis=0, tiled=True)]
    dot_general x10 -> x1, matrix products: 25.7 us -> 1.3 us  [dot(): return jnp.dot(a, b, preferred_element_type=F32)]
    ppermute x0 -> x4, starting transfers between devices: none -> 12.2 us  [turn(): lax.ppermute(value, axis, [(i, (i + shift) % size) for i in range(size)])]
    ppermute x0 -> x4, waiting for transfers between devices: none -> 10.5 us  [turn(): lax.ppermute(value, axis, [(i, (i + shift) % size) for i in range(size)])]
    all_to_all x1 -> x3, starting transfers between devices: 20.6 us -> 29.8 us  [swap(): return lax.all_to_all(value, axes, split_axis=0, concat_axis=0, tiled=True)]
    pallas_call x0 -> x1, Pallas kernels: none -> 7.74 us  [run_step(): pl.pallas_call(step_kernel, out_shape=(jax.ShapeDtypeStruct((CORES, X, SH...]
  transfers between devices with their start and end apart: 2 -> 7, of which waited for: 2 -> 7; matrix products, arithmetic and copies ran while one was open for 0% -> 5% of each run, Pallas kernels for 0% -> 0%
where the time goes in v1:
time: 183 us; the launch traced here: 182 us
  waiting for transfers between devices  66.2 us (36%)
  starting transfers between devices  42 us (23%)
  blocking collectives  41.1 us (22%)
  local copies, waits for them, and re-layouts  13 us (7%)
  other arithmetic  9.9 us (5%)
  Pallas kernels  7.74 us (4%)
    all_to_all x3, waiting for transfers between devices, swap(): return lax.all_to_all(value, axes, split_axis=0, concat_axis=0, tiled=True)  55.7 us
    all_to_all x3, blocking collectives, swap(): return lax.all_to_all(value, axes, split_axis=0, concat_axis=0, tiled=True)  41.1 us
    all_to_all x3, starting transfers between devices, swap(): return lax.all_to_all(value, axes, split_axis=0, concat_axis=0, tiled=True)  29.8 us
    ppermute x4, starting transfers between devices, turn(): lax.ppermute(value, axis, [(i, (i + shift) % size) for i in range(size)])  12.2 us
    ppermute x4, waiting for transfers between devices, turn(): lax.ppermute(value, axis, [(i, (i + shift) % size) for i in range(size)])  10.5 us
    pallas_call x1, Pallas kernels, run_step(): pl.pallas_call(step_kernel, out_shape=(jax.ShapeDtypeStruct((CORES, X, SH...  7.74 us
    unnamed x23, local copies, waits for them, and re-layouts  6.77 us
  transfers between devices with their start and end apart: 7, of which 7 were waited for; matrix products, arithmetic and copies ran while one was open for 5% of the time, Pallas kernels for 0%

profile of v1, /device:TPU:8, one launch (start us, length us, event | category | flops | bytes accessed | tf_op | source)
XLA Modules:
  0.0 182.1 jit_solution(17096755484164334882)
XLA Ops:
  1.2 1.2 reduce.7
  4.0 20.4 %all-to-all-start = ((bf16[32,16,256]{2,1,0:T(8,128)(2,1)}), bf16[32,16,256]{2,1,0:T(8,128)(2,1)S(1)}, u32[]{:S(2)}, u32[]{:S(2)}) async-start(bf16[32,16,256]{2,1,0:T(8,128)(2,1)} %broadcast_in_dim.15), calls=%async_computation | async-start | bytes 524288 | tf_op jit(solution)/shard_map/all_to_all | solution.py:156
  24.4 1.7 convert_element_type.10
  27.7 1.1 reshape.60
  28.8 17.1 %all-to-all-done = bf16[32,16,256]{2,1,0:T(8,128)(2,1)S(1)} async-done(((bf16[32,16,256]{2,1,0:T(8,128)(2,1)}), bf16[32,16,256]{2,1,0:T(8,128)(2,1)S(1)}, u32[]{:S(2)}, u32[]{:S(2)}) %all-to-all-start) | async-done | bytes 262176 | tf_op jit(solution)/shard_map/all_to_all | solution.py:156
  46.0 1.7 copy.52
  47.6 4.8 %all-to-all-start.1 = ((bf16[32,128,128]{2,1,0:T(8,128)(2,1)}), bf16[32,128,128]{2,1,0:T(8,128)(2,1)}, u32[]{:S(2)}, u32[]{:S(2)}) async-start(bf16[32,128,128]{2,1,0:T(8,128)(2,1)} %copy.52), calls=%async_computation.1 | async-start | bytes 2097152 | tf_op jit(solution)/shard_map/all_to_all | solution.py:156
  52.5 4.8 %collective-permute-start.2 = (bf16[32,16,256]{2,1,0:T(8,128)(2,1)S(1)}, bf16[32,16,256]{2,1,0:T(8,128)(2,1)S(1)}, u32[]{:S(2)}, u32[]{:S(2)}) collective-permute-start(bf16[32,16,256]{2,1,0:T(8,128)(2,1)S(1)} %all-to-all-done), channel_id=1, source_target_pairs={{0,768},{256,0},{512,256},{768,512},{1,769},{257,1},{513,257},{769... | collective-permute-start | bytes 786440 | tf_op jit(solution)/shard_map/ppermute | solution.py:164
  57.3 2.7 %collective-permute-start.1 = (bf16[32,16,256]{2,1,0:T(8,128)(2,1)S(1)}, bf16[32,16,256]{2,1,0:T(8,128)(2,1)S(1)}, u32[]{:S(2)}, u32[]{:S(2)}) collective-permute-start(bf16[32,16,256]{2,1,0:T(8,128)(2,1)S(1)} %all-to-all-done), channel_id=1, source_target_pairs={{0,512},{256,768},{512,0},{768,256},{1,513},{257,769},{513,1},{769... | collective-permute-start | bytes 786440 | tf_op jit(solution)/shard_map/ppermute | solution.py:164
  60.0 2.8 %collective-permute-start = (bf16[32,16,256]{2,1,0:T(8,128)(2,1)S(1)}, bf16[32,16,256]{2,1,0:T(8,128)(2,1)S(1)}, u32[]{:S(2)}, u32[]{:S(2)}) collective-permute-start(bf16[32,16,256]{2,1,0:T(8,128)(2,1)S(1)} %all-to-all-done), channel_id=1, source_target_pairs={{0,256},{256,512},{512,768},{768,0},{1,257},{257,513},{513,769},{7... | collective-permute-start | bytes 786440 | tf_op jit(solution)/shard_map/ppermute | solution.py:164
  62.8 3.9 %collective-permute-done.2 = bf16[32,16,256]{2,1,0:T(8,128)(2,1)S(1)} collective-permute-done((bf16[32,16,256]{2,1,0:T(8,128)(2,1)S(1)}, bf16[32,16,256]{2,1,0:T(8,128)(2,1)S(1)}, u32[]{:S(2)}, u32[]{:S(2)}) %collective-permute-start.2) | collective-permute-done | bytes 262176 | tf_op jit(solution)/shard_map/ppermute | solution.py:164
  66.7 2.7 %collective-permute-done.1 = bf16[32,16,256]{2,1,0:T(8,128)(2,1)S(1)} collective-permute-done((bf16[32,16,256]{2,1,0:T(8,128)(2,1)S(1)}, bf16[32,16,256]{2,1,0:T(8,128)(2,1)S(1)}, u32[]{:S(2)}, u32[]{:S(2)}) %collective-permute-start.1) | collective-permute-done | bytes 262176 | tf_op jit(solution)/shard_map/ppermute | solution.py:164
  69.4 2.7 %collective-permute-done = bf16[32,16,256]{2,1,0:T(8,128)(2,1)S(1)} collective-permute-done((bf16[32,16,256]{2,1,0:T(8,128)(2,1)S(1)}, bf16[32,16,256]{2,1,0:T(8,128)(2,1)S(1)}, u32[]{:S(2)}, u32[]{:S(2)}) %collective-permute-start) | collective-permute-done | bytes 262176 | tf_op jit(solution)/shard_map/ppermute | solution.py:164
  72.2 1.2 fusion.7
  73.3 1.9 %collective-permute-start.3 = (bf16[4,32,16,256]{3,2,1,0:T(8,128)(2,1)S(1)}, bf16[4,32,16,256]{3,2,1,0:T(8,128)(2,1)S(1)}, u32[]{:S(2)}, u32[]{:S(2)}) collective-permute-start(bf16[4,32,16,256]{3,2,1,0:T(8,128)(2,1)S(1)} %get-tuple-element.11), channel_id=1, source_target_pairs={{0,32},{32,0},{1,33},{33,1},{2,34},{34,2},{3,35},{35,3},{4,36},{36... | collective-permute-start | bytes 3145736 | tf_op jit(solution)/shard_map/ppermute | solution.py:164
  75.4 1.3 fusion.3.bottom
  76.7 1.1 collective-permute-done.3
  77.9 1.0 copy-done.7
  78.9 1.8 pad_maximum_fusion.looked
  80.6 26.0 %all-to-all-done.1.counts = bf16[32,128,128]{2,1,0:T(8,128)(2,1)} async-done(((bf16[32,128,128]{2,1,0:T(8,128)(2,1)}), bf16[32,128,128]{2,1,0:T(8,128)(2,1)}, u32[]{:S(2)}, u32[]{:S(2)}) %all-to-all-start.1) | async-done | bytes 1048608 | tf_op jit(solution)/shard_map/all_to_all | solution.py:156
  106.6 1.7 copy-done.1
  108.3 1.3 copy-done.2
  109.5 1.3 copy-done.3
  110.8 1.0 copy-done.4
  111.8 7.7 %shard_map.140 = (bf16[2,4,32,16,256]{4,3,2,1,0:T(8,128)(2,1)S(1)}, f32[128,1]{1,0:T(8,128)S(1)}) custom-call(s32[2]{0:T(128)S(1)} %pad_add_fusion.place, s32[32]{0:T(128)S(1)} %copy-done.6, bf16[32,128,128]{2,1,0:T(8,128)(2,1)} %all-to-all-done.1.counts, bf16[2,4,32,16,256]{4,3,2,1,0:T(8,128)(2,1)S(1)} %pad_maximum_fusion.looked, ...), custom_call_target="tpu_custom_call" | custom-call | flops 3000000000 | bytes 12582912 | tf_op jit(solution)/shard_map/pallas_call | solution.py:133
  119.6 5.4 %all_to_all.30 = bf16[2,4,32,16,256]{4,3,2,1,0:T(8,128)(2,1)S(1)} all-to-all(bf16[2,4,32,16,256]{4,3,2,1,0:T(8,128)(2,1)S(1)} %get-tuple-element.8), channel_id=1, replica_groups=mesh['x'=4,'yh'=4,'c'=2,'z'=16,'yl'=2] {'c'}, dimensions={0} | all-to-all | bytes 4194304 | tf_op jit(solution)/shard_map/all_to_all | solution.py:156
  125.0 1.6 reduce_sum.45
  126.6 19.7 %all_to_all.31 = bf16[4,32,16,256]{3,2,1,0:T(8,128)(2,1)S(1)} all-to-all(bf16[4,32,16,256]{3,2,1,0:T(8,128)(2,1)} %reduce_sum.45), channel_id=1, replica_groups=mesh['x'=4,'yh'=4,'c'=2,'z'=16,'yl'=2] {'x'}, dimensions={0} | all-to-all | bytes 2097152 | tf_op jit(solution)/shard_map/all_to_all | solution.py:156
  146.9 15.9 %all_to_all.32 = bf16[4,32,4,256]{3,2,1,0:T(4,128)(2,1)S(1)} all-to-all(bf16[4,32,4,256]{3,2,1,0:T(4,128)(2,1)S(1)} %copy.55), channel_id=1, replica_groups=mesh['x'=4,'yh'=4,'c'=2,'z'=16,'yl'=2] {'yh'}, dimensions={0} | all-to-all | bytes 524288 | tf_op jit(solution)/shard_map/all_to_all | solution.py:156
  162.8 0.7 reduce_sum.47
  163.6 4.6 %all-to-all-start.5 = ((bf16[32,4,256]{2,1,0:T(4,128)(2,1)}), bf16[32,4,256]{2,1,0:T(4,128)(2,1)S(1)}, u32[]{:S(2)}, u32[]{:S(2)}) async-start(bf16[32,4,256]{2,1,0:T(4,128)(2,1)} %reduce_sum.47), calls=%async_computation.5 | async-start | bytes 131072 | tf_op jit(solution)/shard_map/all_to_all | solution.py:156
  168.8 12.6 %all-to-all-done.5 = bf16[32,4,256]{2,1,0:T(4,128)(2,1)S(1)} async-done(((bf16[32,4,256]{2,1,0:T(4,128)(2,1)}), bf16[32,4,256]{2,1,0:T(4,128)(2,1)S(1)}, u32[]{:S(2)}, u32[]{:S(2)}) %all-to-all-start.5) | async-done | bytes 65568 | tf_op jit(solution)/shard_map/all_to_all | solution.py:156
  (37 shorter events, 5.7 us)
Async XLA Ops:
  0.6 2.0 %copy-start = (f32[1024,256]{1,0:T(8,128)S(1)}, f32[1024,256]{1,0:T(8,128)}, u32[]{:S(2)}) copy-start(f32[1024,256]{1,0:T(8,128)} %param.13) | copy-start | bytes 3145732
  4.0 41.9 %all-to-all-start = ((bf16[32,16,256]{2,1,0:T(8,128)(2,1)}), bf16[32,16,256]{2,1,0:T(8,128)(2,1)S(1)}, u32[]{:S(2)}, u32[]{:S(2)}) async-start(bf16[32,16,256]{2,1,0:T(8,128)(2,1)} %broadcast_in_dim.15), calls=%async_computation | async-start | bytes 524288 | tf_op jit(solution)/shard_map/all_to_all | solution.py:156
  47.6 58.9 %all-to-all-start.1 = ((bf16[32,128,128]{2,1,0:T(8,128)(2,1)}), bf16[32,128,128]{2,1,0:T(8,128)(2,1)}, u32[]{:S(2)}, u32[]{:S(2)}) async-start(bf16[32,128,128]{2,1,0:T(8,128)(2,1)} %copy.52), calls=%async_computation.1 | async-start | bytes 2097152 | tf_op jit(solution)/shard_map/all_to_all | solution.py:156
  52.5 22.8 %copy-start.10 = (s32[128]{0:T(128)S(1)}, s32[128]{0:T(128)}, u32[]{:S(2)}) copy-start(s32[128]{0:T(128)} %param.18) | copy-start | bytes 1540
  52.5 23.0 %copy-start.8 = (bf16[13,512]{1,0:T(8,128)(2,1)S(1)}, bf16[13,512]{1,0:T(8,128)(2,1)}, u32[]{:S(2)}) copy-start(bf16[13,512]{1,0:T(8,128)(2,1)} %param.19) | copy-start | bytes 39940
  52.5 23.0 %copy-start.9 = (bf16[13,128]{1,0:T(8,128)(2,1)S(1)}, bf16[13,128]{1,0:T(8,128)(2,1)}, u32[]{:S(2)}) copy-start(bf16[13,128]{1,0:T(8,128)(2,1)} %param.17) | copy-start | bytes 9988
  52.5 14.2 %collective-permute-start.2 = (bf16[32,16,256]{2,1,0:T(8,128)(2,1)S(1)}, bf16[32,16,256]{2,1,0:T(8,128)(2,1)S(1)}, u32[]{:S(2)}, u32[]{:S(2)}) collective-permute-start(bf16[32,16,256]{2,1,0:T(8,128)(2,1)S(1)} %all-to-all-done), channel_id=1, source_target_pairs={{0,768},{256,0},{512,256},{768,512},{1,769},{257,1},{513,257},{769... | collective-permute-start | bytes 786440 | tf_op jit(solution)/shard_map/ppermute | solution.py:164
  57.3 12.1 %collective-permute-start.1 = (bf16[32,16,256]{2,1,0:T(8,128)(2,1)S(1)}, bf16[32,16,256]{2,1,0:T(8,128)(2,1)S(1)}, u32[]{:S(2)}, u32[]{:S(2)}) collective-permute-start(bf16[32,16,256]{2,1,0:T(8,128)(2,1)S(1)} %all-to-all-done), channel_id=1, source_target_pairs={{0,512},{256,768},{512,0},{768,256},{1,513},{257,769},{513,1},{769... | collective-permute-start | bytes 786440 | tf_op jit(solution)/shard_map/ppermute | solution.py:164
  60.0 12.1 %collective-permute-start = (bf16[32,16,256]{2,1,0:T(8,128)(2,1)S(1)}, bf16[32,16,256]{2,1,0:T(8,128)(2,1)S(1)}, u32[]{:S(2)}, u32[]{:S(2)}) collective-permute-start(bf16[32,16,256]{2,1,0:T(8,128)(2,1)S(1)} %all-to-all-done), channel_id=1, source_target_pairs={{0,256},{256,512},{512,768},{768,0},{1,257},{257,513},{513,769},{7... | collective-permute-start | bytes 786440 | tf_op jit(solution)/shard_map/ppermute | solution.py:164
  73.3 4.5 %collective-permute-start.3 = (bf16[4,32,16,256]{3,2,1,0:T(8,128)(2,1)S(1)}, bf16[4,32,16,256]{3,2,1,0:T(8,128)(2,1)S(1)}, u32[]{:S(2)}, u32[]{:S(2)}) collective-permute-start(bf16[4,32,16,256]{3,2,1,0:T(8,128)(2,1)S(1)} %get-tuple-element.11), channel_id=1, source_target_pairs={{0,32},{32,0},{1,33},{33,1},{2,34},{34,2},{3,35},{35,3},{4,36},{36... | collective-permute-start | bytes 3145736 | tf_op jit(solution)/shard_map/ppermute | solution.py:164
  77.9 1.0 copy-start.7
  78.8 27.7 %copy-start.5 = (f32[512]{0:T(512)S(1)}, f32[512]{0:T(512)}, u32[]{:S(2)}) copy-start(f32[512]{0:T(512)} %param.25) | copy-start | bytes 6148
  78.8 27.7 %copy-start.6 = (s32[32]{0:T(128)S(1)}, s32[32]{0:T(128)}, u32[]{:S(2)}) copy-start(s32[32]{0:T(128)} %table_of.1) | copy-start | bytes 388
  106.6 1.7 copy-start.1
  108.2 1.3 copy-start.2
  109.5 1.3 copy-start.3
  110.8 1.0 copy-start.4
  163.6 17.9 %all-to-all-start.5 = ((bf16[32,4,256]{2,1,0:T(4,128)(2,1)}), bf16[32,4,256]{2,1,0:T(4,128)(2,1)S(1)}, u32[]{:S(2)}, u32[]{:S(2)}) async-start(bf16[32,4,256]{2,1,0:T(4,128)(2,1)} %reduce_sum.47), calls=%async_computation.5 | async-start | bytes 131072 | tf_op jit(solution)/shard_map/all_to_all | solution.py:156

commit v2 on v1

--- a/solution.py
+++ b/solution.py
@@ -37,6 +37,16 @@
     return lax.dot_general(a, b, (((0,), (0,)), ((), ())), preferred_element_type=F32)
 
 
+def split_dot(value, weights):
+    high = value.astype(BF)
+    low = (value - high.astype(F32)).astype(BF)
+    return dot(high, weights) + dot(low, weights)
+
+
+def cols(k):
+    return slice(k * E, (k + 1) * E)
+
+
 def step_kernel(
     place,
     table_of,
@@ -44,19 +54,37 @@
     looked,
     bottom,
     labels,
+    w_out,
+    down_hbm,
+    up_hbm,
+    top1_hbm,
+    top2_hbm,
+    grads,
+    logits_out,
     cross_down,
     cross_up,
     w_top1,
     w_top2,
-    w_out,
-    grads,
-    logits_out,
     feats,
     scaled,
     emb_grad,
     order,
     filled,
+    arrived,
 ):
+    copies = [
+        pltpu.make_async_copy(source, target, arrived.at[i])
+        for i, (source, target) in enumerate(
+            (
+                (down_hbm, cross_down),
+                (up_hbm, cross_up),
+                (top1_hbm, w_top1),
+                (top2_hbm, w_top2),
+            )
+        )
+    ]
+    for copy in copies:
+        copy.start()
     my_x, my_c = place[0], place[1]
     for t in range(TABLES):
         filled[t] = 0
@@ -66,10 +94,7 @@
         order[t * PER + k] = m
         filled[t] = k + 1
 
-    def cols(k):
-        return slice(k * E, (k + 1) * E)
-
-    feats[:, cols(0)] = bottom[...]
+    feats[:, cols(0)] = bottom[...].astype(F32)
     for t in range(TABLES):
         acc = None
         for k in range(PER):
@@ -77,25 +102,31 @@
             rows = jnp.concatenate(
                 [
                     looked[lax.bitwise_xor(my_c, c), lax.rem(my_x + X - x, X), m]
+                    for x in range(X)
                     for c in range(CORES)
-                    for x in range(X)
                 ],
                 axis=0,
             )
             term = dot(counts[m], rows)
             acc = term if acc is None else acc + term
-        feats[:, cols(t + 1)] = acc.astype(BF)
-
-    low = dot(feats[...], cross_down[...]).astype(BF)
+        feats[:, cols(t + 1)] = acc
+
+    copies[0].wait()
+    low = split_dot(feats[...], cross_down[...])
+    low_high = low.astype(BF)
+    low_rest = (low - low_high.astype(F32)).astype(BF)
+    copies[1].wait()
+    copies[2].wait()
     pre_one = None
     for k in range(TABLES + 1):
-        scale = dot(low, cross_up[:, cols(k)])
+        scale = dot(low_high, cross_up[:, cols(k)]) + dot(low_rest, cross_up[:, cols(k)])
         scaled[:, cols(k)] = scale
-        feat = feats[:, cols(k)].astype(F32)
-        term = dot((feat * scale + feat).astype(BF), w_top1[cols(k), :])
+        feat = feats[:, cols(k)]
+        term = split_dot(feat * scale + feat, w_top1[cols(k), :])
         pre_one = term if pre_one is None else pre_one + term
+    copies[3].wait()
     sig_one = jax.nn.sigmoid(pre_one)
-    pre_two = dot((pre_one * sig_one).astype(BF), w_top2[...])
+    pre_two = split_dot(pre_one * sig_one, w_top2[...])
     sig_two = jax.nn.sigmoid(pre_two)
     head = w_out[...]
     logits = jnp.sum(pre_two * sig_two * head, axis=1, keepdims=True)
@@ -106,8 +137,7 @@
     low_grad = None
     for k in range(TABLES + 1):
         part = dot_nt(grad_one, w_top1[cols(k), :])
-        feat = feats[:, cols(k)].astype(F32)
-        term = dot_nt((part * feat).astype(BF), cross_up[:, cols(k)])
+        term = dot_nt((part * feats[:, cols(k)]).astype(BF), cross_up[:, cols(k)])
         low_grad = term if low_grad is None else low_grad + term
         if k > 0:
             scaled[:, cols(k)] = part * (scaled[:, cols(k)] + 1.0)
@@ -116,8 +146,14 @@
         back = dot_nt(low_grad, cross_down[cols(t + 1), :])
         emb_grad[t] = (scaled[:, cols(t + 1)] + back).astype(BF)
 
+    to = lax.broadcasted_iota(jnp.int32, (LOOK, LOOK), 0)
+    at = lax.broadcasted_iota(jnp.int32, (LOOK, LOOK), 1)
+    source = (to // 16 % X) * 32 + (to // 4 % YH) * 8 + (to // 64) * 4 + to % 4
+    turned = (at == source).astype(BF)
+
     def one_shard(m, carry):
-        terms = dot_tn(counts[m], emb_grad[table_of[m]]).astype(BF)
+        picked = dot_nt(turned, counts[m]).astype(BF)
+        terms = dot(picked, emb_grad[table_of[m]]).astype(BF)
         for c in range(CORES):
             for x in range(X):
                 at = (c * X + x) * 16
@@ -127,29 +163,66 @@
     lax.fori_loop(0, SHARDS, one_shard, 0, unroll=4)
 
 
-def run_step(place, table_of, *arrays):
+def run_step(place, table_of, arrays, weights):
     smem = pl.BlockSpec(memory_space=pltpu.SMEM)
     vmem = pl.BlockSpec(memory_space=pltpu.VMEM)
+    hbm = pl.BlockSpec(memory_space=pltpu.HBM)
     return pl.pallas_call(
         step_kernel,
         out_shape=(
             jax.ShapeDtypeStruct((CORES, X, SHARDS, 16, E), BF),
             jax.ShapeDtypeStruct((N, 1), F32),
         ),
-        in_specs=[smem, smem] + [vmem] * len(arrays),
+        in_specs=[smem, smem] + [vmem] * len(arrays) + [hbm] * len(weights),
         out_specs=(vmem, vmem),
-        scratch_shapes=[
-            pltpu.VMEM((N, (TABLES + 1) * E), BF),
+        scratch_shapes=[pltpu.VMEM(w.shape, w.dtype) for w in weights]
+        + [
+            pltpu.VMEM((N, (TABLES + 1) * E), F32),
             pltpu.VMEM((N, (TABLES + 1) * E), F32),
             pltpu.VMEM((TABLES, N, E), BF),
             pltpu.SMEM((SHARDS,), jnp.int32),
             pltpu.SMEM((TABLES,), jnp.int32),
+            pltpu.SemaphoreType.DMA((len(weights),)),
         ],
-        compiler_params=pltpu.CompilerParams(vmem_limit_bytes=40 * 2**20),
+        compiler_params=pltpu.CompilerParams(vmem_limit_bytes=32 * 2**20),
         cost_estimate=pl.CostEstimate(
-            flops=3 * 10**9, bytes_accessed=12 * 2**20, transcendentals=2 * 10**5
+            flops=4 * 10**9, bytes_accessed=12 * 2**20, transcendentals=2 * 10**5
         ),
-    )(place, table_of, *arrays)
+    )(place, table_of, *arrays, *weights)
+
+
+def pair_kernel(halves, out):
+    to = lax.broadcasted_iota(jnp.int32, (E, E), 0)
+    at = lax.broadcasted_iota(jnp.int32, (E, E), 1)
+    turned = (at == (to // 4 % Z) * 16 + (to // 64) * 4 + to % 4).astype(BF)
+    for x in range(X):
+        for yl in range(YL):
+            rows = jnp.concatenate(
+                [
+                    (
+                        halves[0, x, z * YL + yl].astype(F32)
+                        + halves[1, x, z * YL + yl].astype(F32)
+                    ).astype(BF)
+                    for z in range(Z)
+                ],
+                axis=0,
+            )
+            rows = dot(turned, rows).astype(BF)
+            for yh in range(YH):
+                out[x, yh, yl] = rows[yh * 64 : yh * 64 + 64]
+
+
+def add_pair(halves):
+    return pl.pallas_call(
+        pair_kernel,
+        out_shape=jax.ShapeDtypeStruct((X, YH, YL, Z * 4, E), BF),
+        in_specs=[pl.BlockSpec(memory_space=pltpu.VMEM)],
+        out_specs=pl.BlockSpec(memory_space=pltpu.VMEM),
+        compiler_params=pltpu.CompilerParams(vmem_limit_bytes=16 * 2**20),
+        cost_estimate=pl.CostEstimate(
+            flops=3 * 10**8, bytes_accessed=3 * 2**20, transcendentals=0
+        ),
+    )(halves)
 
 
 def swap(value, axes):
@@ -180,14 +253,12 @@
     w_out,
 ):
     my_x, my_c = lax.axis_index("x"), lax.axis_index("c")
-    ids = row_ids[0].reshape(X, YH, CORES, 4).transpose(2, 0, 1, 3)
-    ids = lax.dynamic_index_in_dim(ids.reshape(CORES * X, 16), my_c * X + my_x, 0, keepdims=False)
-    mine = jnp.take(table, ids, axis=0).astype(BF)
-    looked = swap(jnp.broadcast_to(mine, (SHARDS, 16, E)), MP)
-    counts = pool_counts.astype(BF).reshape(SHARDS * N, X, YH, CORES, 4)
-    counts = counts.transpose(0, 3, 1, 2, 4).reshape(SHARDS, N, LOOK)
-    counts, looked = lax.optimization_barrier((counts, looked))
-    counts = swap(counts, MP)
+    ids = lax.dynamic_slice(row_ids, (0, (my_x * CORES + my_c) * 16), (1, 16))[0]
+    mine = jnp.take(table, ids, axis=0, mode="clip").astype(BF)
+    mine = jnp.broadcast_to(mine, (SHARDS, 16, E))
+    mine, pool_counts = lax.optimization_barrier((mine, pool_counts))
+    looked = swap(mine, MP)
+    counts = swap(pool_counts.astype(BF).reshape(SHARDS, N, LOOK), MP)
     looked = jnp.stack([looked] + [turn(looked, "x", X, k) for k in range(1, X)])
     looked = jnp.stack([looked, turn(looked, "c", CORES, 1)])
 
@@ -201,21 +272,12 @@
     grads, logits = run_step(
         place,
         table_of,
-        counts,
-        looked,
-        bottom,
-        labels.reshape(N, 1),
-        cross_down,
-        cross_up,
-        w_top1,
-        w_top2,
-        w_out.reshape(1, -1),
+        (counts, looked, bottom, labels.reshape(N, 1), w_out.reshape(1, -1)),
+        (cross_down, cross_up, w_top1, w_top2),
     )
-    grads = add_up(swap(grads, "c")).astype(BF)
-    grads = add_up(swap(grads, "x")).astype(BF)
-    grads = grads.reshape(SHARDS, YH, 4, E).transpose(1, 0, 2, 3)
-    grads = add_up(swap(grads, "yh")).astype(BF)
-    grads = add_up(swap(grads, MP))
+    grads = add_pair(swap(grads, "c")).reshape(X * YH * YL, Z * 4, E)
+    grads = add_up(swap(grads, ("x", "yh", "yl"))).astype(BF)
+    grads = add_up(swap(grads.reshape(Z, 4, E), "z"))
     return grads, logits.reshape(N)
 
 

time: 183 us -> 186 us (1.016)
  Pallas kernels: 7.74 us -> 14.6 us
  local copies, waits for them, and re-layouts: 13 us -> 9.54 us
  other arithmetic: 9.9 us -> 7.05 us
  blocking collectives: 41.1 us -> 43.4 us
    pallas_call x1, Pallas kernels: 7.74 us -> 14.1 us  [run_step(): pl.pallas_call(step_kernel, out_shape=(jax.ShapeDtypeStruct((CORES, X, SH...]
    reduce_sum x4 -> x2, other arithmetic: 3.25 us -> 0.77 us  [add_up(): return jnp.sum(value.astype(F32), axis=0)]
    all_to_all x3 -> x2, blocking collectives: 41.1 us -> 43.4 us  [swap(): return lax.all_to_all(value, axes, split_axis=0, concat_axis=0, tiled=True)]
    unnamed x23 -> x22, local copies, waits for them, and re-layouts: 6.77 us -> 6.67 us
  transfers between devices with their start and end apart: 7 -> 7, of which waited for: 7 -> 7; matrix products, arithmetic and copies ran while one was open for 5% -> 4% of each run, Pallas kernels for 0% -> 0%
where the time goes in v2:
time: 186 us; the launch traced here: 185 us
  waiting for transfers between devices  67.2 us (36%)
  blocking collectives  43.4 us (23%)
  starting transfers between devices  40.9 us (22%)
  Pallas kernels  14.6 us (8%)
  local copies, waits for them, and re-layouts  9.54 us (5%)
  other arithmetic  7.05 us (4%)
    all_to_all x3, waiting for transfers between devices, swap(): return lax.all_to_all(value, axes, split_axis=0, concat_axis=0, tiled=True)  56.8 us
    all_to_all x2, blocking collectives, swap(): return lax.all_to_all(value, axes, split_axis=0, concat_axis=0, tiled=True)  43.4 us
    all_to_all x3, starting transfers between devices, swap(): return lax.all_to_all(value, axes, split_axis=0, concat_axis=0, tiled=True)  28.7 us
    pallas_call x1, Pallas kernels, run_step(): pl.pallas_call(step_kernel, out_shape=(jax.ShapeDtypeStruct((CORES, X, SH...  14.1 us
    ppermute x4, starting transfers between devices, turn(): lax.ppermute(value, axis, [(i, (i + shift) % size) for i in range(size)])  12.2 us
    ppermute x4, waiting for transfers between devices, turn(): lax.ppermute(value, axis, [(i, (i + shift) % size) for i in range(size)])  10.5 us
    unnamed x22, local copies, waits for them, and re-layouts  6.67 us
  transfers between devices with their start and end apart: 7, of which 7 were waited for; matrix products, arithmetic and copies ran while one was open for 4% of the time, Pallas kernels for 0%

profile of v2, /device:TPU:8, one launch (start us, length us, event | category | flops | bytes accessed | tf_op | source)
XLA Modules:
  0.0 184.8 jit_solution(13487224129719580233)
XLA Ops:
  0.7 0.8 dynamic-slice_bitcast_fusion
  1.9 0.6 gather_fusion
  2.5 0.7 broadcast_in_dim.8
  3.2 20.4 %all-to-all-start.1 = ((bf16[32,16,256]{2,1,0:T(8,128)(2,1)}), bf16[32,16,256]{2,1,0:T(8,128)(2,1)S(1)}, u32[]{:S(2)}, u32[]{:S(2)}) async-start(bf16[32,16,256]{2,1,0:T(8,128)(2,1)} %broadcast_in_dim.8), calls=%async_computation.1 | async-start | bytes 524288 | tf_op jit(solution)/shard_map/all_to_all | solution.py:229
  23.6 2.7 %convert_element_type.18 = bf16[4096,128]{1,0:T(8,128)(2,1)} convert(s32[4096,128]{1,0:T(8,128)} %param.15) | non-fusion elementwise | flops 524288 | bytes 3145728 | tf_op jit(solution)/shard_map/convert_element_type | solution.py:261
  26.3 18.9 %all-to-all-done.1 = bf16[32,16,256]{2,1,0:T(8,128)(2,1)S(1)} async-done(((bf16[32,16,256]{2,1,0:T(8,128)(2,1)}), bf16[32,16,256]{2,1,0:T(8,128)(2,1)S(1)}, u32[]{:S(2)}, u32[]{:S(2)}) %all-to-all-start.1) | async-done | bytes 262176 | tf_op jit(solution)/shard_map/all_to_all | solution.py:229
  45.1 4.8 %all-to-all-start = ((bf16[32,128,128]{2,1,0:T(8,128)(2,1)}), bf16[32,128,128]{2,1,0:T(8,128)(2,1)}, u32[]{:S(2)}, u32[]{:S(2)}) async-start(bf16[32,128,128]{2,1,0:T(8,128)(2,1)} %bitcast.3), calls=%async_computation | async-start | bytes 2097152 | tf_op jit(solution)/shard_map/all_to_all | solution.py:229
  50.0 4.8 %collective-permute-start.2 = (bf16[32,16,256]{2,1,0:T(8,128)(2,1)S(1)}, bf16[32,16,256]{2,1,0:T(8,128)(2,1)S(1)}, u32[]{:S(2)}, u32[]{:S(2)}) collective-permute-start(bf16[32,16,256]{2,1,0:T(8,128)(2,1)S(1)} %all-to-all-done.1), channel_id=1, source_target_pairs={{0,768},{256,0},{512,256},{768,512},{1,769},{257,1},{513,257},{769... | collective-permute-start | bytes 786440 | tf_op jit(solution)/shard_map/ppermute | solution.py:237
  54.8 2.7 %collective-permute-start.1 = (bf16[32,16,256]{2,1,0:T(8,128)(2,1)S(1)}, bf16[32,16,256]{2,1,0:T(8,128)(2,1)S(1)}, u32[]{:S(2)}, u32[]{:S(2)}) collective-permute-start(bf16[32,16,256]{2,1,0:T(8,128)(2,1)S(1)} %all-to-all-done.1), channel_id=1, source_target_pairs={{0,512},{256,768},{512,0},{768,256},{1,513},{257,769},{513,1},{769... | collective-permute-start | bytes 786440 | tf_op jit(solution)/shard_map/ppermute | solution.py:237
  57.5 2.8 %collective-permute-start = (bf16[32,16,256]{2,1,0:T(8,128)(2,1)S(1)}, bf16[32,16,256]{2,1,0:T(8,128)(2,1)S(1)}, u32[]{:S(2)}, u32[]{:S(2)}) collective-permute-start(bf16[32,16,256]{2,1,0:T(8,128)(2,1)S(1)} %all-to-all-done.1), channel_id=1, source_target_pairs={{0,256},{256,512},{512,768},{768,0},{1,257},{257,513},{513,769},{7... | collective-permute-start | bytes 786440 | tf_op jit(solution)/shard_map/ppermute | solution.py:237
  60.3 3.9 %collective-permute-done.2 = bf16[32,16,256]{2,1,0:T(8,128)(2,1)S(1)} collective-permute-done((bf16[32,16,256]{2,1,0:T(8,128)(2,1)S(1)}, bf16[32,16,256]{2,1,0:T(8,128)(2,1)S(1)}, u32[]{:S(2)}, u32[]{:S(2)}) %collective-permute-start.2) | collective-permute-done | bytes 262176 | tf_op jit(solution)/shard_map/ppermute | solution.py:237
  64.2 2.7 %collective-permute-done.1 = bf16[32,16,256]{2,1,0:T(8,128)(2,1)S(1)} collective-permute-done((bf16[32,16,256]{2,1,0:T(8,128)(2,1)S(1)}, bf16[32,16,256]{2,1,0:T(8,128)(2,1)S(1)}, u32[]{:S(2)}, u32[]{:S(2)}) %collective-permute-start.1) | collective-permute-done | bytes 262176 | tf_op jit(solution)/shard_map/ppermute | solution.py:237
  66.9 2.7 %collective-permute-done = bf16[32,16,256]{2,1,0:T(8,128)(2,1)S(1)} collective-permute-done((bf16[32,16,256]{2,1,0:T(8,128)(2,1)S(1)}, bf16[32,16,256]{2,1,0:T(8,128)(2,1)S(1)}, u32[]{:S(2)}, u32[]{:S(2)}) %collective-permute-start) | collective-permute-done | bytes 262176 | tf_op jit(solution)/shard_map/ppermute | solution.py:237
  69.6 1.1 fusion.6
  70.8 1.9 %collective-permute-start.3 = (bf16[4,32,16,256]{3,2,1,0:T(8,128)(2,1)S(1)}, bf16[4,32,16,256]{3,2,1,0:T(8,128)(2,1)S(1)}, u32[]{:S(2)}, u32[]{:S(2)}) collective-permute-start(bf16[4,32,16,256]{3,2,1,0:T(8,128)(2,1)S(1)} %get-tuple-element.11), channel_id=1, source_target_pairs={{0,32},{32,0},{1,33},{33,1},{2,34},{34,2},{3,35},{35,3},{4,36},{36... | collective-permute-start | bytes 3145736 | tf_op jit(solution)/shard_map/ppermute | solution.py:237
  72.9 1.3 fusion.3.bottom
  74.2 1.1 collective-permute-done.3
  75.3 1.0 copy-done.7
  76.3 1.8 pad_maximum_fusion.looked
  78.1 26.0 %all-to-all-done.counts = bf16[32,128,128]{2,1,0:T(8,128)(2,1)} async-done(((bf16[32,128,128]{2,1,0:T(8,128)(2,1)}), bf16[32,128,128]{2,1,0:T(8,128)(2,1)}, u32[]{:S(2)}, u32[]{:S(2)}) %all-to-all-start) | async-done | bytes 1048608 | tf_op jit(solution)/shard_map/all_to_all | solution.py:229
  104.1 1.7 copy-done.1
  105.7 1.3 copy-done.2
  107.0 1.3 copy-done.3
  108.3 1.0 copy-done.4
  109.3 14.1 %shard_map.140 = (bf16[2,4,32,16,256]{4,3,2,1,0:T(8,128)(2,1)S(1)}, f32[128,1]{1,0:T(8,128)S(1)}) custom-call(s32[2]{0:T(128)S(1)} %pad_add_fusion.place, s32[32]{0:T(128)S(1)} %copy-done.6, bf16[32,128,128]{2,1,0:T(8,128)(2,1)} %all-to-all-done.counts, bf16[2,4,32,16,256]{4,3,2,1,0:T(8,128)(2,1)S(1)} %pad_maximum_fusion.looked, ...), custom_call_target="tpu_custom_call" | custom-call | flops 4000000000 | bytes 12582912 | tf_op jit(solution)/shard_map/pallas_call | solution.py:170
  123.4 5.4 %all_to_all.25.halves = bf16[2,4,32,16,256]{4,3,2,1,0:T(8,128)(2,1)S(1)} all-to-all(bf16[2,4,32,16,256]{4,3,2,1,0:T(8,128)(2,1)S(1)} %get-tuple-element.8), channel_id=1, replica_groups=mesh['x'=4,'yh'=4,'c'=2,'z'=16,'yl'=2] {'c'}, dimensions={0} | all-to-all | bytes 4194304 | tf_op jit(solution)/shard_map/all_to_all | solution.py:229
  129.4 38.0 %all_to_all.26 = bf16[32,64,256]{2,1,0:T(8,128)(2,1)S(1)} all-to-all(bf16[32,64,256]{2,1,0:T(8,128)(2,1)S(1)} %bitcast.18), channel_id=1, replica_groups=mesh['x'=4,'yh'=4,'c'=2,'z'=16,'yl'=2] {'x','yh','yl'}, dimensions={0} | all-to-all | bytes 2097152 | tf_op jit(solution)/shard_map/all_to_all | solution.py:229
  167.5 0.6 reshape.27
  168.1 3.5 %all-to-all-start.4 = ((bf16[16,4,256]{2,1,0:T(4,128)(2,1)}), bf16[16,4,256]{2,1,0:T(4,128)(2,1)S(1)}, u32[]{:S(2)}, u32[]{:S(2)}) async-start(bf16[16,4,256]{2,1,0:T(4,128)(2,1)} %reshape.27), calls=%async_computation.4 | async-start | bytes 65536 | tf_op jit(solution)/shard_map/all_to_all | solution.py:229
  171.6 0.6 reduce.1
  172.2 11.9 %all-to-all-done.4 = bf16[16,4,256]{2,1,0:T(4,128)(2,1)S(1)} async-done(((bf16[16,4,256]{2,1,0:T(4,128)(2,1)}), bf16[16,4,256]{2,1,0:T(4,128)(2,1)S(1)}, u32[]{:S(2)}, u32[]{:S(2)}) %all-to-all-start.4) | async-done | bytes 32800 | tf_op jit(solution)/shard_map/all_to_all | solution.py:229
  184.2 0.6 convert_reduce_fusion
  (22 shorter events, 1.3 us)
Async XLA Ops:
  0.6 1.2 copy-start
  3.2 41.9 %all-to-all-start.1 = ((bf16[32,16,256]{2,1,0:T(8,128)(2,1)}), bf16[32,16,256]{2,1,0:T(8,128)(2,1)S(1)}, u32[]{:S(2)}, u32[]{:S(2)}) async-start(bf16[32,16,256]{2,1,0:T(8,128)(2,1)} %broadcast_in_dim.8), calls=%async_computation.1 | async-start | bytes 524288 | tf_op jit(solution)/shard_map/all_to_all | solution.py:229
  45.1 58.9 %all-to-all-start = ((bf16[32,128,128]{2,1,0:T(8,128)(2,1)}), bf16[32,128,128]{2,1,0:T(8,128)(2,1)}, u32[]{:S(2)}, u32[]{:S(2)}) async-start(bf16[32,128,128]{2,1,0:T(8,128)(2,1)} %bitcast.3), calls=%async_computation | async-start | bytes 2097152 | tf_op jit(solution)/shard_map/all_to_all | solution.py:229
  49.9 22.8 %copy-start.10 = (s32[128]{0:T(128)S(1)}, s32[128]{0:T(128)}, u32[]{:S(2)}) copy-start(s32[128]{0:T(128)} %param.18) | copy-start | bytes 1540
  49.9 23.0 %copy-start.8 = (bf16[13,512]{1,0:T(8,128)(2,1)S(1)}, bf16[13,512]{1,0:T(8,128)(2,1)}, u32[]{:S(2)}) copy-start(bf16[13,512]{1,0:T(8,128)(2,1)} %param.19) | copy-start | bytes 39940
  50.0 22.9 %copy-start.9 = (bf16[13,128]{1,0:T(8,128)(2,1)S(1)}, bf16[13,128]{1,0:T(8,128)(2,1)}, u32[]{:S(2)}) copy-start(bf16[13,128]{1,0:T(8,128)(2,1)} %param.17) | copy-start | bytes 9988
  50.0 14.2 %collective-permute-start.2 = (bf16[32,16,256]{2,1,0:T(8,128)(2,1)S(1)}, bf16[32,16,256]{2,1,0:T(8,128)(2,1)S(1)}, u32[]{:S(2)}, u32[]{:S(2)}) collective-permute-start(bf16[32,16,256]{2,1,0:T(8,128)(2,1)S(1)} %all-to-all-done.1), channel_id=1, source_target_pairs={{0,768},{256,0},{512,256},{768,512},{1,769},{257,1},{513,257},{769... | collective-permute-start | bytes 786440 | tf_op jit(solution)/shard_map/ppermute | solution.py:237
  54.8 12.1 %collective-permute-start.1 = (bf16[32,16,256]{2,1,0:T(8,128)(2,1)S(1)}, bf16[32,16,256]{2,1,0:T(8,128)(2,1)S(1)}, u32[]{:S(2)}, u32[]{:S(2)}) collective-permute-start(bf16[32,16,256]{2,1,0:T(8,128)(2,1)S(1)} %all-to-all-done.1), channel_id=1, source_target_pairs={{0,512},{256,768},{512,0},{768,256},{1,513},{257,769},{513,1},{769... | collective-permute-start | bytes 786440 | tf_op jit(solution)/shard_map/ppermute | solution.py:237
  57.5 12.1 %collective-permute-start = (bf16[32,16,256]{2,1,0:T(8,128)(2,1)S(1)}, bf16[32,16,256]{2,1,0:T(8,128)(2,1)S(1)}, u32[]{:S(2)}, u32[]{:S(2)}) collective-permute-start(bf16[32,16,256]{2,1,0:T(8,128)(2,1)S(1)} %all-to-all-done.1), channel_id=1, source_target_pairs={{0,256},{256,512},{512,768},{768,0},{1,257},{257,513},{513,769},{7... | collective-permute-start | bytes 786440 | tf_op jit(solution)/shard_map/ppermute | solution.py:237
  70.8 4.5 %collective-permute-start.3 = (bf16[4,32,16,256]{3,2,1,0:T(8,128)(2,1)S(1)}, bf16[4,32,16,256]{3,2,1,0:T(8,128)(2,1)S(1)}, u32[]{:S(2)}, u32[]{:S(2)}) collective-permute-start(bf16[4,32,16,256]{3,2,1,0:T(8,128)(2,1)S(1)} %get-tuple-element.11), channel_id=1, source_target_pairs={{0,32},{32,0},{1,33},{33,1},{2,34},{34,2},{3,35},{35,3},{4,36},{36... | collective-permute-start | bytes 3145736 | tf_op jit(solution)/shard_map/ppermute | solution.py:237
  75.3 1.0 copy-start.7
  76.3 27.7 %copy-start.5 = (f32[512]{0:T(512)S(1)}, f32[512]{0:T(512)}, u32[]{:S(2)}) copy-start(f32[512]{0:T(512)} %param.25) | copy-start | bytes 6148
  76.3 27.7 %copy-start.6 = (s32[32]{0:T(128)S(1)}, s32[32]{0:T(128)}, u32[]{:S(2)}) copy-start(s32[32]{0:T(128)} %table_of.1) | copy-start | bytes 388
  104.1 1.7 copy-start.1
  105.7 1.3 copy-start.2
  107.0 1.3 copy-start.3
  108.3 1.0 copy-start.4
  168.1 16.0 %all-to-all-start.4 = ((bf16[16,4,256]{2,1,0:T(4,128)(2,1)}), bf16[16,4,256]{2,1,0:T(4,128)(2,1)S(1)}, u32[]{:S(2)}, u32[]{:S(2)}) async-start(bf16[16,4,256]{2,1,0:T(4,128)(2,1)} %reshape.27), calls=%async_computation.4 | async-start | bytes 65536 | tf_op jit(solution)/shard_map/all_to_all | solution.py:229

commit v3 on v2

--- a/solution.py
+++ b/solution.py
@@ -50,17 +50,20 @@
 def step_kernel(
     place,
     table_of,
-    counts,
-    looked,
     bottom,
     labels,
     w_out,
+    counts_hbm,
+    own_hbm,
+    other_hbm,
     down_hbm,
     up_hbm,
     top1_hbm,
     top2_hbm,
     grads,
     logits_out,
+    counts,
+    looked,
     cross_down,
     cross_up,
     w_top1,
@@ -72,20 +75,19 @@
     filled,
     arrived,
 ):
-    copies = [
-        pltpu.make_async_copy(source, target, arrived.at[i])
-        for i, (source, target) in enumerate(
-            (
-                (down_hbm, cross_down),
-                (up_hbm, cross_up),
-                (top1_hbm, w_top1),
-                (top2_hbm, w_top2),
-            )
-        )
-    ]
+    moves = (
+        (counts_hbm, counts),
+        (own_hbm, looked.at[0]),
+        (other_hbm, looked.at[1]),
+        (down_hbm, cross_down),
+        (up_hbm, cross_up),
+        (top1_hbm, w_top1),
+        (top2_hbm, w_top2),
+    )
+    copies = [pltpu.make_async_copy(*move, arrived.at[i]) for i, move in enumerate(moves)]
     for copy in copies:
         copy.start()
-    my_x, my_c = place[0], place[1]
+    my_x, my_yh, my_c = place[0], place[1], place[2]
     for t in range(TABLES):
         filled[t] = 0
     for m in range(SHARDS):
@@ -95,6 +97,8 @@
         filled[t] = k + 1
 
     feats[:, cols(0)] = bottom[...].astype(F32)
+    for copy in copies[:3]:
+        copy.wait()
     for t in range(TABLES):
         acc = None
         for k in range(PER):
@@ -102,8 +106,8 @@
             rows = jnp.concatenate(
                 [
                     looked[lax.bitwise_xor(my_c, c), lax.rem(my_x + X - x, X), m]
+                    for c in range(CORES)
                     for x in range(X)
-                    for c in range(CORES)
                 ],
                 axis=0,
             )
@@ -111,12 +115,12 @@
             acc = term if acc is None else acc + term
         feats[:, cols(t + 1)] = acc
 
-    copies[0].wait()
+    copies[3].wait()
     low = split_dot(feats[...], cross_down[...])
     low_high = low.astype(BF)
     low_rest = (low - low_high.astype(F32)).astype(BF)
-    copies[1].wait()
-    copies[2].wait()
+    copies[4].wait()
+    copies[5].wait()
     pre_one = None
     for k in range(TABLES + 1):
         scale = dot(low_high, cross_up[:, cols(k)]) + dot(low_rest, cross_up[:, cols(k)])
@@ -124,7 +128,7 @@
         feat = feats[:, cols(k)]
         term = split_dot(feat * scale + feat, w_top1[cols(k), :])
         pre_one = term if pre_one is None else pre_one + term
-    copies[3].wait()
+    copies[6].wait()
     sig_one = jax.nn.sigmoid(pre_one)
     pre_two = split_dot(pre_one * sig_one, w_top2[...])
     sig_two = jax.nn.sigmoid(pre_two)
@@ -148,7 +152,7 @@
 
     to = lax.broadcasted_iota(jnp.int32, (LOOK, LOOK), 0)
     at = lax.broadcasted_iota(jnp.int32, (LOOK, LOOK), 1)
-    source = (to // 16 % X) * 32 + (to // 4 % YH) * 8 + (to // 64) * 4 + to % 4
+    source = to - to % 16 + ((my_yh + YH - to // 4 % YH) % YH) * 4 + to % 4
     turned = (at == source).astype(BF)
 
     def one_shard(m, carry):
@@ -157,72 +161,100 @@
         for c in range(CORES):
             for x in range(X):
                 at = (c * X + x) * 16
-                grads[c, x, m] = terms[at : at + 16]
+                grads[c, x, m % YL, m // YL] = terms[at : at + 16]
         return carry
 
     lax.fori_loop(0, SHARDS, one_shard, 0, unroll=4)
 
 
-def run_step(place, table_of, arrays, weights):
+def run_step(place, table_of, small, large):
     smem = pl.BlockSpec(memory_space=pltpu.SMEM)
     vmem = pl.BlockSpec(memory_space=pltpu.VMEM)
-    hbm = pl.BlockSpec(memory_space=pltpu.HBM)
+    hbm = pl.BlockSpec(memory_space=pl.ANY)
+    counts, own, _, *weights = large
     return pl.pallas_call(
         step_kernel,
         out_shape=(
-            jax.ShapeDtypeStruct((CORES, X, SHARDS, 16, E), BF),
+            jax.ShapeDtypeStruct((CORES, X, YL, Z, 16, E), BF),
             jax.ShapeDtypeStruct((N, 1), F32),
         ),
-        in_specs=[smem, smem] + [vmem] * len(arrays) + [hbm] * len(weights),
+        in_specs=[smem, smem] + [vmem] * len(small) + [hbm] * len(large),
         out_specs=(vmem, vmem),
-        scratch_shapes=[pltpu.VMEM(w.shape, w.dtype) for w in weights]
-        + [
+        scratch_shapes=[
+            pltpu.VMEM(counts.shape, BF),
+            pltpu.VMEM((CORES, *own.shape), BF),
+            *[pltpu.VMEM(w.shape, BF) for w in weights],
             pltpu.VMEM((N, (TABLES + 1) * E), F32),
             pltpu.VMEM((N, (TABLES + 1) * E), F32),
             pltpu.VMEM((TABLES, N, E), BF),
             pltpu.SMEM((SHARDS,), jnp.int32),
             pltpu.SMEM((TABLES,), jnp.int32),
-            pltpu.SemaphoreType.DMA((len(weights),)),
+            pltpu.SemaphoreType.DMA((len(large),)),
         ],
-        compiler_params=pltpu.CompilerParams(vmem_limit_bytes=32 * 2**20),
+        compiler_params=pltpu.CompilerParams(vmem_limit_bytes=60 * 2**20),
         cost_estimate=pl.CostEstimate(
             flops=4 * 10**9, bytes_accessed=12 * 2**20, transcendentals=2 * 10**5
         ),
-    )(place, table_of, *arrays, *weights)
+    )(place, table_of, *small, *large)
+
+
+def lanes_kernel(place, counts, out):
+    my_yh = place[1]
+    at = lax.broadcasted_iota(jnp.int32, (LOOK, LOOK), 0)
+    to = lax.broadcasted_iota(jnp.int32, (LOOK, LOOK), 1)
+    yh = (my_yh + YH - to // 4 % YH) % YH
+    source = (to // 16 % X) * 32 + yh * 8 + (to // 64) * 4 + to % 4
+    turned = (at == source).astype(BF)
+    out[...] = dot(counts[...].astype(F32).astype(BF), turned).astype(BF)
+
+
+def turn_lanes(place, counts):
+    rows = counts.shape[0] // 8
+    return pl.pallas_call(
+        lanes_kernel,
+        out_shape=jax.ShapeDtypeStruct(counts.shape, BF),
+        grid=(8,),
+        in_specs=[
+            pl.BlockSpec(memory_space=pltpu.SMEM),
+            pl.BlockSpec((rows, LOOK), lambda i: (i, 0)),
+        ],
+        out_specs=pl.BlockSpec((rows, LOOK), lambda i: (i, 0)),
+        cost_estimate=pl.CostEstimate(
+            flops=2 * 10**8, bytes_accessed=3 * 2**20, transcendentals=0
+        ),
+    )(place, counts)
 
 
 def pair_kernel(halves, out):
+    def one_block(i, carry):
+        at = pl.ds(i * 256, 256)
+        out[at] = (halves[0, at].astype(F32) + halves[1, at].astype(F32)).astype(BF)
+        return carry
+
+    lax.fori_loop(0, out.shape[0] // 256, one_block, 0, unroll=2)
+
+
+def sum_kernel(parts, out):
     to = lax.broadcasted_iota(jnp.int32, (E, E), 0)
     at = lax.broadcasted_iota(jnp.int32, (E, E), 1)
     turned = (at == (to // 4 % Z) * 16 + (to // 64) * 4 + to % 4).astype(BF)
-    for x in range(X):
-        for yl in range(YL):
-            rows = jnp.concatenate(
-                [
-                    (
-                        halves[0, x, z * YL + yl].astype(F32)
-                        + halves[1, x, z * YL + yl].astype(F32)
-                    ).astype(BF)
-                    for z in range(Z)
-                ],
-                axis=0,
-            )
-            rows = dot(turned, rows).astype(BF)
-            for yh in range(YH):
-                out[x, yh, yl] = rows[yh * 64 : yh * 64 + 64]
-
-
-def add_pair(halves):
+    total = parts[0].astype(F32)
+    for i in range(1, parts.shape[0]):
+        total = total + parts[i].astype(F32)
+    out[...] = dot(turned, total.astype(BF)).astype(BF)
+
+
+def fold(kernel, parts):
     return pl.pallas_call(
-        pair_kernel,
-        out_shape=jax.ShapeDtypeStruct((X, YH, YL, Z * 4, E), BF),
+        kernel,
+        out_shape=jax.ShapeDtypeStruct(parts.shape[1:], BF),
         in_specs=[pl.BlockSpec(memory_space=pltpu.VMEM)],
         out_specs=pl.BlockSpec(memory_space=pltpu.VMEM),
-        compiler_params=pltpu.CompilerParams(vmem_limit_bytes=16 * 2**20),
+        compiler_params=pltpu.CompilerParams(vmem_limit_bytes=12 * 2**20),
         cost_estimate=pl.CostEstimate(
-            flops=3 * 10**8, bytes_accessed=3 * 2**20, transcendentals=0
-        ),
-    )(halves)
+            flops=5 * 10**7, bytes_accessed=3 * 2**20, transcendentals=0
+        ),
+    )(parts)
 
 
 def swap(value, axes):
@@ -252,15 +284,22 @@
     w_top2,
     w_out,
 ):
-    my_x, my_c = lax.axis_index("x"), lax.axis_index("c")
-    ids = lax.dynamic_slice(row_ids, (0, (my_x * CORES + my_c) * 16), (1, 16))[0]
+    my_x, my_yh, my_c = lax.axis_index("x"), lax.axis_index("yh"), lax.axis_index("c")
+    place = jnp.stack([my_x, my_yh, my_c]).astype(jnp.int32)
+    first = ((my_x * YH + my_yh) * CORES + my_c) * 4
+    ids = lax.dynamic_slice(row_ids, (0, first), (1, 4))[0]
     mine = jnp.take(table, ids, axis=0, mode="clip").astype(BF)
-    mine = jnp.broadcast_to(mine, (SHARDS, 16, E))
+    mine = jnp.broadcast_to(mine, (SHARDS, 4, E))
     mine, pool_counts = lax.optimization_barrier((mine, pool_counts))
     looked = swap(mine, MP)
-    counts = swap(pool_counts.astype(BF).reshape(SHARDS, N, LOOK), MP)
+    counts = turn_lanes(place, pool_counts).reshape(SHARDS, N, LOOK)
+    looked, counts = lax.optimization_barrier((looked, counts))
+    counts = swap(counts, MP)
+    looked = jnp.concatenate(
+        [looked] + [turn(looked, "yh", YH, k) for k in range(1, YH)], axis=1
+    )
     looked = jnp.stack([looked] + [turn(looked, "x", X, k) for k in range(1, X)])
-    looked = jnp.stack([looked, turn(looked, "c", CORES, 1)])
+    others = turn(looked, "c", CORES, 1)
 
     hidden = lax.dot_general(
         dense_feat, w_bottom1, (((0,), (0,)), ((), ())), preferred_element_type=F32
@@ -268,16 +307,16 @@
     hidden = jax.nn.relu(hidden).astype(BF)
     bottom = jax.nn.relu(dot(hidden, w_bottom2)).astype(BF)
 
-    place = jnp.stack([my_x, my_c]).astype(jnp.int32)
     grads, logits = run_step(
         place,
         table_of,
-        (counts, looked, bottom, labels.reshape(N, 1), w_out.reshape(1, -1)),
-        (cross_down, cross_up, w_top1, w_top2),
-    )
-    grads = add_pair(swap(grads, "c")).reshape(X * YH * YL, Z * 4, E)
-    grads = add_up(swap(grads, ("x", "yh", "yl"))).astype(BF)
-    grads = add_up(swap(grads.reshape(Z, 4, E), "z"))
+        (bottom, labels.reshape(N, 1), w_out.reshape(1, -1)),
+        (counts, looked, others, cross_down, cross_up, w_top1, w_top2),
+    )
+    grads = swap(grads.reshape(CORES, X * YL * Z * 16, E), "c")
+    grads = fold(pair_kernel, grads).reshape(X * YL, Z * 16, E)
+    grads = fold(sum_kernel, swap(grads, ("x", "yl"))).reshape(YH * Z, 4, E)
+    grads = add_up(swap(grads, ("yh", "z")))
     return grads, logits.reshape(N)
 
 

time: 186 us -> 171 us (0.919)
  starting transfers between devices: 40.9 us -> 63.8 us
  waiting for transfers between devices: 67.2 us -> 47 us
  blocking collectives: 43.4 us -> 27.1 us
  Pallas kernels: 14.6 us -> 22.8 us
  other arithmetic: 7.05 us -> 2.22 us
  local copies, waits for them, and re-layouts: 9.54 us -> 4.86 us
    all_to_all x3, waiting for transfers between devices: 56.8 us -> 37.3 us  [swap(): return lax.all_to_all(value, axes, split_axis=0, concat_axis=0, tiled=True)]
    all_to_all x2, blocking collectives: 43.4 us -> 27.1 us  [swap(): return lax.all_to_all(value, axes, split_axis=0, concat_axis=0, tiled=True)]
    ppermute x4 -> x7, starting transfers between devices: 12.2 us -> 27.5 us  [turn(): lax.ppermute(value, axis, [(i, (i + shift) % size) for i in range(size)])]
    pallas_call x2 -> x4, Pallas kernels: 14.6 us -> 22.8 us  [the longest x1 16.1 us: run_step(): pl.pallas_call(step_kernel, out_shape=(jax.ShapeDtypeStruct((CORES, X, YL...]
    all_to_all x3, starting transfers between devices: 28.7 us -> 36.3 us  [swap(): return lax.all_to_all(value, axes, split_axis=0, concat_axis=0, tiled=True)]
    unnamed x22 -> x16, local copies, waits for them, and re-layouts: 6.67 us -> 1.4 us
    convert_element_type x1 -> x0, other arithmetic: 2.68 us -> none  [shards(): counts = swap(pool_counts.astype(BF).reshape(SHARDS, N, LOOK), MP)]
    another operation x3, other arithmetic: 2.97 us -> 0.9 us  [the longest x1 0.6 us: shards(): place = jnp.stack([my_x, my_yh, my_c]).astype(jnp.int32)]
  transfers between devices with their start and end apart: 7 -> 10, of which waited for: 7 -> 7; matrix products, arithmetic and copies ran while one was open for 4% -> 2% of each run, Pallas kernels for 0% -> 4%
where the time goes in v3:
time: 171 us; the launch traced here: 170 us
  starting transfers between devices  63.8 us (37%)
  waiting for transfers between devices  47 us (27%)
  blocking collectives  27.1 us (16%)
  Pallas kernels  22.8 us (13%)
  local copies, waits for them, and re-layouts  4.86 us (3%)
  other arithmetic  2.22 us (1%)
    all_to_all x3, waiting for transfers between devices, swap(): return lax.all_to_all(value, axes, split_axis=0, concat_axis=0, tiled=True)  37.3 us
    all_to_all x3, starting transfers between devices, swap(): return lax.all_to_all(value, axes, split_axis=0, concat_axis=0, tiled=True)  36.3 us
    ppermute x7, starting transfers between devices, turn(): lax.ppermute(value, axis, [(i, (i + shift) % size) for i in range(size)])  27.5 us
    all_to_all x2, blocking collectives, swap(): return lax.all_to_all(value, axes, split_axis=0, concat_axis=0, tiled=True)  27.1 us
    pallas_call x1, Pallas kernels, run_step(): pl.pallas_call(step_kernel, out_shape=(jax.ShapeDtypeStruct((CORES, X, YL...  16.1 us
    ppermute x7, waiting for transfers between devices, turn(): lax.ppermute(value, axis, [(i, (i + shift) % size) for i in range(size)])  9.72 us
    pallas_call x1, Pallas kernels, turn_lanes(): pl.pallas_call(lanes_kernel, out_shape=jax.ShapeDtypeStruct(counts.shape,...  6.12 us
  transfers between devices with their start and end apart: 10, of which 7 were waited for; matrix products, arithmetic and copies ran while one was open for 2% of the time, Pallas kernels for 4%

profile of v3, /device:TPU:8, one launch (start us, length us, event | category | flops | bytes accessed | tf_op | source)
XLA Modules:
  0.0 169.6 jit_solution(11081828069675795825)
XLA Ops:
  0.7 0.8 dynamic-slice_bitcast_fusion
  1.5 0.4 copy-done
  1.9 0.6 gather_fusion
  2.4 0.6 broadcast_in_dim.8
  3.1 20.4 %all-to-all-start = ((bf16[32,4,256]{2,1,0:T(4,128)(2,1)}), bf16[32,4,256]{2,1,0:T(4,128)(2,1)S(1)}, u32[]{:S(2)}, u32[]{:S(2)}) async-start(bf16[32,4,256]{2,1,0:T(4,128)(2,1)} %broadcast_in_dim.8), calls=%async_computation | async-start | bytes 131072 | tf_op jit(solution)/shard_map/all_to_all | solution.py:261
  23.5 0.6 pad_add_fusion.place
  24.1 6.1 %shard_map.140 = bf16[4096,128]{1,0:T(8,128)(2,1)} custom-call(s32[3]{0:T(128)} %pad_add_fusion.place, s32[4096,128]{1,0:T(8,128)} %counts), custom_call_target="tpu_custom_call" | custom-call | flops 200000000 | bytes 3145728 | tf_op jit(solution)/shard_map/pallas_call | solution.py:213
  30.2 6.5 %all-to-all-done = bf16[32,4,256]{2,1,0:T(4,128)(2,1)S(1)} async-done(((bf16[32,4,256]{2,1,0:T(4,128)(2,1)}), bf16[32,4,256]{2,1,0:T(4,128)(2,1)S(1)}, u32[]{:S(2)}, u32[]{:S(2)}) %all-to-all-start) | async-done | bytes 65568 | tf_op jit(solution)/shard_map/all_to_all | solution.py:261
  36.7 6.8 %all-to-all-start.1 = ((bf16[32,128,128]{2,1,0:T(8,128)(2,1)}), bf16[32,128,128]{2,1,0:T(8,128)(2,1)S(1)}, u32[]{:S(2)}, u32[]{:S(2)}) async-start(bf16[32,128,128]{2,1,0:T(8,128)(2,1)} %bitcast.19), calls=%async_computation.1 | async-start | bytes 2097152 | tf_op jit(solution)/shard_map/all_to_all | solution.py:261
  43.5 5.3 %collective-permute-start.2 = (bf16[32,4,256]{2,1,0:T(4,128)(2,1)S(1)}, bf16[32,4,256]{2,1,0:T(4,128)(2,1)S(1)}, u32[]{:S(2)}, u32[]{:S(2)}) collective-permute-start(bf16[32,4,256]{2,1,0:T(4,128)(2,1)S(1)} %all-to-all-done), channel_id=1, source_target_pairs={{0,192},{64,0},{128,64},{192,128},{1,193},{65,1},{129,65},{193,129... | collective-permute-start | bytes 196616 | tf_op jit(solution)/shard_map/ppermute | solution.py:269
  48.7 4.7 %collective-permute-start.1 = (bf16[32,4,256]{2,1,0:T(4,128)(2,1)S(1)}, bf16[32,4,256]{2,1,0:T(4,128)(2,1)S(1)}, u32[]{:S(2)}, u32[]{:S(2)}) collective-permute-start(bf16[32,4,256]{2,1,0:T(4,128)(2,1)S(1)} %all-to-all-done), channel_id=1, source_target_pairs={{0,128},{64,192},{128,0},{192,64},{1,129},{65,193},{129,1},{193,65... | collective-permute-start | bytes 196616 | tf_op jit(solution)/shard_map/ppermute | solution.py:269
  53.4 3.6 %collective-permute-start = (bf16[32,4,256]{2,1,0:T(4,128)(2,1)S(1)}, bf16[32,4,256]{2,1,0:T(4,128)(2,1)S(1)}, u32[]{:S(2)}, u32[]{:S(2)}) collective-permute-start(bf16[32,4,256]{2,1,0:T(4,128)(2,1)S(1)} %all-to-all-done), channel_id=1, source_target_pairs={{0,64},{64,128},{128,192},{192,0},{1,65},{65,129},{129,193},{193,1... | collective-permute-start | bytes 196616 | tf_op jit(solution)/shard_map/ppermute | solution.py:269
  57.1 3.1 %collective-permute-done.1 = bf16[32,4,256]{2,1,0:T(4,128)(2,1)S(1)} collective-permute-done((bf16[32,4,256]{2,1,0:T(4,128)(2,1)S(1)}, bf16[32,4,256]{2,1,0:T(4,128)(2,1)S(1)}, u32[]{:S(2)}, u32[]{:S(2)}) %collective-permute-start.1) | collective-permute-done | bytes 65568 | tf_op jit(solution)/shard_map/ppermute | solution.py:269
  60.2 1.7 %collective-permute-done = bf16[32,4,256]{2,1,0:T(4,128)(2,1)S(1)} collective-permute-done((bf16[32,4,256]{2,1,0:T(4,128)(2,1)S(1)}, bf16[32,4,256]{2,1,0:T(4,128)(2,1)S(1)}, u32[]{:S(2)}, u32[]{:S(2)}) %collective-permute-start) | collective-permute-done | bytes 65568 | tf_op jit(solution)/shard_map/ppermute | solution.py:269
  62.1 4.9 %collective-permute-start.4 = (bf16[32,16,256]{2,1,0:T(8,128)(2,1)S(1)}, bf16[32,16,256]{2,1,0:T(8,128)(2,1)S(1)}, u32[]{:S(2)}, u32[]{:S(2)}) collective-permute-start(bf16[32,16,256]{2,1,0:T(8,128)(2,1)S(1)} %get-tuple-element.15), channel_id=1, source_target_pairs={{0,512},{256,768},{512,0},{768,256},{1,513},{257,769},{513,1},{769... | collective-permute-start | bytes 786440 | tf_op jit(solution)/shard_map/ppermute | solution.py:269
  67.0 2.5 %collective-permute-start.3 = (bf16[32,16,256]{2,1,0:T(8,128)(2,1)S(1)}, bf16[32,16,256]{2,1,0:T(8,128)(2,1)S(1)}, u32[]{:S(2)}, u32[]{:S(2)}) collective-permute-start(bf16[32,16,256]{2,1,0:T(8,128)(2,1)S(1)} %get-tuple-element.15), channel_id=1, source_target_pairs={{0,256},{256,512},{512,768},{768,0},{1,257},{257,513},{513,769},{7... | collective-permute-start | bytes 786440 | tf_op jit(solution)/shard_map/ppermute | solution.py:269
  69.5 4.6 %collective-permute-start.5 = (bf16[32,16,256]{2,1,0:T(8,128)(2,1)S(1)}, bf16[32,16,256]{2,1,0:T(8,128)(2,1)S(1)}, u32[]{:S(2)}, u32[]{:S(2)}) collective-permute-start(bf16[32,16,256]{2,1,0:T(8,128)(2,1)S(1)} %get-tuple-element.15), channel_id=1, source_target_pairs={{0,768},{256,0},{512,256},{768,512},{1,769},{257,1},{513,257},{769... | collective-permute-start | bytes 786440 | tf_op jit(solution)/shard_map/ppermute | solution.py:269
  74.1 3.9 %collective-permute-done.3 = bf16[32,16,256]{2,1,0:T(8,128)(2,1)S(1)} collective-permute-done((bf16[32,16,256]{2,1,0:T(8,128)(2,1)S(1)}, bf16[32,16,256]{2,1,0:T(8,128)(2,1)S(1)}, u32[]{:S(2)}, u32[]{:S(2)}) %collective-permute-start.3) | collective-permute-done | bytes 262176 | tf_op jit(solution)/shard_map/ppermute | solution.py:269
  78.1 1.9 %collective-permute-start.6 = (bf16[4,32,16,256]{3,2,1,0:T(8,128)(2,1)S(1)}, bf16[4,32,16,256]{3,2,1,0:T(8,128)(2,1)}, u32[]{:S(2)}, u32[]{:S(2)}) collective-permute-start(bf16[4,32,16,256]{3,2,1,0:T(8,128)(2,1)S(1)} %pad_maximum_fusion.own_hbm), channel_id=1, source_target_pairs={{0,32},{32,0},{1,33},{33,1},{2,34},{34,2},{3,35},{35,3},{4,36},{36... | collective-permute-start | bytes 3145736 | tf_op jit(solution)/shard_map/ppermute | solution.py:269
  80.0 0.7 copy.16.labels
  80.8 1.0 fusion.3.bottom
  81.8 1.0 collective-permute-done.6.other_hbm
  82.8 13.5 %all-to-all-done.1.counts_hbm = bf16[32,128,128]{2,1,0:T(8,128)(2,1)S(1)} async-done(((bf16[32,128,128]{2,1,0:T(8,128)(2,1)}), bf16[32,128,128]{2,1,0:T(8,128)(2,1)S(1)}, u32[]{:S(2)}, u32[]{:S(2)}) %all-to-all-start.1) | async-done | bytes 1048608 | tf_op jit(solution)/shard_map/all_to_all | solution.py:261
  96.3 1.0 copy-done.1
  97.3 16.1 %shard_map.141 = (bf16[2,4,2,16,16,256]{5,4,3,2,1,0:T(8,128)(2,1)}, f32[128,1]{1,0:T(8,128)}) custom-call(s32[3]{0:T(128)} %pad_add_fusion.place, s32[32]{0:T(128)} %table_of.1, bf16[128,256]{1,0:T(8,128)(2,1)} %fusion.3.bottom, s32[128,1]{1,0:T(8,128)} %copy.16.labels, f32[1,512]{1,0:T(1,128)} %bitcast.25, bf16[32,128,128]{2,1,0:T(8,128)(2,1)} %copy-done.1, ...), custom_call_target="tpu_custom_call" | custom-call | flops 4000000000 | bytes 12582912 | tf_op jit(solution)/shard_map/pallas_call | solution.py:175
  113.4 6.6 %all_to_all.25.halves = bf16[2,2048,256]{2,1,0:T(8,128)(2,1)S(1)} all-to-all(bf16[2,2048,256]{2,1,0:T(8,128)(2,1)} %bitcast.20), channel_id=1, replica_groups=mesh['x'=4,'yh'=4,'c'=2,'z'=16,'yl'=2] {'c'}, dimensions={0} | all-to-all | bytes 4194304 | tf_op jit(solution)/shard_map/all_to_all | solution.py:261
  120.3 20.5 %all_to_all.26.parts = bf16[8,256,256]{2,1,0:T(8,128)(2,1)S(1)} all-to-all(bf16[8,256,256]{2,1,0:T(8,128)(2,1)S(1)} %bitcast.18), channel_id=1, replica_groups=mesh['x'=4,'yh'=4,'c'=2,'z'=16,'yl'=2] {'x','yl'}, dimensions={0} | all-to-all | bytes 2097152 | tf_op jit(solution)/shard_map/all_to_all | solution.py:261
  141.1 0.7 reshape.31
  141.8 9.2 %all-to-all-start.4 = ((bf16[64,4,256]{2,1,0:T(4,128)(2,1)}), bf16[64,4,256]{2,1,0:T(4,128)(2,1)S(1)}, u32[]{:S(2)}, u32[]{:S(2)}) async-start(bf16[64,4,256]{2,1,0:T(4,128)(2,1)} %reshape.31), calls=%async_computation.4 | async-start | bytes 262144 | tf_op jit(solution)/shard_map/all_to_all | solution.py:261
  151.0 0.6 reduce
  151.6 17.3 %all-to-all-done.4 = bf16[64,4,256]{2,1,0:T(4,128)(2,1)S(1)} async-done(((bf16[64,4,256]{2,1,0:T(4,128)(2,1)}), bf16[64,4,256]{2,1,0:T(4,128)(2,1)S(1)}, u32[]{:S(2)}, u32[]{:S(2)}) %all-to-all-start.4) | async-done | bytes 131104 | tf_op jit(solution)/shard_map/all_to_all | solution.py:261
  168.9 0.7 convert_reduce_fusion
  (22 shorter events, 0.9 us)
Async XLA Ops:
  0.6 1.2 copy-start
  3.1 33.6 %all-to-all-start = ((bf16[32,4,256]{2,1,0:T(4,128)(2,1)}), bf16[32,4,256]{2,1,0:T(4,128)(2,1)S(1)}, u32[]{:S(2)}, u32[]{:S(2)}) async-start(bf16[32,4,256]{2,1,0:T(4,128)(2,1)} %broadcast_in_dim.8), calls=%async_computation | async-start | bytes 131072 | tf_op jit(solution)/shard_map/all_to_all | solution.py:261
  36.7 43.4 %copy-start.7 = (s32[128]{0:T(128)S(1)}, s32[128]{0:T(128)}, u32[]{:S(2)}) copy-start(s32[128]{0:T(128)} %param.18) | copy-start | bytes 1540
  36.7 44.1 %copy-start.3 = (bf16[512,256]{1,0:T(8,128)(2,1)S(1)}, bf16[512,256]{1,0:T(8,128)(2,1)}, u32[]{:S(2)}) copy-start(bf16[512,256]{1,0:T(8,128)(2,1)} %param.20) | copy-start | bytes 786436
  36.7 44.1 %copy-start.5 = (bf16[13,512]{1,0:T(8,128)(2,1)S(1)}, bf16[13,512]{1,0:T(8,128)(2,1)}, u32[]{:S(2)}) copy-start(bf16[13,512]{1,0:T(8,128)(2,1)} %param.19) | copy-start | bytes 39940
  36.7 44.1 %copy-start.6 = (bf16[13,128]{1,0:T(8,128)(2,1)S(1)}, bf16[13,128]{1,0:T(8,128)(2,1)}, u32[]{:S(2)}) copy-start(bf16[13,128]{1,0:T(8,128)(2,1)} %param.17) | copy-start | bytes 9988
  36.7 59.6 %all-to-all-start.1 = ((bf16[32,128,128]{2,1,0:T(8,128)(2,1)}), bf16[32,128,128]{2,1,0:T(8,128)(2,1)S(1)}, u32[]{:S(2)}, u32[]{:S(2)}) async-start(bf16[32,128,128]{2,1,0:T(8,128)(2,1)} %bitcast.19), calls=%async_computation.1 | async-start | bytes 2097152 | tf_op jit(solution)/shard_map/all_to_all | solution.py:261
  43.5 13.6 %collective-permute-start.2 = (bf16[32,4,256]{2,1,0:T(4,128)(2,1)S(1)}, bf16[32,4,256]{2,1,0:T(4,128)(2,1)S(1)}, u32[]{:S(2)}, u32[]{:S(2)}) collective-permute-start(bf16[32,4,256]{2,1,0:T(4,128)(2,1)S(1)} %all-to-all-done), channel_id=1, source_target_pairs={{0,192},{64,0},{128,64},{192,128},{1,193},{65,1},{129,65},{193,129... | collective-permute-start | bytes 196616 | tf_op jit(solution)/shard_map/ppermute | solution.py:269
  48.7 11.5 %collective-permute-start.1 = (bf16[32,4,256]{2,1,0:T(4,128)(2,1)S(1)}, bf16[32,4,256]{2,1,0:T(4,128)(2,1)S(1)}, u32[]{:S(2)}, u32[]{:S(2)}) collective-permute-start(bf16[32,4,256]{2,1,0:T(4,128)(2,1)S(1)} %all-to-all-done), channel_id=1, source_target_pairs={{0,128},{64,192},{128,0},{192,64},{1,129},{65,193},{129,1},{193,65... | collective-permute-start | bytes 196616 | tf_op jit(solution)/shard_map/ppermute | solution.py:269
  53.4 8.4 %collective-permute-start = (bf16[32,4,256]{2,1,0:T(4,128)(2,1)S(1)}, bf16[32,4,256]{2,1,0:T(4,128)(2,1)S(1)}, u32[]{:S(2)}, u32[]{:S(2)}) collective-permute-start(bf16[32,4,256]{2,1,0:T(4,128)(2,1)S(1)} %all-to-all-done), channel_id=1, source_target_pairs={{0,64},{64,128},{128,192},{192,0},{1,65},{65,129},{129,193},{193,1... | collective-permute-start | bytes 196616 | tf_op jit(solution)/shard_map/ppermute | solution.py:269
  62.1 12.0 %collective-permute-start.4 = (bf16[32,16,256]{2,1,0:T(8,128)(2,1)S(1)}, bf16[32,16,256]{2,1,0:T(8,128)(2,1)S(1)}, u32[]{:S(2)}, u32[]{:S(2)}) collective-permute-start(bf16[32,16,256]{2,1,0:T(8,128)(2,1)S(1)} %get-tuple-element.15), channel_id=1, source_target_pairs={{0,512},{256,768},{512,0},{768,256},{1,513},{257,769},{513,1},{769... | collective-permute-start | bytes 786440 | tf_op jit(solution)/shard_map/ppermute | solution.py:269
  67.0 11.0 %collective-permute-start.3 = (bf16[32,16,256]{2,1,0:T(8,128)(2,1)S(1)}, bf16[32,16,256]{2,1,0:T(8,128)(2,1)S(1)}, u32[]{:S(2)}, u32[]{:S(2)}) collective-permute-start(bf16[32,16,256]{2,1,0:T(8,128)(2,1)S(1)} %get-tuple-element.15), channel_id=1, source_target_pairs={{0,256},{256,512},{512,768},{768,0},{1,257},{257,513},{513,769},{7... | collective-permute-start | bytes 786440 | tf_op jit(solution)/shard_map/ppermute | solution.py:269
  69.5 8.5 %collective-permute-start.5 = (bf16[32,16,256]{2,1,0:T(8,128)(2,1)S(1)}, bf16[32,16,256]{2,1,0:T(8,128)(2,1)S(1)}, u32[]{:S(2)}, u32[]{:S(2)}) collective-permute-start(bf16[32,16,256]{2,1,0:T(8,128)(2,1)S(1)} %get-tuple-element.15), channel_id=1, source_target_pairs={{0,768},{256,0},{512,256},{768,512},{1,769},{257,1},{513,257},{769... | collective-permute-start | bytes 786440 | tf_op jit(solution)/shard_map/ppermute | solution.py:269
  78.1 18.2 %copy-start.2 = (bf16[4,32,16,256]{3,2,1,0:T(8,128)(2,1)}, bf16[4,32,16,256]{3,2,1,0:T(8,128)(2,1)S(1)}, u32[]{:S(2)}) copy-start(bf16[4,32,16,256]{3,2,1,0:T(8,128)(2,1)S(1)} %pad_maximum_fusion.own_hbm) | copy-start | bytes 3145732
  78.1 4.7 %collective-permute-start.6 = (bf16[4,32,16,256]{3,2,1,0:T(8,128)(2,1)S(1)}, bf16[4,32,16,256]{3,2,1,0:T(8,128)(2,1)}, u32[]{:S(2)}, u32[]{:S(2)}) collective-permute-start(bf16[4,32,16,256]{3,2,1,0:T(8,128)(2,1)S(1)} %pad_maximum_fusion.own_hbm), channel_id=1, source_target_pairs={{0,32},{32,0},{1,33},{33,1},{2,34},{34,2},{3,35},{35,3},{4,36},{36... | collective-permute-start | bytes 3145736 | tf_op jit(solution)/shard_map/ppermute | solution.py:269
  96.3 1.0 copy-start.1
  120.3 30.7 %copy-start.4 = (f32[128,1]{1,0:T(8,128)S(1)}, f32[128,1]{1,0:T(8,128)}, u32[]{:S(2)}) copy-start(f32[128,1]{1,0:T(8,128)} %get-tuple-element.13) | copy-start | bytes 1540
  141.8 27.1 %all-to-all-start.4 = ((bf16[64,4,256]{2,1,0:T(4,128)(2,1)}), bf16[64,4,256]{2,1,0:T(4,128)(2,1)S(1)}, u32[]{:S(2)}, u32[]{:S(2)}) async-start(bf16[64,4,256]{2,1,0:T(4,128)(2,1)} %reshape.31), calls=%async_computation.4 | async-start | bytes 262144 | tf_op jit(solution)/shard_map/all_to_all | solution.py:261

commit v4 on v3

--- a/solution.py
+++ b/solution.py
@@ -47,27 +47,25 @@
     return slice(k * E, (k + 1) * E)
 
 
+WIDE = (TABLES + 1) * E
+TOP = 512
+PIECES = ((0, WIDE), (WIDE, WIDE), (2 * WIDE, 2 * WIDE), (4 * WIDE, 2 * TOP))
+PACKED = 4 * WIDE + 2 * TOP
+
+
 def step_kernel(
     place,
     table_of,
     bottom,
     labels,
     w_out,
-    counts_hbm,
-    own_hbm,
-    other_hbm,
-    down_hbm,
-    up_hbm,
-    top1_hbm,
-    top2_hbm,
+    counts,
+    own,
+    other,
+    packed_hbm,
     grads,
     logits_out,
-    counts,
-    looked,
-    cross_down,
-    cross_up,
-    w_top1,
-    w_top2,
+    packed,
     feats,
     scaled,
     emb_grad,
@@ -75,19 +73,28 @@
     filled,
     arrived,
 ):
-    moves = (
-        (counts_hbm, counts),
-        (own_hbm, looked.at[0]),
-        (other_hbm, looked.at[1]),
-        (down_hbm, cross_down),
-        (up_hbm, cross_up),
-        (top1_hbm, w_top1),
-        (top2_hbm, w_top2),
-    )
-    copies = [pltpu.make_async_copy(*move, arrived.at[i]) for i, move in enumerate(moves)]
+    copies = [
+        pltpu.make_async_copy(
+            packed_hbm.at[pl.ds(first, rows)], packed.at[pl.ds(first, rows)], arrived.at[i]
+        )
+        for i, (first, rows) in enumerate(PIECES)
+    ]
     for copy in copies:
         copy.start()
-    my_x, my_yh, my_c = place[0], place[1], place[2]
+    my_x, my_c = place[0], place[2]
+
+    def down(k):
+        return packed[cols(k), :]
+
+    def up(k):
+        return packed[cols(TABLES + 1 + k), :]
+
+    def top1(k, half):
+        return packed[cols((2 + half) * (TABLES + 1) + k), :]
+
+    def top2(half):
+        return packed[4 * WIDE + half * TOP : 4 * WIDE + (half + 1) * TOP, :]
+
     for t in range(TABLES):
         filled[t] = 0
     for m in range(SHARDS):
@@ -97,105 +104,126 @@
         filled[t] = k + 1
 
     feats[:, cols(0)] = bottom[...].astype(F32)
-    for copy in copies[:3]:
-        copy.wait()
     for t in range(TABLES):
         acc = None
         for k in range(PER):
             m = order[t * PER + k]
+            turns = [lax.rem(my_x + X - x, X) for x in range(X)]
+            near = [own[k_x, m] for k_x in turns]
+            far = [other[k_x, m] for k_x in turns]
             rows = jnp.concatenate(
-                [
-                    looked[lax.bitwise_xor(my_c, c), lax.rem(my_x + X - x, X), m]
-                    for c in range(CORES)
-                    for x in range(X)
-                ],
+                [jnp.where(my_c == 0, a, b) for a, b in zip(near, far)]
+                + [jnp.where(my_c == 0, b, a) for a, b in zip(near, far)],
                 axis=0,
             )
             term = dot(counts[m], rows)
             acc = term if acc is None else acc + term
         feats[:, cols(t + 1)] = acc
 
-    copies[3].wait()
-    low = split_dot(feats[...], cross_down[...])
+    copies[0].wait()
+    low = split_dot(feats[...], packed[0:WIDE, :])
     low_high = low.astype(BF)
     low_rest = (low - low_high.astype(F32)).astype(BF)
-    copies[4].wait()
-    copies[5].wait()
-    pre_one = None
+    copies[1].wait()
+    copies[2].wait()
+    pre_one = [None, None]
     for k in range(TABLES + 1):
-        scale = dot(low_high, cross_up[:, cols(k)]) + dot(low_rest, cross_up[:, cols(k)])
+        scale = dot(low_high, up(k)) + dot(low_rest, up(k))
         scaled[:, cols(k)] = scale
         feat = feats[:, cols(k)]
-        term = split_dot(feat * scale + feat, w_top1[cols(k), :])
-        pre_one = term if pre_one is None else pre_one + term
-    copies[6].wait()
+        crossed = feat * scale + feat
+        for half in range(2):
+            term = split_dot(crossed, top1(k, half))
+            pre_one[half] = term if k == 0 else pre_one[half] + term
+    pre_one = jnp.concatenate(pre_one, axis=1)
+    copies[3].wait()
     sig_one = jax.nn.sigmoid(pre_one)
-    pre_two = split_dot(pre_one * sig_one, w_top2[...])
+    act_one = pre_one * sig_one
+    pre_two = jnp.concatenate([split_dot(act_one, top2(0)), split_dot(act_one, top2(1))], axis=1)
     sig_two = jax.nn.sigmoid(pre_two)
     head = w_out[...]
     logits = jnp.sum(pre_two * sig_two * head, axis=1, keepdims=True)
     logits_out[...] = logits
     logit_grad = (jax.nn.sigmoid(logits) - labels[...].astype(F32)) * (1.0 / 32.0)
     grad_two = (logit_grad * head * silu_slope(pre_two, sig_two)).astype(BF)
-    grad_one = (dot_nt(grad_two, w_top2[...]) * silu_slope(pre_one, sig_one)).astype(BF)
+    grad_act = dot_nt(grad_two[:, cols(0)], top2(0)) + dot_nt(grad_two[:, cols(1)], top2(1))
+    grad_one = (grad_act * silu_slope(pre_one, sig_one)).astype(BF)
     low_grad = None
     for k in range(TABLES + 1):
-        part = dot_nt(grad_one, w_top1[cols(k), :])
-        term = dot_nt((part * feats[:, cols(k)]).astype(BF), cross_up[:, cols(k)])
+        part = dot_nt(grad_one[:, cols(0)], top1(k, 0)) + dot_nt(grad_one[:, cols(1)], top1(k, 1))
+        term = dot_nt((part * feats[:, cols(k)]).astype(BF), up(k))
         low_grad = term if low_grad is None else low_grad + term
         if k > 0:
             scaled[:, cols(k)] = part * (scaled[:, cols(k)] + 1.0)
     low_grad = low_grad.astype(BF)
     for t in range(TABLES):
-        back = dot_nt(low_grad, cross_down[cols(t + 1), :])
+        back = dot_nt(low_grad, down(t + 1))
         emb_grad[t] = (scaled[:, cols(t + 1)] + back).astype(BF)
 
-    to = lax.broadcasted_iota(jnp.int32, (LOOK, LOOK), 0)
-    at = lax.broadcasted_iota(jnp.int32, (LOOK, LOOK), 1)
-    source = to - to % 16 + ((my_yh + YH - to // 4 % YH) % YH) * 4 + to % 4
-    turned = (at == source).astype(BF)
-
     def one_shard(m, carry):
-        picked = dot_nt(turned, counts[m]).astype(BF)
-        terms = dot(picked, emb_grad[table_of[m]]).astype(BF)
+        terms = dot_tn(counts[m], emb_grad[table_of[m]]).astype(BF)
         for c in range(CORES):
             for x in range(X):
                 at = (c * X + x) * 16
                 grads[c, x, m % YL, m // YL] = terms[at : at + 16]
         return carry
 
-    lax.fori_loop(0, SHARDS, one_shard, 0, unroll=4)
-
-
-def run_step(place, table_of, small, large):
+    lax.fori_loop(0, SHARDS, one_shard, 0, unroll=8)
+
+
+def run_step(place, table_of, small, packed):
     smem = pl.BlockSpec(memory_space=pltpu.SMEM)
     vmem = pl.BlockSpec(memory_space=pltpu.VMEM)
     hbm = pl.BlockSpec(memory_space=pl.ANY)
-    counts, own, _, *weights = large
     return pl.pallas_call(
         step_kernel,
         out_shape=(
             jax.ShapeDtypeStruct((CORES, X, YL, Z, 16, E), BF),
             jax.ShapeDtypeStruct((N, 1), F32),
         ),
-        in_specs=[smem, smem] + [vmem] * len(small) + [hbm] * len(large),
+        in_specs=[smem, smem] + [vmem] * len(small) + [hbm],
         out_specs=(vmem, vmem),
         scratch_shapes=[
-            pltpu.VMEM(counts.shape, BF),
-            pltpu.VMEM((CORES, *own.shape), BF),
-            *[pltpu.VMEM(w.shape, BF) for w in weights],
+            pltpu.VMEM((PACKED, E), BF),
             pltpu.VMEM((N, (TABLES + 1) * E), F32),
             pltpu.VMEM((N, (TABLES + 1) * E), F32),
             pltpu.VMEM((TABLES, N, E), BF),
             pltpu.SMEM((SHARDS,), jnp.int32),
             pltpu.SMEM((TABLES,), jnp.int32),
-            pltpu.SemaphoreType.DMA((len(large),)),
+            pltpu.SemaphoreType.DMA((len(PIECES),)),
         ],
-        compiler_params=pltpu.CompilerParams(vmem_limit_bytes=60 * 2**20),
+        compiler_params=pltpu.CompilerParams(vmem_limit_bytes=46 * 2**20),
         cost_estimate=pl.CostEstimate(
             flops=4 * 10**9, bytes_accessed=12 * 2**20, transcendentals=2 * 10**5
         ),
-    )(place, table_of, *small, *large)
+    )(place, table_of, *small, packed)
+
+
+def pack_kernel(down, up, top1, top2, packed, arrived):
+    moves = [(down, 0)]
+    moves += [(up.at[:, pl.ds(k * E, E)], WIDE + k * E) for k in range(TABLES + 1)]
+    moves += [(top1.at[:, pl.ds(h * E, E)], (2 + h) * WIDE) for h in range(2)]
+    moves += [(top2.at[:, pl.ds(h * E, E)], 4 * WIDE + h * TOP) for h in range(2)]
+    copies = [
+        pltpu.make_async_copy(source, packed.at[pl.ds(first, source.shape[0])], arrived.at[i])
+        for i, (source, first) in enumerate(moves)
+    ]
+    for copy in copies:
+        copy.start()
+    for copy in copies:
+        copy.wait()
+
+
+def pack(*weights):
+    anywhere = pl.BlockSpec(memory_space=pl.ANY)
+    return pl.pallas_call(
+        pack_kernel,
+        out_shape=jax.ShapeDtypeStruct((PACKED, E), BF),
+        in_specs=[anywhere] * len(weights),
+        out_specs=anywhere,
+        scratch_shapes=[pltpu.SemaphoreType.DMA((TABLES + 6,))],
+        cost_estimate=pl.CostEstimate(flops=0, bytes_accessed=10 * 2**20, transcendentals=0),
+    )(*weights)
 
 
 def lanes_kernel(place, counts, out):
@@ -225,7 +253,7 @@
     )(place, counts)
 
 
-def pair_kernel(halves, out):
+def pair_kernel(_, halves, out):
     def one_block(i, carry):
         at = pl.ds(i * 256, 256)
         out[at] = (halves[0, at].astype(F32) + halves[1, at].astype(F32)).astype(BF)
@@ -234,27 +262,31 @@
     lax.fori_loop(0, out.shape[0] // 256, one_block, 0, unroll=2)
 
 
-def sum_kernel(parts, out):
+def sum_kernel(place, parts, out):
     to = lax.broadcasted_iota(jnp.int32, (E, E), 0)
     at = lax.broadcasted_iota(jnp.int32, (E, E), 1)
-    turned = (at == (to // 4 % Z) * 16 + (to // 64) * 4 + to % 4).astype(BF)
+    back = (place[1] + YH - to // 64) % YH
+    turned = (at == (to // 4 % Z) * 16 + back * 4 + to % 4).astype(BF)
     total = parts[0].astype(F32)
     for i in range(1, parts.shape[0]):
         total = total + parts[i].astype(F32)
     out[...] = dot(turned, total.astype(BF)).astype(BF)
 
 
-def fold(kernel, parts):
+def fold(kernel, place, parts):
     return pl.pallas_call(
         kernel,
         out_shape=jax.ShapeDtypeStruct(parts.shape[1:], BF),
-        in_specs=[pl.BlockSpec(memory_space=pltpu.VMEM)],
+        in_specs=[
+            pl.BlockSpec(memory_space=pltpu.SMEM),
+            pl.BlockSpec(memory_space=pltpu.VMEM),
+        ],
         out_specs=pl.BlockSpec(memory_space=pltpu.VMEM),
         compiler_params=pltpu.CompilerParams(vmem_limit_bytes=12 * 2**20),
         cost_estimate=pl.CostEstimate(
             flops=5 * 10**7, bytes_accessed=3 * 2**20, transcendentals=0
         ),
-    )(parts)
+    )(place, parts)
 
 
 def swap(value, axes):
@@ -298,6 +330,8 @@
     looked = jnp.concatenate(
         [looked] + [turn(looked, "yh", YH, k) for k in range(1, YH)], axis=1
     )
+    looked, *weights = lax.optimization_barrier((looked, cross_down, cross_up, w_top1, w_top2))
+    packed = pack(*weights)
     looked = jnp.stack([looked] + [turn(looked, "x", X, k) for k in range(1, X)])
     others = turn(looked, "c", CORES, 1)
 
@@ -310,12 +344,12 @@
     grads, logits = run_step(
         place,
         table_of,
-        (bottom, labels.reshape(N, 1), w_out.reshape(1, -1)),
-        (counts, looked, others, cross_down, cross_up, w_top1, w_top2),
+        (bottom, labels.reshape(N, 1), w_out.reshape(1, -1), counts, looked, others),
+        packed,
     )
     grads = swap(grads.reshape(CORES, X * YL * Z * 16, E), "c")
-    grads = fold(pair_kernel, grads).reshape(X * YL, Z * 16, E)
-    grads = fold(sum_kernel, swap(grads, ("x", "yl"))).reshape(YH * Z, 4, E)
+    grads = fold(pair_kernel, place, grads).reshape(X * YL, Z * 16, E)
+    grads = fold(sum_kernel, place, swap(grads, ("x", "yl"))).reshape(YH * Z, 4, E)
     grads = add_up(swap(grads, ("yh", "z")))
     return grads, logits.reshape(N)
 

time: 171 us -> 317 us (1.85)
  Pallas kernels: 22.8 us -> 178 us
  waiting for transfers between devices: 47 us -> 38.3 us
  starting transfers between devices: 63.8 us -> 68.5 us
  blocking collectives: 27.1 us -> 23.6 us
    pallas_call x0 -> x1, Pallas kernels: none -> 160 us  [pack(): pl.pallas_call(pack_kernel, out_shape=jax.ShapeDtypeStruct((PACKED, E), B...]
    all_to_all x3, waiting for transfers between devices: 37.3 us -> 23.7 us  [swap(): return lax.all_to_all(value, axes, split_axis=0, concat_axis=0, tiled=True)]
    all_to_all x3, starting transfers between devices: 36.3 us -> 42.9 us  [swap(): return lax.all_to_all(value, axes, split_axis=0, concat_axis=0, tiled=True)]
    pallas_call x1, Pallas kernels: 16.1 us -> 10.3 us  [run_step(): pl.pallas_call(step_kernel, out_shape=(jax.ShapeDtypeStruct((CORES, X, YL...]
    ppermute x7, waiting for transfers between devices: 9.72 us -> 14.6 us  [turn(): lax.ppermute(value, axis, [(i, (i + shift) % size) for i in range(size)])]
    all_to_all x2, blocking collectives: 27.1 us -> 23.6 us  [swap(): return lax.all_to_all(value, axes, split_axis=0, concat_axis=0, tiled=True)]
  transfers between devices with their start and end apart: 10 -> 10, of which waited for: 7 -> 7; matrix products, arithmetic and copies ran while one was open for 2% -> 1% of each run, Pallas kernels for 4% -> 53%
where the time goes in v4:
time: 317 us; the launch traced here: 316 us
  Pallas kernels  178 us (56%)
  starting transfers between devices  68.5 us (22%)
  waiting for transfers between devices  38.3 us (12%)
  blocking collectives  23.6 us (7%)
  local copies, waits for them, and re-layouts  3.26 us (1%)
    pallas_call x1, Pallas kernels, pack(): pl.pallas_call(pack_kernel, out_shape=jax.ShapeDtypeStruct((PACKED, E), B...  160 us
    all_to_all x3, starting transfers between devices, swap(): return lax.all_to_all(value, axes, split_axis=0, concat_axis=0, tiled=True)  42.9 us
    ppermute x7, starting transfers between devices, turn(): lax.ppermute(value, axis, [(i, (i + shift) % size) for i in range(size)])  25.7 us
    all_to_all x3, waiting for transfers between devices, swap(): return lax.all_to_all(value, axes, split_axis=0, concat_axis=0, tiled=True)  23.7 us
    all_to_all x2, blocking collectives, swap(): return lax.all_to_all(value, axes, split_axis=0, concat_axis=0, tiled=True)  23.6 us
    ppermute x7, waiting for transfers between devices, turn(): lax.ppermute(value, axis, [(i, (i + shift) % size) for i in range(size)])  14.6 us
    pallas_call x1, Pallas kernels, run_step(): pl.pallas_call(step_kernel, out_shape=(jax.ShapeDtypeStruct((CORES, X, YL...  10.3 us
  transfers between devices with their start and end apart: 10, of which 7 were waited for; matrix products, arithmetic and copies ran while one was open for 1% of the time, Pallas kernels for 53%

profile of v4, /device:TPU:8, one launch (start us, length us, event | category | flops | bytes accessed | tf_op | source)
XLA Modules:
  0.0 316.4 jit_solution(11128150624790583237)
XLA Ops:
  0.7 0.8 dynamic-slice_bitcast_fusion
  1.9 0.6 gather_fusion
  2.4 0.6 broadcast_in_dim.8
  3.1 20.4 %all-to-all-start = ((bf16[32,4,256]{2,1,0:T(4,128)(2,1)}), bf16[32,4,256]{2,1,0:T(4,128)(2,1)S(1)}, u32[]{:S(2)}, u32[]{:S(2)}) async-start(bf16[32,4,256]{2,1,0:T(4,128)(2,1)} %broadcast_in_dim.8), calls=%async_computation | async-start | bytes 131072 | tf_op jit(solution)/shard_map/all_to_all | solution.py:293
  23.5 0.7 pad_add_fusion.place._
  24.1 6.1 %shard_map.140 = bf16[4096,128]{1,0:T(8,128)(2,1)} custom-call(s32[3]{0:T(128)} %pad_add_fusion.place._, s32[4096,128]{1,0:T(8,128)} %counts), custom_call_target="tpu_custom_call" | custom-call | flops 200000000 | bytes 3145728 | tf_op jit(solution)/shard_map/pallas_call | solution.py:241
  30.3 6.4 %all-to-all-done = bf16[32,4,256]{2,1,0:T(4,128)(2,1)S(1)} async-done(((bf16[32,4,256]{2,1,0:T(4,128)(2,1)}), bf16[32,4,256]{2,1,0:T(4,128)(2,1)S(1)}, u32[]{:S(2)}, u32[]{:S(2)}) %all-to-all-start) | async-done | bytes 65568 | tf_op jit(solution)/shard_map/all_to_all | solution.py:293
  36.7 6.8 %all-to-all-start.1 = ((bf16[32,128,128]{2,1,0:T(8,128)(2,1)}), bf16[32,128,128]{2,1,0:T(8,128)(2,1)S(1)}, u32[]{:S(2)}, u32[]{:S(2)}) async-start(bf16[32,128,128]{2,1,0:T(8,128)(2,1)} %bitcast.20), calls=%async_computation.1 | async-start | bytes 2097152 | tf_op jit(solution)/shard_map/all_to_all | solution.py:293
  43.5 5.3 %collective-permute-start.2 = (bf16[32,4,256]{2,1,0:T(4,128)(2,1)S(1)}, bf16[32,4,256]{2,1,0:T(4,128)(2,1)S(1)}, u32[]{:S(2)}, u32[]{:S(2)}) collective-permute-start(bf16[32,4,256]{2,1,0:T(4,128)(2,1)S(1)} %all-to-all-done), channel_id=1, source_target_pairs={{0,192},{64,0},{128,64},{192,128},{1,193},{65,1},{129,65},{193,129... | collective-permute-start | bytes 196616 | tf_op jit(solution)/shard_map/ppermute | solution.py:301
  48.8 4.7 %collective-permute-start.1 = (bf16[32,4,256]{2,1,0:T(4,128)(2,1)S(1)}, bf16[32,4,256]{2,1,0:T(4,128)(2,1)S(1)}, u32[]{:S(2)}, u32[]{:S(2)}) collective-permute-start(bf16[32,4,256]{2,1,0:T(4,128)(2,1)S(1)} %all-to-all-done), channel_id=1, source_target_pairs={{0,128},{64,192},{128,0},{192,64},{1,129},{65,193},{129,1},{193,65... | collective-permute-start | bytes 196616 | tf_op jit(solution)/shard_map/ppermute | solution.py:301
  53.5 3.6 %collective-permute-start = (bf16[32,4,256]{2,1,0:T(4,128)(2,1)S(1)}, bf16[32,4,256]{2,1,0:T(4,128)(2,1)S(1)}, u32[]{:S(2)}, u32[]{:S(2)}) collective-permute-start(bf16[32,4,256]{2,1,0:T(4,128)(2,1)S(1)} %all-to-all-done), channel_id=1, source_target_pairs={{0,64},{64,128},{128,192},{192,0},{1,65},{65,129},{129,193},{193,1... | collective-permute-start | bytes 196616 | tf_op jit(solution)/shard_map/ppermute | solution.py:301
  57.1 3.1 collective-permute-done.1
  60.3 1.7 collective-permute-done
  62.1 4.7 %collective-permute-start.5 = (bf16[32,16,256]{2,1,0:T(8,128)(2,1)S(1)}, bf16[32,16,256]{2,1,0:T(8,128)(2,1)S(1)}, u32[]{:S(2)}, u32[]{:S(2)}) collective-permute-start(bf16[32,16,256]{2,1,0:T(8,128)(2,1)S(1)} %pad_maximum_fusion.1), channel_id=1, source_target_pairs={{0,768},{256,0},{512,256},{768,512},{1,769},{257,1},{513,257},{769... | collective-permute-start | bytes 786440 | tf_op jit(solution)/shard_map/ppermute | solution.py:301
  66.8 2.7 collective-permute-start.4
  69.5 2.8 collective-permute-start.3
  72.3 4.2 %collective-permute-done.5 = bf16[32,16,256]{2,1,0:T(8,128)(2,1)S(1)} collective-permute-done((bf16[32,16,256]{2,1,0:T(8,128)(2,1)S(1)}, bf16[32,16,256]{2,1,0:T(8,128)(2,1)S(1)}, u32[]{:S(2)}, u32[]{:S(2)}) %collective-permute-start.5) | collective-permute-done | bytes 262176 | tf_op jit(solution)/shard_map/ppermute | solution.py:301
  76.5 2.8 collective-permute-done.4
  79.3 2.8 collective-permute-done.3
  82.2 1.9 collective-permute-start.6
  84.3 1.3 fusion.3.bottom
  85.6 160.1 %shard_map.141.packed_hbm = bf16[10240,256]{1,0:T(8,128)(2,1)} custom-call(bf16[2304,256]{1,0:T(8,128)(2,1)} %down, bf16[256,2304]{1,0:T(8,128)(2,1)} %up, bf16[2304,512]{1,0:T(8,128)(2,1)} %top1, bf16[512,512]{1,0:T(8,128)(2,1)} %top2), custom_call_target="tpu_custom_call" | custom-call | bytes 10485760 | tf_op jit(solution)/shard_map/pallas_call | solution.py:219
  245.7 10.3 %shard_map.142 = (bf16[2,4,2,16,16,256]{5,4,3,2,1,0:T(8,128)(2,1)S(1)}, f32[128,1]{1,0:T(8,128)S(1)}) custom-call(s32[3]{0:T(128)S(1)} %copy-done.1, s32[32]{0:T(128)S(1)} %copy-done.3, bf16[128,256]{1,0:T(8,128)(2,1)S(1)} %fusion.3.bottom, s32[128,1]{1,0:T(8,128)S(1)} %copy.16.labels, f32[1,512]{1,0:T(1,128)S(1)} %bitcast.19, ...), custom_call_target="tpu_custom_call" | custom-call | flops 4000000000 | bytes 12582912 | tf_op jit(solution)/shard_map/pallas_call | solution.py:178
  256.0 5.4 %all_to_all.25.halves = bf16[2,2048,256]{2,1,0:T(8,128)(2,1)S(1)} all-to-all(bf16[2,2048,256]{2,1,0:T(8,128)(2,1)S(1)} %bitcast.18), channel_id=1, replica_groups=mesh['x'=4,'yh'=4,'c'=2,'z'=16,'yl'=2] {'c'}, dimensions={0} | all-to-all | bytes 4194304 | tf_op jit(solution)/shard_map/all_to_all | solution.py:293
  261.4 0.8 shard_map.143
  262.2 18.2 %all_to_all.26.parts = bf16[8,256,256]{2,1,0:T(8,128)(2,1)S(1)} all-to-all(bf16[8,256,256]{2,1,0:T(8,128)(2,1)S(1)} %bitcast.17), channel_id=1, replica_groups=mesh['x'=4,'yh'=4,'c'=2,'z'=16,'yl'=2] {'x','yl'}, dimensions={0} | all-to-all | bytes 2097152 | tf_op jit(solution)/shard_map/all_to_all | solution.py:293
  280.5 0.9 shard_map.144
  281.4 0.7 reshape.31
  282.1 15.7 %all-to-all-start.4 = ((bf16[64,4,256]{2,1,0:T(4,128)(2,1)}), bf16[64,4,256]{2,1,0:T(4,128)(2,1)S(1)}, u32[]{:S(2)}, u32[]{:S(2)}) async-start(bf16[64,4,256]{2,1,0:T(4,128)(2,1)} %reshape.31), calls=%async_computation.4 | async-start | bytes 262144 | tf_op jit(solution)/shard_map/all_to_all | solution.py:293
  297.7 0.6 reduce
  298.4 17.3 %all-to-all-done.4 = bf16[64,4,256]{2,1,0:T(4,128)(2,1)S(1)} async-done(((bf16[64,4,256]{2,1,0:T(4,128)(2,1)}), bf16[64,4,256]{2,1,0:T(4,128)(2,1)S(1)}, u32[]{:S(2)}, u32[]{:S(2)}) %all-to-all-start.4) | async-done | bytes 131104 | tf_op jit(solution)/shard_map/all_to_all | solution.py:293
  315.7 0.7 convert_reduce_fusion
  (21 shorter events, 0.9 us)
Async XLA Ops:
  0.6 1.2 copy-start
  3.1 33.6 %all-to-all-start = ((bf16[32,4,256]{2,1,0:T(4,128)(2,1)}), bf16[32,4,256]{2,1,0:T(4,128)(2,1)S(1)}, u32[]{:S(2)}, u32[]{:S(2)}) async-start(bf16[32,4,256]{2,1,0:T(4,128)(2,1)} %broadcast_in_dim.8), calls=%async_computation | async-start | bytes 131072 | tf_op jit(solution)/shard_map/all_to_all | solution.py:293
  36.7 47.5 %copy-start.6 = (s32[128]{0:T(128)S(1)}, s32[128]{0:T(128)}, u32[]{:S(2)}) copy-start(s32[128]{0:T(128)} %param.18) | copy-start | bytes 1540
  36.7 47.6 %copy-start.4 = (bf16[13,512]{1,0:T(8,128)(2,1)S(1)}, bf16[13,512]{1,0:T(8,128)(2,1)}, u32[]{:S(2)}) copy-start(bf16[13,512]{1,0:T(8,128)(2,1)} %param.19) | copy-start | bytes 39940
  36.7 47.6 %copy-start.5 = (bf16[13,128]{1,0:T(8,128)(2,1)S(1)}, bf16[13,128]{1,0:T(8,128)(2,1)}, u32[]{:S(2)}) copy-start(bf16[13,128]{1,0:T(8,128)(2,1)} %param.17) | copy-start | bytes 9988
  36.7 209.0 %all-to-all-start.1 = ((bf16[32,128,128]{2,1,0:T(8,128)(2,1)}), bf16[32,128,128]{2,1,0:T(8,128)(2,1)S(1)}, u32[]{:S(2)}, u32[]{:S(2)}) async-start(bf16[32,128,128]{2,1,0:T(8,128)(2,1)} %bitcast.20), calls=%async_computation.1 | async-start | bytes 2097152 | tf_op jit(solution)/shard_map/all_to_all | solution.py:293
  43.5 13.6 %collective-permute-start.2 = (bf16[32,4,256]{2,1,0:T(4,128)(2,1)S(1)}, bf16[32,4,256]{2,1,0:T(4,128)(2,1)S(1)}, u32[]{:S(2)}, u32[]{:S(2)}) collective-permute-start(bf16[32,4,256]{2,1,0:T(4,128)(2,1)S(1)} %all-to-all-done), channel_id=1, source_target_pairs={{0,192},{64,0},{128,64},{192,128},{1,193},{65,1},{129,65},{193,129... | collective-permute-start | bytes 196616 | tf_op jit(solution)/shard_map/ppermute | solution.py:301
  48.8 11.5 %collective-permute-start.1 = (bf16[32,4,256]{2,1,0:T(4,128)(2,1)S(1)}, bf16[32,4,256]{2,1,0:T(4,128)(2,1)S(1)}, u32[]{:S(2)}, u32[]{:S(2)}) collective-permute-start(bf16[32,4,256]{2,1,0:T(4,128)(2,1)S(1)} %all-to-all-done), channel_id=1, source_target_pairs={{0,128},{64,192},{128,0},{192,64},{1,129},{65,193},{129,1},{193,65... | collective-permute-start | bytes 196616 | tf_op jit(solution)/shard_map/ppermute | solution.py:301
  53.5 8.4 %collective-permute-start = (bf16[32,4,256]{2,1,0:T(4,128)(2,1)S(1)}, bf16[32,4,256]{2,1,0:T(4,128)(2,1)S(1)}, u32[]{:S(2)}, u32[]{:S(2)}) collective-permute-start(bf16[32,4,256]{2,1,0:T(4,128)(2,1)S(1)} %all-to-all-done), channel_id=1, source_target_pairs={{0,64},{64,128},{128,192},{192,0},{1,65},{65,129},{129,193},{193,1... | collective-permute-start | bytes 196616 | tf_op jit(solution)/shard_map/ppermute | solution.py:301
  62.1 14.4 %collective-permute-start.5 = (bf16[32,16,256]{2,1,0:T(8,128)(2,1)S(1)}, bf16[32,16,256]{2,1,0:T(8,128)(2,1)S(1)}, u32[]{:S(2)}, u32[]{:S(2)}) collective-permute-start(bf16[32,16,256]{2,1,0:T(8,128)(2,1)S(1)} %pad_maximum_fusion.1), channel_id=1, source_target_pairs={{0,768},{256,0},{512,256},{768,512},{1,769},{257,1},{513,257},{769... | collective-permute-start | bytes 786440 | tf_op jit(solution)/shard_map/ppermute | solution.py:301
  66.8 12.5 %collective-permute-start.4 = (bf16[32,16,256]{2,1,0:T(8,128)(2,1)S(1)}, bf16[32,16,256]{2,1,0:T(8,128)(2,1)S(1)}, u32[]{:S(2)}, u32[]{:S(2)}) collective-permute-start(bf16[32,16,256]{2,1,0:T(8,128)(2,1)S(1)} %pad_maximum_fusion.1), channel_id=1, source_target_pairs={{0,512},{256,768},{512,0},{768,256},{1,513},{257,769},{513,1},{769... | collective-permute-start | bytes 786440 | tf_op jit(solution)/shard_map/ppermute | solution.py:301
  69.5 12.6 %collective-permute-start.3 = (bf16[32,16,256]{2,1,0:T(8,128)(2,1)S(1)}, bf16[32,16,256]{2,1,0:T(8,128)(2,1)S(1)}, u32[]{:S(2)}, u32[]{:S(2)}) collective-permute-start(bf16[32,16,256]{2,1,0:T(8,128)(2,1)S(1)} %pad_maximum_fusion.1), channel_id=1, source_target_pairs={{0,256},{256,512},{512,768},{768,0},{1,257},{257,513},{513,769},{7... | collective-permute-start | bytes 786440 | tf_op jit(solution)/shard_map/ppermute | solution.py:301
  82.2 163.5 %collective-permute-start.6 = (bf16[4,32,16,256]{3,2,1,0:T(8,128)(2,1)S(1)}, bf16[4,32,16,256]{3,2,1,0:T(8,128)(2,1)}, u32[]{:S(2)}, u32[]{:S(2)}) collective-permute-start(bf16[4,32,16,256]{3,2,1,0:T(8,128)(2,1)S(1)} %pad_maximum_fusion.own), channel_id=1, source_target_pairs={{0,32},{32,0},{1,33},{33,1},{2,34},{34,2},{3,35},{35,3},{4,36},{36... | collective-permute-start | bytes 3145736 | tf_op jit(solution)/shard_map/ppermute | solution.py:301
  85.6 160.1 %copy-start.1 = (s32[3]{0:T(128)S(1)}, s32[3]{0:T(128)}, u32[]{:S(2)}) copy-start(s32[3]{0:T(128)} %pad_add_fusion.place._) | copy-start | bytes 40
  85.6 160.1 %copy-start.2 = (f32[512]{0:T(512)S(1)}, f32[512]{0:T(512)}, u32[]{:S(2)}) copy-start(f32[512]{0:T(512)} %param.25) | copy-start | bytes 6148
  85.6 160.1 %copy-start.3 = (s32[32]{0:T(128)S(1)}, s32[32]{0:T(128)}, u32[]{:S(2)}) copy-start(s32[32]{0:T(128)} %table_of.1) | copy-start | bytes 388
  282.1 33.6 %all-to-all-start.4 = ((bf16[64,4,256]{2,1,0:T(4,128)(2,1)}), bf16[64,4,256]{2,1,0:T(4,128)(2,1)S(1)}, u32[]{:S(2)}, u32[]{:S(2)}) async-start(bf16[64,4,256]{2,1,0:T(4,128)(2,1)} %reshape.31), calls=%async_computation.4 | async-start | bytes 262144 | tf_op jit(solution)/shard_map/all_to_all | solution.py:293

commit v5 on v4

--- a/solution.py
+++ b/solution.py
@@ -199,7 +199,7 @@
     )(place, table_of, *small, packed)
 
 
-def pack_kernel(down, up, top1, top2, packed, arrived):
+def pack_kernel(down, up, top1, top2, packed_hbm, packed, arrived):
     moves = [(down, 0)]
     moves += [(up.at[:, pl.ds(k * E, E)], WIDE + k * E) for k in range(TABLES + 1)]
     moves += [(top1.at[:, pl.ds(h * E, E)], (2 + h) * WIDE) for h in range(2)]
@@ -212,6 +212,9 @@
         copy.start()
     for copy in copies:
         copy.wait()
+    result = pltpu.make_async_copy(packed, packed_hbm, arrived.at[len(moves)])
+    result.start()
+    result.wait()
 
 
 def pack(*weights):
@@ -221,7 +224,11 @@
         out_shape=jax.ShapeDtypeStruct((PACKED, E), BF),
         in_specs=[anywhere] * len(weights),
         out_specs=anywhere,
-        scratch_shapes=[pltpu.SemaphoreType.DMA((TABLES + 6,))],
+        scratch_shapes=[
+            pltpu.VMEM((PACKED, E), BF),
+            pltpu.SemaphoreType.DMA((TABLES + 7,)),
+        ],
+        compiler_params=pltpu.CompilerParams(vmem_limit_bytes=12 * 2**20),
         cost_estimate=pl.CostEstimate(flops=0, bytes_accessed=10 * 2**20, transcendentals=0),
     )(*weights)
 

time: 317 us -> 166 us (0.52)
  Pallas kernels: 178 us -> 19.7 us
  local copies, waits for them, and re-layouts: 3.26 us -> 9.14 us
  starting transfers between devices: 68.5 us -> 63.8 us
    pallas_call x1, Pallas kernels: 160 us -> 1.02 us  [pack(): pl.pallas_call(pack_kernel, out_shape=jax.ShapeDtypeStruct((PACKED, E), B...]
    unnamed x14 -> x22, local copies, waits for them, and re-layouts: 0.43 us -> 6.3 us
    all_to_all x3, starting transfers between devices: 42.9 us -> 38.1 us  [swap(): return lax.all_to_all(value, axes, split_axis=0, concat_axis=0, tiled=True)]
  transfers between devices with their start and end apart: 10 -> 10, of which waited for: 7 -> 8; matrix products, arithmetic and copies ran while one was open for 1% -> 2% of each run, Pallas kernels for 53% -> 4%
where the time goes in v5:
time: 166 us; the launch traced here: 165 us
  starting transfers between devices  63.8 us (38%)
  waiting for transfers between devices  41.1 us (25%)
  blocking collectives  25.8 us (16%)
  Pallas kernels  19.7 us (12%)
  local copies, waits for them, and re-layouts  9.14 us (6%)
  other arithmetic  3.34 us (2%)
    all_to_all x3, starting transfers between devices, swap(): return lax.all_to_all(value, axes, split_axis=0, concat_axis=0, tiled=True)  38.1 us
    all_to_all x3, waiting for transfers between devices, swap(): return lax.all_to_all(value, axes, split_axis=0, concat_axis=0, tiled=True)  26.3 us
    all_to_all x2, blocking collectives, swap(): return lax.all_to_all(value, axes, split_axis=0, concat_axis=0, tiled=True)  25.8 us
    ppermute x7, starting transfers between devices, turn(): lax.ppermute(value, axis, [(i, (i + shift) % size) for i in range(size)])  25.7 us
    ppermute x7, waiting for transfers between devices, turn(): lax.ppermute(value, axis, [(i, (i + shift) % size) for i in range(size)])  14.8 us
    pallas_call x1, Pallas kernels, run_step(): pl.pallas_call(step_kernel, out_shape=(jax.ShapeDtypeStruct((CORES, X, YL...  10.9 us
    unnamed x22, local copies, waits for them, and re-layouts  6.3 us
    pallas_call x1, Pallas kernels, turn_lanes(): pl.pallas_call(lanes_kernel, out_shape=jax.ShapeDtypeStruct(counts.shape,...  6.11 us
  transfers between devices with their start and end apart: 10, of which 8 were waited for; matrix products, arithmetic and copies ran while one was open for 2% of the time, Pallas kernels for 4%

profile of v5, /device:TPU:8, one launch (start us, length us, event | category | flops | bytes accessed | tf_op | source)
XLA Modules:
  0.0 165.1 jit_solution(3502153661311093401)
XLA Ops:
  0.7 0.8 dynamic-slice_bitcast_fusion
  3.1 20.4 %all-to-all-start = ((bf16[32,4,256]{2,1,0:T(4,128)(2,1)}), bf16[32,4,256]{2,1,0:T(4,128)(2,1)S(1)}, u32[]{:S(2)}, u32[]{:S(2)}) async-start(bf16[32,4,256]{2,1,0:T(4,128)(2,1)} %broadcast_in_dim.8), calls=%async_computation | async-start | bytes 131072 | tf_op jit(solution)/shard_map/all_to_all | solution.py:300
  24.1 6.1 %shard_map.140 = bf16[4096,128]{1,0:T(8,128)(2,1)} custom-call(s32[3]{0:T(128)} %pad_add_fusion.place._, s32[4096,128]{1,0:T(8,128)} %counts), custom_call_target="tpu_custom_call" | custom-call | flops 200000000 | bytes 3145728 | tf_op jit(solution)/shard_map/pallas_call | solution.py:248
  30.3 6.4 %all-to-all-done = bf16[32,4,256]{2,1,0:T(4,128)(2,1)S(1)} async-done(((bf16[32,4,256]{2,1,0:T(4,128)(2,1)}), bf16[32,4,256]{2,1,0:T(4,128)(2,1)S(1)}, u32[]{:S(2)}, u32[]{:S(2)}) %all-to-all-start) | async-done | bytes 65568 | tf_op jit(solution)/shard_map/all_to_all | solution.py:300
  36.7 6.9 %all-to-all-start.1 = ((bf16[32,128,128]{2,1,0:T(8,128)(2,1)}), bf16[32,128,128]{2,1,0:T(8,128)(2,1)}, u32[]{:S(2)}, u32[]{:S(2)}) async-start(bf16[32,128,128]{2,1,0:T(8,128)(2,1)} %bitcast.20), calls=%async_computation.1 | async-start | bytes 2097152 | tf_op jit(solution)/shard_map/all_to_all | solution.py:300
  43.6 5.3 %collective-permute-start.2 = (bf16[32,4,256]{2,1,0:T(4,128)(2,1)S(1)}, bf16[32,4,256]{2,1,0:T(4,128)(2,1)S(1)}, u32[]{:S(2)}, u32[]{:S(2)}) collective-permute-start(bf16[32,4,256]{2,1,0:T(4,128)(2,1)S(1)} %all-to-all-done), channel_id=1, source_target_pairs={{0,192},{64,0},{128,64},{192,128},{1,193},{65,1},{129,65},{193,129... | collective-permute-start | bytes 196616 | tf_op jit(solution)/shard_map/ppermute | solution.py:308
  48.8 4.7 %collective-permute-start.1 = (bf16[32,4,256]{2,1,0:T(4,128)(2,1)S(1)}, bf16[32,4,256]{2,1,0:T(4,128)(2,1)S(1)}, u32[]{:S(2)}, u32[]{:S(2)}) collective-permute-start(bf16[32,4,256]{2,1,0:T(4,128)(2,1)S(1)} %all-to-all-done), channel_id=1, source_target_pairs={{0,128},{64,192},{128,0},{192,64},{1,129},{65,193},{129,1},{193,65... | collective-permute-start | bytes 196616 | tf_op jit(solution)/shard_map/ppermute | solution.py:308
  53.6 3.6 %collective-permute-start = (bf16[32,4,256]{2,1,0:T(4,128)(2,1)S(1)}, bf16[32,4,256]{2,1,0:T(4,128)(2,1)S(1)}, u32[]{:S(2)}, u32[]{:S(2)}) collective-permute-start(bf16[32,4,256]{2,1,0:T(4,128)(2,1)S(1)} %all-to-all-done), channel_id=1, source_target_pairs={{0,64},{64,128},{128,192},{192,0},{1,65},{65,129},{129,193},{193,1... | collective-permute-start | bytes 196616 | tf_op jit(solution)/shard_map/ppermute | solution.py:308
  57.2 3.0 %collective-permute-done.1 = bf16[32,4,256]{2,1,0:T(4,128)(2,1)S(1)} collective-permute-done((bf16[32,4,256]{2,1,0:T(4,128)(2,1)S(1)}, bf16[32,4,256]{2,1,0:T(4,128)(2,1)S(1)}, u32[]{:S(2)}, u32[]{:S(2)}) %collective-permute-start.1) | collective-permute-done | bytes 65568 | tf_op jit(solution)/shard_map/ppermute | solution.py:308
  60.2 1.8 %collective-permute-done = bf16[32,4,256]{2,1,0:T(4,128)(2,1)S(1)} collective-permute-done((bf16[32,4,256]{2,1,0:T(4,128)(2,1)S(1)}, bf16[32,4,256]{2,1,0:T(4,128)(2,1)S(1)}, u32[]{:S(2)}, u32[]{:S(2)}) %collective-permute-start) | collective-permute-done | bytes 65568 | tf_op jit(solution)/shard_map/ppermute | solution.py:308
  62.2 4.7 %collective-permute-start.5 = (bf16[32,16,256]{2,1,0:T(8,128)(2,1)S(1)}, bf16[32,16,256]{2,1,0:T(8,128)(2,1)S(1)}, u32[]{:S(2)}, u32[]{:S(2)}) collective-permute-start(bf16[32,16,256]{2,1,0:T(8,128)(2,1)S(1)} %pad_maximum_fusion.1), channel_id=1, source_target_pairs={{0,768},{256,0},{512,256},{768,512},{1,769},{257,1},{513,257},{769... | collective-permute-start | bytes 786440 | tf_op jit(solution)/shard_map/ppermute | solution.py:308
  66.8 2.7 %collective-permute-start.4 = (bf16[32,16,256]{2,1,0:T(8,128)(2,1)S(1)}, bf16[32,16,256]{2,1,0:T(8,128)(2,1)S(1)}, u32[]{:S(2)}, u32[]{:S(2)}) collective-permute-start(bf16[32,16,256]{2,1,0:T(8,128)(2,1)S(1)} %pad_maximum_fusion.1), channel_id=1, source_target_pairs={{0,512},{256,768},{512,0},{768,256},{1,513},{257,769},{513,1},{769... | collective-permute-start | bytes 786440 | tf_op jit(solution)/shard_map/ppermute | solution.py:308
  69.5 2.8 %collective-permute-start.3 = (bf16[32,16,256]{2,1,0:T(8,128)(2,1)S(1)}, bf16[32,16,256]{2,1,0:T(8,128)(2,1)S(1)}, u32[]{:S(2)}, u32[]{:S(2)}) collective-permute-start(bf16[32,16,256]{2,1,0:T(8,128)(2,1)S(1)} %pad_maximum_fusion.1), channel_id=1, source_target_pairs={{0,256},{256,512},{512,768},{768,0},{1,257},{257,513},{513,769},{7... | collective-permute-start | bytes 786440 | tf_op jit(solution)/shard_map/ppermute | solution.py:308
  72.4 4.4 %collective-permute-done.5 = bf16[32,16,256]{2,1,0:T(8,128)(2,1)S(1)} collective-permute-done((bf16[32,16,256]{2,1,0:T(8,128)(2,1)S(1)}, bf16[32,16,256]{2,1,0:T(8,128)(2,1)S(1)}, u32[]{:S(2)}, u32[]{:S(2)}) %collective-permute-start.5) | collective-permute-done | bytes 262176 | tf_op jit(solution)/shard_map/ppermute | solution.py:308
  76.8 2.7 %collective-permute-done.4 = bf16[32,16,256]{2,1,0:T(8,128)(2,1)S(1)} collective-permute-done((bf16[32,16,256]{2,1,0:T(8,128)(2,1)S(1)}, bf16[32,16,256]{2,1,0:T(8,128)(2,1)S(1)}, u32[]{:S(2)}, u32[]{:S(2)}) %collective-permute-start.4) | collective-permute-done | bytes 262176 | tf_op jit(solution)/shard_map/ppermute | solution.py:308
  79.5 2.9 %collective-permute-done.3 = bf16[32,16,256]{2,1,0:T(8,128)(2,1)S(1)} collective-permute-done((bf16[32,16,256]{2,1,0:T(8,128)(2,1)S(1)}, bf16[32,16,256]{2,1,0:T(8,128)(2,1)S(1)}, u32[]{:S(2)}, u32[]{:S(2)}) %collective-permute-start.3) | collective-permute-done | bytes 262176 | tf_op jit(solution)/shard_map/ppermute | solution.py:308
  82.4 1.2 pad_maximum_fusion.own
  83.6 1.9 %collective-permute-start.6 = (bf16[4,32,16,256]{3,2,1,0:T(8,128)(2,1)}, bf16[4,32,16,256]{3,2,1,0:T(8,128)(2,1)}, u32[]{:S(2)}, u32[]{:S(2)}) collective-permute-start(bf16[4,32,16,256]{3,2,1,0:T(8,128)(2,1)} %pad_maximum_fusion.own), channel_id=1, source_target_pairs={{0,32},{32,0},{1,33},{33,1},{2,34},{34,2},{3,35},{35,3},{4,36},{36... | collective-permute-start | bytes 3145736 | tf_op jit(solution)/shard_map/ppermute | solution.py:308
  85.6 1.3 fusion.3.bottom
  87.0 1.3 copy-done.3
  88.2 1.3 copy-done.4
  89.5 1.0 copy-done.5
  90.5 1.0 shard_map.141.packed_hbm
  91.6 2.3 %copy-done.1 = bf16[10240,256]{1,0:T(8,128)(2,1)} copy-done((bf16[10240,256]{1,0:T(8,128)(2,1)}, bf16[10240,256]{1,0:T(8,128)(2,1)S(1)}, u32[]{:S(2)}) %copy-start.1) | copy-done | bytes 5242904
  93.9 2.6 %all-to-all-done.1.counts = bf16[32,128,128]{2,1,0:T(8,128)(2,1)} async-done(((bf16[32,128,128]{2,1,0:T(8,128)(2,1)}), bf16[32,128,128]{2,1,0:T(8,128)(2,1)}, u32[]{:S(2)}, u32[]{:S(2)}) %all-to-all-start.1) | async-done | bytes 1048608 | tf_op jit(solution)/shard_map/all_to_all | solution.py:300
  96.4 10.9 %shard_map.142 = (bf16[2,4,2,16,16,256]{5,4,3,2,1,0:T(8,128)(2,1)S(1)}, f32[128,1]{1,0:T(8,128)S(1)}) custom-call(s32[3]{0:T(128)S(1)} %copy-done.6, s32[32]{0:T(128)S(1)} %copy-done.8, bf16[128,256]{1,0:T(8,128)(2,1)S(1)} %fusion.3.bottom, s32[128,1]{1,0:T(8,128)S(1)} %copy.16.labels, f32[1,512]{1,0:T(1,128)S(1)} %bitcast.19, ...), custom_call_target="tpu_custom_call" | custom-call | flops 4000000000 | bytes 12582912 | tf_op jit(solution)/shard_map/pallas_call | solution.py:178
  107.4 5.4 %all_to_all.25.halves = bf16[2,2048,256]{2,1,0:T(8,128)(2,1)S(1)} all-to-all(bf16[2,2048,256]{2,1,0:T(8,128)(2,1)S(1)} %bitcast.18), channel_id=1, replica_groups=mesh['x'=4,'yh'=4,'c'=2,'z'=16,'yl'=2] {'c'}, dimensions={0} | all-to-all | bytes 4194304 | tf_op jit(solution)/shard_map/all_to_all | solution.py:300
  112.8 0.8 shard_map.143
  113.6 20.4 %all_to_all.26.parts = bf16[8,256,256]{2,1,0:T(8,128)(2,1)S(1)} all-to-all(bf16[8,256,256]{2,1,0:T(8,128)(2,1)S(1)} %bitcast.17), channel_id=1, replica_groups=mesh['x'=4,'yh'=4,'c'=2,'z'=16,'yl'=2] {'x','yl'}, dimensions={0} | all-to-all | bytes 2097152 | tf_op jit(solution)/shard_map/all_to_all | solution.py:300
  134.0 0.9 shard_map.144
  135.6 10.9 %all-to-all-start.4 = ((bf16[64,4,256]{2,1,0:T(4,128)(2,1)}), bf16[64,4,256]{2,1,0:T(4,128)(2,1)S(1)}, u32[]{:S(2)}, u32[]{:S(2)}) async-start(bf16[64,4,256]{2,1,0:T(4,128)(2,1)} %reshape.31), calls=%async_computation.4 | async-start | bytes 262144 | tf_op jit(solution)/shard_map/all_to_all | solution.py:300
  147.1 17.3 %all-to-all-done.4 = bf16[64,4,256]{2,1,0:T(4,128)(2,1)S(1)} async-done(((bf16[64,4,256]{2,1,0:T(4,128)(2,1)}), bf16[64,4,256]{2,1,0:T(4,128)(2,1)S(1)}, u32[]{:S(2)}, u32[]{:S(2)}) %all-to-all-start.4) | async-done | bytes 131104 | tf_op jit(solution)/shard_map/all_to_all | solution.py:300
  (29 shorter events, 4.6 us)
Async XLA Ops:
  0.6 1.2 copy-start
  3.1 33.6 %all-to-all-start = ((bf16[32,4,256]{2,1,0:T(4,128)(2,1)}), bf16[32,4,256]{2,1,0:T(4,128)(2,1)S(1)}, u32[]{:S(2)}, u32[]{:S(2)}) async-start(bf16[32,4,256]{2,1,0:T(4,128)(2,1)} %broadcast_in_dim.8), calls=%async_computation | async-start | bytes 131072 | tf_op jit(solution)/shard_map/all_to_all | solution.py:300
  36.7 48.8 %copy-start.10 = (s32[128]{0:T(128)S(1)}, s32[128]{0:T(128)}, u32[]{:S(2)}) copy-start(s32[128]{0:T(128)} %param.18) | copy-start | bytes 1540
  36.7 48.9 %copy-start.9 = (bf16[13,128]{1,0:T(8,128)(2,1)S(1)}, bf16[13,128]{1,0:T(8,128)(2,1)}, u32[]{:S(2)}) copy-start(bf16[13,128]{1,0:T(8,128)(2,1)} %param.17) | copy-start | bytes 9988
  36.7 50.3 %copy-start.2 = (bf16[2304,512]{1,0:T(8,128)(2,1)S(1)}, bf16[2304,512]{1,0:T(8,128)(2,1)}, u32[]{:S(2)}) copy-start(bf16[2304,512]{1,0:T(8,128)(2,1)} %top1) | copy-start | bytes 7077892
  36.7 59.7 %all-to-all-start.1 = ((bf16[32,128,128]{2,1,0:T(8,128)(2,1)}), bf16[32,128,128]{2,1,0:T(8,128)(2,1)}, u32[]{:S(2)}, u32[]{:S(2)}) async-start(bf16[32,128,128]{2,1,0:T(8,128)(2,1)} %bitcast.20), calls=%async_computation.1 | async-start | bytes 2097152 | tf_op jit(solution)/shard_map/all_to_all | solution.py:300
  43.6 13.6 %collective-permute-start.2 = (bf16[32,4,256]{2,1,0:T(4,128)(2,1)S(1)}, bf16[32,4,256]{2,1,0:T(4,128)(2,1)S(1)}, u32[]{:S(2)}, u32[]{:S(2)}) collective-permute-start(bf16[32,4,256]{2,1,0:T(4,128)(2,1)S(1)} %all-to-all-done), channel_id=1, source_target_pairs={{0,192},{64,0},{128,64},{192,128},{1,193},{65,1},{129,65},{193,129... | collective-permute-start | bytes 196616 | tf_op jit(solution)/shard_map/ppermute | solution.py:308
  48.8 11.4 %collective-permute-start.1 = (bf16[32,4,256]{2,1,0:T(4,128)(2,1)S(1)}, bf16[32,4,256]{2,1,0:T(4,128)(2,1)S(1)}, u32[]{:S(2)}, u32[]{:S(2)}) collective-permute-start(bf16[32,4,256]{2,1,0:T(4,128)(2,1)S(1)} %all-to-all-done), channel_id=1, source_target_pairs={{0,128},{64,192},{128,0},{192,64},{1,129},{65,193},{129,1},{193,65... | collective-permute-start | bytes 196616 | tf_op jit(solution)/shard_map/ppermute | solution.py:308
  53.6 8.4 %collective-permute-start = (bf16[32,4,256]{2,1,0:T(4,128)(2,1)S(1)}, bf16[32,4,256]{2,1,0:T(4,128)(2,1)S(1)}, u32[]{:S(2)}, u32[]{:S(2)}) collective-permute-start(bf16[32,4,256]{2,1,0:T(4,128)(2,1)S(1)} %all-to-all-done), channel_id=1, source_target_pairs={{0,64},{64,128},{128,192},{192,0},{1,65},{65,129},{129,193},{193,1... | collective-permute-start | bytes 196616 | tf_op jit(solution)/shard_map/ppermute | solution.py:308
  62.2 14.6 %collective-permute-start.5 = (bf16[32,16,256]{2,1,0:T(8,128)(2,1)S(1)}, bf16[32,16,256]{2,1,0:T(8,128)(2,1)S(1)}, u32[]{:S(2)}, u32[]{:S(2)}) collective-permute-start(bf16[32,16,256]{2,1,0:T(8,128)(2,1)S(1)} %pad_maximum_fusion.1), channel_id=1, source_target_pairs={{0,768},{256,0},{512,256},{768,512},{1,769},{257,1},{513,257},{769... | collective-permute-start | bytes 786440 | tf_op jit(solution)/shard_map/ppermute | solution.py:308
  66.8 12.6 %collective-permute-start.4 = (bf16[32,16,256]{2,1,0:T(8,128)(2,1)S(1)}, bf16[32,16,256]{2,1,0:T(8,128)(2,1)S(1)}, u32[]{:S(2)}, u32[]{:S(2)}) collective-permute-start(bf16[32,16,256]{2,1,0:T(8,128)(2,1)S(1)} %pad_maximum_fusion.1), channel_id=1, source_target_pairs={{0,512},{256,768},{512,0},{768,256},{1,513},{257,769},{513,1},{769... | collective-permute-start | bytes 786440 | tf_op jit(solution)/shard_map/ppermute | solution.py:308
  69.5 12.9 %collective-permute-start.3 = (bf16[32,16,256]{2,1,0:T(8,128)(2,1)S(1)}, bf16[32,16,256]{2,1,0:T(8,128)(2,1)S(1)}, u32[]{:S(2)}, u32[]{:S(2)}) collective-permute-start(bf16[32,16,256]{2,1,0:T(8,128)(2,1)S(1)} %pad_maximum_fusion.1), channel_id=1, source_target_pairs={{0,256},{256,512},{512,768},{768,0},{1,257},{257,513},{513,769},{7... | collective-permute-start | bytes 786440 | tf_op jit(solution)/shard_map/ppermute | solution.py:308
  83.6 10.3 %collective-permute-start.6 = (bf16[4,32,16,256]{3,2,1,0:T(8,128)(2,1)}, bf16[4,32,16,256]{3,2,1,0:T(8,128)(2,1)}, u32[]{:S(2)}, u32[]{:S(2)}) collective-permute-start(bf16[4,32,16,256]{3,2,1,0:T(8,128)(2,1)} %pad_maximum_fusion.own), channel_id=1, source_target_pairs={{0,32},{32,0},{1,33},{33,1},{2,34},{34,2},{3,35},{35,3},{4,36},{36... | collective-permute-start | bytes 3145736 | tf_op jit(solution)/shard_map/ppermute | solution.py:308
  86.9 1.3 copy-start.3
  88.2 1.3 copy-start.4
  89.5 1.0 copy-start.5
  90.5 5.9 %copy-start.6 = (s32[3]{0:T(128)S(1)}, s32[3]{0:T(128)}, u32[]{:S(2)}) copy-start(s32[3]{0:T(128)} %pad_add_fusion.place._) | copy-start | bytes 40
  90.5 5.9 %copy-start.7 = (f32[512]{0:T(512)S(1)}, f32[512]{0:T(512)}, u32[]{:S(2)}) copy-start(f32[512]{0:T(512)} %param.25) | copy-start | bytes 6148
  90.5 5.9 %copy-start.8 = (s32[32]{0:T(128)S(1)}, s32[32]{0:T(128)}, u32[]{:S(2)}) copy-start(s32[32]{0:T(128)} %table_of.1) | copy-start | bytes 388
  91.6 2.3 %copy-start.1 = (bf16[10240,256]{1,0:T(8,128)(2,1)}, bf16[10240,256]{1,0:T(8,128)(2,1)S(1)}, u32[]{:S(2)}) copy-start(bf16[10240,256]{1,0:T(8,128)(2,1)S(1)} %shard_map.141.packed_hbm) | copy-start | bytes 15728644
  135.6 28.9 %all-to-all-start.4 = ((bf16[64,4,256]{2,1,0:T(4,128)(2,1)}), bf16[64,4,256]{2,1,0:T(4,128)(2,1)S(1)}, u32[]{:S(2)}, u32[]{:S(2)}) async-start(bf16[64,4,256]{2,1,0:T(4,128)(2,1)} %reshape.31), calls=%async_computation.4 | async-start | bytes 262144 | tf_op jit(solution)/shard_map/all_to_all | solution.py:300

commit v6 on v5

--- a/solution.py
+++ b/solution.py
@@ -143,7 +143,10 @@
     sig_two = jax.nn.sigmoid(pre_two)
     head = w_out[...]
     logits = jnp.sum(pre_two * sig_two * head, axis=1, keepdims=True)
-    logits_out[...] = logits
+    across = lax.broadcasted_iota(jnp.int32, (N, N), 0) == lax.broadcasted_iota(
+        jnp.int32, (N, N), 1
+    )
+    logits_out[...] = jnp.sum(jnp.where(across, logits, 0.0), axis=0, keepdims=True)
     logit_grad = (jax.nn.sigmoid(logits) - labels[...].astype(F32)) * (1.0 / 32.0)
     grad_two = (logit_grad * head * silu_slope(pre_two, sig_two)).astype(BF)
     grad_act = dot_nt(grad_two[:, cols(0)], top2(0)) + dot_nt(grad_two[:, cols(1)], top2(1))
@@ -179,7 +182,7 @@
         step_kernel,
         out_shape=(
             jax.ShapeDtypeStruct((CORES, X, YL, Z, 16, E), BF),
-            jax.ShapeDtypeStruct((N, 1), F32),
+            jax.ShapeDtypeStruct((1, N), F32),
         ),
         in_specs=[smem, smem] + [vmem] * len(small) + [hbm],
         out_specs=(vmem, vmem),
@@ -228,7 +231,7 @@
             pltpu.VMEM((PACKED, E), BF),
             pltpu.SemaphoreType.DMA((TABLES + 7,)),
         ],
-        compiler_params=pltpu.CompilerParams(vmem_limit_bytes=12 * 2**20),
+        compiler_params=pltpu.CompilerParams(vmem_limit_bytes=60 * 2**20),
         cost_estimate=pl.CostEstimate(flops=0, bytes_accessed=10 * 2**20, transcendentals=0),
     )(*weights)
 
@@ -237,7 +240,7 @@
     my_yh = place[1]
     at = lax.broadcasted_iota(jnp.int32, (LOOK, LOOK), 0)
     to = lax.broadcasted_iota(jnp.int32, (LOOK, LOOK), 1)
-    yh = (my_yh + YH - to // 4 % YH) % YH
+    yh = (to // 4 % 2) * 2 + (my_yh + to // 8) % 2
     source = (to // 16 % X) * 32 + yh * 8 + (to // 64) * 4 + to % 4
     turned = (at == source).astype(BF)
     out[...] = dot(counts[...].astype(F32).astype(BF), turned).astype(BF)
@@ -272,8 +275,10 @@
 def sum_kernel(place, parts, out):
     to = lax.broadcasted_iota(jnp.int32, (E, E), 0)
     at = lax.broadcasted_iota(jnp.int32, (E, E), 1)
-    back = (place[1] + YH - to // 64) % YH
-    turned = (at == (to // 4 % Z) * 16 + back * 4 + to % 4).astype(BF)
+    yh = to // 64
+    turned = (
+        at == (to // 4 % Z) * 16 + ((place[1] + yh) % 2) * 8 + (yh // 2) * 4 + to % 4
+    ).astype(BF)
     total = parts[0].astype(F32)
     for i in range(1, parts.shape[0]):
         total = total + parts[i].astype(F32)
@@ -325,20 +330,20 @@
 ):
     my_x, my_yh, my_c = lax.axis_index("x"), lax.axis_index("yh"), lax.axis_index("c")
     place = jnp.stack([my_x, my_yh, my_c]).astype(jnp.int32)
-    first = ((my_x * YH + my_yh) * CORES + my_c) * 4
-    ids = lax.dynamic_slice(row_ids, (0, first), (1, 4))[0]
+    first = my_x * 32 + jnp.bitwise_and(my_yh, 1) * 8 + my_c * 4
+    span = lax.dynamic_slice(row_ids, (0, first), (1, 20))[0]
+    ids = jnp.concatenate([span[:4], span[16:]])
     mine = jnp.take(table, ids, axis=0, mode="clip").astype(BF)
-    mine = jnp.broadcast_to(mine, (SHARDS, 4, E))
+    mine = jnp.broadcast_to(mine, (SHARDS, 8, E))
     mine, pool_counts = lax.optimization_barrier((mine, pool_counts))
     looked = swap(mine, MP)
     counts = turn_lanes(place, pool_counts).reshape(SHARDS, N, LOOK)
-    looked, counts = lax.optimization_barrier((looked, counts))
+    counts, *weights = lax.optimization_barrier((counts, cross_down, cross_up, w_top1, w_top2))
+    packed = pack(*weights)
+    looked, counts, packed = lax.optimization_barrier((looked, counts, packed))
     counts = swap(counts, MP)
-    looked = jnp.concatenate(
-        [looked] + [turn(looked, "yh", YH, k) for k in range(1, YH)], axis=1
-    )
-    looked, *weights = lax.optimization_barrier((looked, cross_down, cross_up, w_top1, w_top2))
-    packed = pack(*weights)
+    exchanged = lax.ppermute(looked, "yh", [(i, i ^ 1) for i in range(YH)])
+    looked = jnp.concatenate([looked, exchanged], axis=1)
     looked = jnp.stack([looked] + [turn(looked, "x", X, k) for k in range(1, X)])
     others = turn(looked, "c", CORES, 1)
 

time: 166 us -> 168 us (1.012)
  blocking collectives: 25.8 us -> 52.7 us
  starting transfers between devices: 63.8 us -> 46 us
  local copies, waits for them, and re-layouts: 9.14 us -> 2.57 us
  Pallas kernels: 19.7 us -> 23.4 us
  waiting for transfers between devices: 41.1 us -> 39.1 us
  other arithmetic: 3.34 us -> 1.56 us
    all_to_all x2 -> x3, blocking collectives: 25.8 us -> 52.7 us  [swap(): return lax.all_to_all(value, axes, split_axis=0, concat_axis=0, tiled=True)]
    ppermute x7 -> x4, starting transfers between devices: 25.7 us -> 12.1 us  [turn(): lax.ppermute(value, axis, [(i, (i + shift) % size) for i in range(size)])]
    all_to_all x3 -> x2, starting transfers between devices: 38.1 us -> 29.4 us  [swap(): return lax.all_to_all(value, axes, split_axis=0, concat_axis=0, tiled=True)]
    unnamed x22 -> x15, local copies, waits for them, and re-layouts: 6.3 us -> 0.3 us
    ppermute x0 -> x1, waiting for transfers between devices: none -> 4.61 us  [shards(): exchanged = lax.ppermute(looked, 'yh', [(i, i ^ 1) for i in range(YH)])]
    ppermute x0 -> x1, starting transfers between devices: none -> 4.5 us  [shards(): exchanged = lax.ppermute(looked, 'yh', [(i, i ^ 1) for i in range(YH)])]
    all_to_all x3 -> x2, waiting for transfers between devices: 26.3 us -> 22.4 us  [swap(): return lax.all_to_all(value, axes, split_axis=0, concat_axis=0, tiled=True)]
    pallas_call x1, Pallas kernels: 1.02 us -> 4.9 us  [pack(): pl.pallas_call(pack_kernel, out_shape=jax.ShapeDtypeStruct((PACKED, E), B...]
  transfers between devices with their start and end apart: 10 -> 7, of which waited for: 8 -> 7; matrix products, arithmetic and copies ran while one was open for 2% -> 1% of each run, Pallas kernels for 4% -> 7%
where the time goes in v6:
time: 168 us; the launch traced here: 167 us
  blocking collectives  52.7 us (31%)
  starting transfers between devices  46 us (27%)
  waiting for transfers between devices  39.1 us (23%)
  Pallas kernels  23.4 us (14%)
  local copies, waits for them, and re-layouts  2.57 us (2%)
    all_to_all x3, blocking collectives, swap(): return lax.all_to_all(value, axes, split_axis=0, concat_axis=0, tiled=True)  52.7 us
    all_to_all x2, starting transfers between devices, swap(): return lax.all_to_all(value, axes, split_axis=0, concat_axis=0, tiled=True)  29.4 us
    all_to_all x2, waiting for transfers between devices, swap(): return lax.all_to_all(value, axes, split_axis=0, concat_axis=0, tiled=True)  22.4 us
    ppermute x4, starting transfers between devices, turn(): lax.ppermute(value, axis, [(i, (i + shift) % size) for i in range(size)])  12.1 us
    ppermute x4, waiting for transfers between devices, turn(): lax.ppermute(value, axis, [(i, (i + shift) % size) for i in range(size)])  12.1 us
    pallas_call x1, Pallas kernels, run_step(): pl.pallas_call(step_kernel, out_shape=(jax.ShapeDtypeStruct((CORES, X, YL...  10.8 us
    pallas_call x1, Pallas kernels, turn_lanes(): pl.pallas_call(lanes_kernel, out_shape=jax.ShapeDtypeStruct(counts.shape,...  6.1 us
    pallas_call x1, Pallas kernels, pack(): pl.pallas_call(pack_kernel, out_shape=jax.ShapeDtypeStruct((PACKED, E), B...  4.9 us
  transfers between devices with their start and end apart: 7, of which 7 were waited for; matrix products, arithmetic and copies ran while one was open for 1% of the time, Pallas kernels for 7%

profile of v6, /device:TPU:8, one launch (start us, length us, event | category | flops | bytes accessed | tf_op | source)
XLA Modules:
  0.0 167.2 jit_solution(8327397775480853936)
XLA Ops:
  0.7 0.8 constant_dynamic-slice_fusion
  1.5 0.1 pad_add_fusion.1
  1.6 0.2 copy-done
  1.9 0.6 gather_fusion
  2.4 0.7 broadcast_in_dim.8
  3.1 20.4 %all-to-all-start = ((bf16[32,8,256]{2,1,0:T(8,128)(2,1)}), bf16[32,8,256]{2,1,0:T(8,128)(2,1)S(1)}, u32[]{:S(2)}, u32[]{:S(2)}) async-start(bf16[32,8,256]{2,1,0:T(8,128)(2,1)} %broadcast_in_dim.8), calls=%async_computation | async-start | bytes 262144 | tf_op jit(solution)/shard_map/all_to_all | solution.py:305
  23.5 0.7 pad_add_fusion.place._
  24.1 6.1 %shard_map.140 = bf16[4096,128]{1,0:T(8,128)(2,1)} custom-call(s32[3]{0:T(128)} %pad_add_fusion.place._, s32[4096,128]{1,0:T(8,128)} %counts), custom_call_target="tpu_custom_call" | custom-call | flops 200000000 | bytes 3145728 | tf_op jit(solution)/shard_map/pallas_call | solution.py:251
  30.2 4.9 %shard_map.141.packed_hbm = bf16[10240,256]{1,0:T(8,128)(2,1)} custom-call(bf16[2304,256]{1,0:T(8,128)(2,1)} %down, bf16[256,2304]{1,0:T(8,128)(2,1)} %up, bf16[2304,512]{1,0:T(8,128)(2,1)} %top1, bf16[512,512]{1,0:T(8,128)(2,1)} %top2), custom_call_target="tpu_custom_call" | custom-call | bytes 10485760 | tf_op jit(solution)/shard_map/pallas_call | solution.py:225
  35.2 4.2 %all-to-all-done = bf16[32,8,256]{2,1,0:T(8,128)(2,1)S(1)} async-done(((bf16[32,8,256]{2,1,0:T(8,128)(2,1)}), bf16[32,8,256]{2,1,0:T(8,128)(2,1)S(1)}, u32[]{:S(2)}, u32[]{:S(2)}) %all-to-all-start) | async-done | bytes 131104 | tf_op jit(solution)/shard_map/all_to_all | solution.py:305
  39.5 9.0 %all-to-all-start.1 = ((bf16[32,128,128]{2,1,0:T(8,128)(2,1)}), bf16[32,128,128]{2,1,0:T(8,128)(2,1)S(1)}, u32[]{:S(2)}, u32[]{:S(2)}) async-start(bf16[32,128,128]{2,1,0:T(8,128)(2,1)} %bitcast.7), calls=%async_computation.1 | async-start | bytes 2097152 | tf_op jit(solution)/shard_map/all_to_all | solution.py:305
  48.5 4.5 %collective-permute-start = (bf16[32,8,256]{2,1,0:T(8,128)(2,1)S(1)}, bf16[32,8,256]{2,1,0:T(8,128)(2,1)S(1)}, u32[]{:S(2)}, u32[]{:S(2)}) collective-permute-start(bf16[32,8,256]{2,1,0:T(8,128)(2,1)S(1)} %all-to-all-done), channel_id=1, source_target_pairs={{0,64},{64,0},{128,192},{192,128},{1,65},{65,1},{129,193},{193,129... | collective-permute-start | bytes 393224 | tf_op jit(solution)/shard_map/ppermute | solution.py:345
  53.0 4.6 %collective-permute-done = bf16[32,8,256]{2,1,0:T(8,128)(2,1)S(1)} collective-permute-done((bf16[32,8,256]{2,1,0:T(8,128)(2,1)S(1)}, bf16[32,8,256]{2,1,0:T(8,128)(2,1)S(1)}, u32[]{:S(2)}, u32[]{:S(2)}) %collective-permute-start) | collective-permute-done | bytes 131104 | tf_op jit(solution)/shard_map/ppermute | solution.py:345
  57.6 4.7 %collective-permute-start.3 = (bf16[32,16,256]{2,1,0:T(8,128)(2,1)S(1)}, bf16[32,16,256]{2,1,0:T(8,128)(2,1)S(1)}, u32[]{:S(2)}, u32[]{:S(2)}) collective-permute-start(bf16[32,16,256]{2,1,0:T(8,128)(2,1)S(1)} %constant_dynamic-update-slice_fusion), channel_id=1, source_target_pairs={{0,768},{256,0},{512,256},{768,512},{1,769},{257,1},{513,257},{769... | collective-permute-start | bytes 786440 | tf_op jit(solution)/shard_map/ppermute | solution.py:313
  62.3 2.7 %collective-permute-start.2 = (bf16[32,16,256]{2,1,0:T(8,128)(2,1)S(1)}, bf16[32,16,256]{2,1,0:T(8,128)(2,1)S(1)}, u32[]{:S(2)}, u32[]{:S(2)}) collective-permute-start(bf16[32,16,256]{2,1,0:T(8,128)(2,1)S(1)} %constant_dynamic-update-slice_fusion), channel_id=1, source_target_pairs={{0,512},{256,768},{512,0},{768,256},{1,513},{257,769},{513,1},{769... | collective-permute-start | bytes 786440 | tf_op jit(solution)/shard_map/ppermute | solution.py:313
  65.0 2.8 %collective-permute-start.1 = (bf16[32,16,256]{2,1,0:T(8,128)(2,1)S(1)}, bf16[32,16,256]{2,1,0:T(8,128)(2,1)S(1)}, u32[]{:S(2)}, u32[]{:S(2)}) collective-permute-start(bf16[32,16,256]{2,1,0:T(8,128)(2,1)S(1)} %constant_dynamic-update-slice_fusion), channel_id=1, source_target_pairs={{0,256},{256,512},{512,768},{768,0},{1,257},{257,513},{513,769},{7... | collective-permute-start | bytes 786440 | tf_op jit(solution)/shard_map/ppermute | solution.py:313
  67.8 4.9 %collective-permute-done.3 = bf16[32,16,256]{2,1,0:T(8,128)(2,1)S(1)} collective-permute-done((bf16[32,16,256]{2,1,0:T(8,128)(2,1)S(1)}, bf16[32,16,256]{2,1,0:T(8,128)(2,1)S(1)}, u32[]{:S(2)}, u32[]{:S(2)}) %collective-permute-start.3) | collective-permute-done | bytes 262176 | tf_op jit(solution)/shard_map/ppermute | solution.py:313
  72.7 2.2 %collective-permute-done.2 = bf16[32,16,256]{2,1,0:T(8,128)(2,1)S(1)} collective-permute-done((bf16[32,16,256]{2,1,0:T(8,128)(2,1)S(1)}, bf16[32,16,256]{2,1,0:T(8,128)(2,1)S(1)}, u32[]{:S(2)}, u32[]{:S(2)}) %collective-permute-start.2) | collective-permute-done | bytes 262176 | tf_op jit(solution)/shard_map/ppermute | solution.py:313
  74.9 3.4 %collective-permute-done.1 = bf16[32,16,256]{2,1,0:T(8,128)(2,1)S(1)} collective-permute-done((bf16[32,16,256]{2,1,0:T(8,128)(2,1)S(1)}, bf16[32,16,256]{2,1,0:T(8,128)(2,1)S(1)}, u32[]{:S(2)}, u32[]{:S(2)}) %collective-permute-start.1) | collective-permute-done | bytes 262176 | tf_op jit(solution)/shard_map/ppermute | solution.py:313
  78.3 0.1 pad_maximum_fusion.own
  78.4 1.9 %collective-permute-start.4 = (bf16[4,32,16,256]{3,2,1,0:T(8,128)(2,1)S(1)}, bf16[4,32,16,256]{3,2,1,0:T(8,128)(2,1)}, u32[]{:S(2)}, u32[]{:S(2)}) collective-permute-start(bf16[4,32,16,256]{3,2,1,0:T(8,128)(2,1)S(1)} %pad_maximum_fusion.own), channel_id=1, source_target_pairs={{0,32},{32,0},{1,33},{33,1},{2,34},{34,2},{3,35},{35,3},{4,36},{36... | collective-permute-start | bytes 3145736 | tf_op jit(solution)/shard_map/ppermute | solution.py:313
  80.4 0.1 copy.15.labels
  80.5 1.1 fusion.3.bottom
  81.6 1.6 collective-permute-done.4.other
  83.1 18.1 %all-to-all-done.1.counts = bf16[32,128,128]{2,1,0:T(8,128)(2,1)S(1)} async-done(((bf16[32,128,128]{2,1,0:T(8,128)(2,1)}), bf16[32,128,128]{2,1,0:T(8,128)(2,1)S(1)}, u32[]{:S(2)}, u32[]{:S(2)}) %all-to-all-start.1) | async-done | bytes 1048608 | tf_op jit(solution)/shard_map/all_to_all | solution.py:305
  101.3 10.8 %shard_map.142 = (bf16[2,4,2,16,16,256]{5,4,3,2,1,0:T(8,128)(2,1)S(1)}, f32[1,128]{1,0:T(1,128)}) custom-call(s32[3]{0:T(128)S(1)} %copy-done.1, s32[32]{0:T(128)S(1)} %copy-done.3, bf16[128,256]{1,0:T(8,128)(2,1)S(1)} %fusion.3.bottom, s32[128,1]{1,0:T(8,128)S(1)} %copy.15.labels, f32[1,512]{1,0:T(1,128)S(1)} %bitcast.22, ...), custom_call_target="tpu_custom_call" | custom-call | flops 4000000000 | bytes 12582912 | tf_op jit(solution)/shard_map/pallas_call | solution.py:181
  112.0 5.4 %all_to_all.25.halves = bf16[2,2048,256]{2,1,0:T(8,128)(2,1)S(1)} all-to-all(bf16[2,2048,256]{2,1,0:T(8,128)(2,1)S(1)} %bitcast.21), channel_id=1, replica_groups=mesh['x'=4,'yh'=4,'c'=2,'z'=16,'yl'=2] {'c'}, dimensions={0} | all-to-all | bytes 4194304 | tf_op jit(solution)/shard_map/all_to_all | solution.py:305
  117.5 0.8 shard_map.143
  118.3 20.4 %all_to_all.26.parts = bf16[8,256,256]{2,1,0:T(8,128)(2,1)S(1)} all-to-all(bf16[8,256,256]{2,1,0:T(8,128)(2,1)S(1)} %bitcast.20), channel_id=1, replica_groups=mesh['x'=4,'yh'=4,'c'=2,'z'=16,'yl'=2] {'x','yl'}, dimensions={0} | all-to-all | bytes 2097152 | tf_op jit(solution)/shard_map/all_to_all | solution.py:305
  138.7 0.9 shard_map.144
  139.6 26.9 %all_to_all.27 = bf16[64,4,256]{2,1,0:T(4,128)(2,1)S(1)} all-to-all(bf16[64,4,256]{2,1,0:T(4,128)(2,1)S(1)} %reshape.32), channel_id=1, replica_groups=mesh['x'=4,'yh'=4,'c'=2,'z'=16,'yl'=2] {'yh','z'}, dimensions={0} | all-to-all | bytes 262144 | tf_op jit(solution)/shard_map/all_to_all | solution.py:305
  166.5 0.7 convert_reduce_fusion
  (18 shorter events, 0.2 us)
Async XLA Ops:
  0.6 1.2 copy-start
  3.1 36.4 %all-to-all-start = ((bf16[32,8,256]{2,1,0:T(8,128)(2,1)}), bf16[32,8,256]{2,1,0:T(8,128)(2,1)S(1)}, u32[]{:S(2)}, u32[]{:S(2)}) async-start(bf16[32,8,256]{2,1,0:T(8,128)(2,1)} %broadcast_in_dim.8), calls=%async_computation | async-start | bytes 262144 | tf_op jit(solution)/shard_map/all_to_all | solution.py:305
  35.1 45.2 %copy-start.6 = (s32[128]{0:T(128)S(1)}, s32[128]{0:T(128)}, u32[]{:S(2)}) copy-start(s32[128]{0:T(128)} %param.18) | copy-start | bytes 1540
  35.2 45.3 %copy-start.4 = (bf16[512,256]{1,0:T(8,128)(2,1)S(1)}, bf16[512,256]{1,0:T(8,128)(2,1)}, u32[]{:S(2)}) copy-start(bf16[512,256]{1,0:T(8,128)(2,1)} %param.20) | copy-start | bytes 786436
  35.2 45.3 %copy-start.5 = (bf16[13,128]{1,0:T(8,128)(2,1)S(1)}, bf16[13,128]{1,0:T(8,128)(2,1)}, u32[]{:S(2)}) copy-start(bf16[13,128]{1,0:T(8,128)(2,1)} %param.17) | copy-start | bytes 9988
  35.2 66.1 %copy-start.1 = (s32[3]{0:T(128)S(1)}, s32[3]{0:T(128)}, u32[]{:S(2)}) copy-start(s32[3]{0:T(128)} %pad_add_fusion.place._) | copy-start | bytes 40
  35.2 66.1 %copy-start.2 = (f32[512]{0:T(512)S(1)}, f32[512]{0:T(512)}, u32[]{:S(2)}) copy-start(f32[512]{0:T(512)} %param.25) | copy-start | bytes 6148
  35.2 66.1 %copy-start.3 = (s32[32]{0:T(128)S(1)}, s32[32]{0:T(128)}, u32[]{:S(2)}) copy-start(s32[32]{0:T(128)} %table_of.1) | copy-start | bytes 388
  39.5 61.8 %all-to-all-start.1 = ((bf16[32,128,128]{2,1,0:T(8,128)(2,1)}), bf16[32,128,128]{2,1,0:T(8,128)(2,1)S(1)}, u32[]{:S(2)}, u32[]{:S(2)}) async-start(bf16[32,128,128]{2,1,0:T(8,128)(2,1)} %bitcast.7), calls=%async_computation.1 | async-start | bytes 2097152 | tf_op jit(solution)/shard_map/all_to_all | solution.py:305
  48.5 9.1 %collective-permute-start = (bf16[32,8,256]{2,1,0:T(8,128)(2,1)S(1)}, bf16[32,8,256]{2,1,0:T(8,128)(2,1)S(1)}, u32[]{:S(2)}, u32[]{:S(2)}) collective-permute-start(bf16[32,8,256]{2,1,0:T(8,128)(2,1)S(1)} %all-to-all-done), channel_id=1, source_target_pairs={{0,64},{64,0},{128,192},{192,128},{1,65},{65,1},{129,193},{193,129... | collective-permute-start | bytes 393224 | tf_op jit(solution)/shard_map/ppermute | solution.py:345
  57.6 15.1 %collective-permute-start.3 = (bf16[32,16,256]{2,1,0:T(8,128)(2,1)S(1)}, bf16[32,16,256]{2,1,0:T(8,128)(2,1)S(1)}, u32[]{:S(2)}, u32[]{:S(2)}) collective-permute-start(bf16[32,16,256]{2,1,0:T(8,128)(2,1)S(1)} %constant_dynamic-update-slice_fusion), channel_id=1, source_target_pairs={{0,768},{256,0},{512,256},{768,512},{1,769},{257,1},{513,257},{769... | collective-permute-start | bytes 786440 | tf_op jit(solution)/shard_map/ppermute | solution.py:313
  62.3 12.6 %collective-permute-start.2 = (bf16[32,16,256]{2,1,0:T(8,128)(2,1)S(1)}, bf16[32,16,256]{2,1,0:T(8,128)(2,1)S(1)}, u32[]{:S(2)}, u32[]{:S(2)}) collective-permute-start(bf16[32,16,256]{2,1,0:T(8,128)(2,1)S(1)} %constant_dynamic-update-slice_fusion), channel_id=1, source_target_pairs={{0,512},{256,768},{512,0},{768,256},{1,513},{257,769},{513,1},{769... | collective-permute-start | bytes 786440 | tf_op jit(solution)/shard_map/ppermute | solution.py:313
  65.0 13.3 %collective-permute-start.1 = (bf16[32,16,256]{2,1,0:T(8,128)(2,1)S(1)}, bf16[32,16,256]{2,1,0:T(8,128)(2,1)S(1)}, u32[]{:S(2)}, u32[]{:S(2)}) collective-permute-start(bf16[32,16,256]{2,1,0:T(8,128)(2,1)S(1)} %constant_dynamic-update-slice_fusion), channel_id=1, source_target_pairs={{0,256},{256,512},{512,768},{768,0},{1,257},{257,513},{513,769},{7... | collective-permute-start | bytes 786440 | tf_op jit(solution)/shard_map/ppermute | solution.py:313
  78.4 4.7 %collective-permute-start.4 = (bf16[4,32,16,256]{3,2,1,0:T(8,128)(2,1)S(1)}, bf16[4,32,16,256]{3,2,1,0:T(8,128)(2,1)}, u32[]{:S(2)}, u32[]{:S(2)}) collective-permute-start(bf16[4,32,16,256]{3,2,1,0:T(8,128)(2,1)S(1)} %pad_maximum_fusion.own), channel_id=1, source_target_pairs={{0,32},{32,0},{1,33},{33,1},{2,34},{34,2},{3,35},{35,3},{4,36},{36... | collective-permute-start | bytes 3145736 | tf_op jit(solution)/shard_map/ppermute | solution.py:313

commit v7 on v6

--- a/solution.py
+++ b/solution.py
@@ -247,16 +247,17 @@
 
 
 def turn_lanes(place, counts):
-    rows = counts.shape[0] // 8
+    rows = counts.shape[0] // 2
     return pl.pallas_call(
         lanes_kernel,
         out_shape=jax.ShapeDtypeStruct(counts.shape, BF),
-        grid=(8,),
+        grid=(2,),
         in_specs=[
             pl.BlockSpec(memory_space=pltpu.SMEM),
             pl.BlockSpec((rows, LOOK), lambda i: (i, 0)),
         ],
         out_specs=pl.BlockSpec((rows, LOOK), lambda i: (i, 0)),
+        compiler_params=pltpu.CompilerParams(vmem_limit_bytes=60 * 2**20),
         cost_estimate=pl.CostEstimate(
             flops=2 * 10**8, bytes_accessed=3 * 2**20, transcendentals=0
         ),
@@ -338,12 +339,12 @@
     mine, pool_counts = lax.optimization_barrier((mine, pool_counts))
     looked = swap(mine, MP)
     counts = turn_lanes(place, pool_counts).reshape(SHARDS, N, LOOK)
-    counts, *weights = lax.optimization_barrier((counts, cross_down, cross_up, w_top1, w_top2))
-    packed = pack(*weights)
-    looked, counts, packed = lax.optimization_barrier((looked, counts, packed))
+    looked, counts = lax.optimization_barrier((looked, counts))
     counts = swap(counts, MP)
     exchanged = lax.ppermute(looked, "yh", [(i, i ^ 1) for i in range(YH)])
     looked = jnp.concatenate([looked, exchanged], axis=1)
+    looked, *weights = lax.optimization_barrier((looked, cross_down, cross_up, w_top1, w_top2))
+    packed = pack(*weights)
     looked = jnp.stack([looked] + [turn(looked, "x", X, k) for k in range(1, X)])
     others = turn(looked, "c", CORES, 1)
 

time: 168 us -> 163 us (0.970)
  starting transfers between devices: 46 us -> 41.3 us
  waiting for transfers between devices: 39.1 us -> 43.4 us
  Pallas kernels: 23.4 us -> 20 us
    all_to_all x2, waiting for transfers between devices: 22.4 us -> 30.2 us  [swap(): return lax.all_to_all(value, axes, split_axis=0, concat_axis=0, tiled=True)]
    all_to_all x2, starting transfers between devices: 29.4 us -> 24.7 us  [swap(): return lax.all_to_all(value, axes, split_axis=0, concat_axis=0, tiled=True)]
    pallas_call x1, Pallas kernels: 6.1 us -> 2.68 us  [turn_lanes(): pl.pallas_call(lanes_kernel, out_shape=jax.ShapeDtypeStruct(counts.shape,...]
    ppermute x4, waiting for transfers between devices: 12.1 us -> 9.15 us  [turn(): lax.ppermute(value, axis, [(i, (i + shift) % size) for i in range(size)])]
  transfers between devices with their start and end apart: 7 -> 7, of which waited for: 7 -> 6; matrix products, arithmetic and copies ran while one was open for 1% -> 1% of each run, Pallas kernels for 7% -> 5%
where the time goes in v7:
time: 163 us; the launch traced here: 162 us
  blocking collectives  51.5 us (32%)
  waiting for transfers between devices  43.4 us (27%)
  starting transfers between devices  41.3 us (25%)
  Pallas kernels  20 us (12%)
  local copies, waits for them, and re-layouts  2.55 us (2%)
    all_to_all x3, blocking collectives, swap(): return lax.all_to_all(value, axes, split_axis=0, concat_axis=0, tiled=True)  51.5 us
    all_to_all x2, waiting for transfers between devices, swap(): return lax.all_to_all(value, axes, split_axis=0, concat_axis=0, tiled=True)  30.2 us
    all_to_all x2, starting transfers between devices, swap(): return lax.all_to_all(value, axes, split_axis=0, concat_axis=0, tiled=True)  24.7 us
    ppermute x4, starting transfers between devices, turn(): lax.ppermute(value, axis, [(i, (i + shift) % size) for i in range(size)])  12.1 us
    pallas_call x1, Pallas kernels, run_step(): pl.pallas_call(step_kernel, out_shape=(jax.ShapeDtypeStruct((CORES, X, YL...  10.7 us
    ppermute x4, waiting for transfers between devices, turn(): lax.ppermute(value, axis, [(i, (i + shift) % size) for i in range(size)])  9.15 us
    pallas_call x1, Pallas kernels, pack(): pl.pallas_call(pack_kernel, out_shape=jax.ShapeDtypeStruct((PACKED, E), B...  4.91 us
    ppermute x1, starting transfers between devices, shards(): exchanged = lax.ppermute(looked, 'yh', [(i, i ^ 1) for i in range(YH)])  4.5 us
  transfers between devices with their start and end apart: 7, of which 6 were waited for; matrix products, arithmetic and copies ran while one was open for 1% of the time, Pallas kernels for 5%

profile of v7, /device:TPU:8, one launch (start us, length us, event | category | flops | bytes accessed | tf_op | source)
XLA Modules:
  0.0 162.1 jit_solution(14430356334872126971)
XLA Ops:
  0.7 0.8 constant_dynamic-slice_fusion
  1.5 0.1 slice_bitcast_fusion.1
  1.5 0.1 pad_add_fusion.1
  1.6 0.2 copy-done
  1.9 0.6 gather_fusion
  2.4 0.7 broadcast_in_dim.8
  3.1 20.4 %all-to-all-start = ((bf16[32,8,256]{2,1,0:T(8,128)(2,1)}), bf16[32,8,256]{2,1,0:T(8,128)(2,1)S(1)}, u32[]{:S(2)}, u32[]{:S(2)}) async-start(bf16[32,8,256]{2,1,0:T(8,128)(2,1)} %broadcast_in_dim.8), calls=%async_computation | async-start | bytes 262144 | tf_op jit(solution)/shard_map/all_to_all | solution.py:306
  23.5 0.7 pad_add_fusion.place._
  24.1 2.7 %shard_map.140 = bf16[4096,128]{1,0:T(8,128)(2,1)} custom-call(s32[3]{0:T(128)} %pad_add_fusion.place._, s32[4096,128]{1,0:T(8,128)} %counts), custom_call_target="tpu_custom_call" | custom-call | flops 200000000 | bytes 3145728 | tf_op jit(solution)/shard_map/pallas_call | solution.py:251
  26.8 12.6 %all-to-all-done = bf16[32,8,256]{2,1,0:T(8,128)(2,1)S(1)} async-done(((bf16[32,8,256]{2,1,0:T(8,128)(2,1)}), bf16[32,8,256]{2,1,0:T(8,128)(2,1)S(1)}, u32[]{:S(2)}, u32[]{:S(2)}) %all-to-all-start) | async-done | bytes 131104 | tf_op jit(solution)/shard_map/all_to_all | solution.py:306
  39.5 4.3 %all-to-all-start.1 = ((bf16[32,128,128]{2,1,0:T(8,128)(2,1)}), bf16[32,128,128]{2,1,0:T(8,128)(2,1)S(1)}, u32[]{:S(2)}, u32[]{:S(2)}) async-start(bf16[32,128,128]{2,1,0:T(8,128)(2,1)} %bitcast.23), calls=%async_computation.1 | async-start | bytes 2097152 | tf_op jit(solution)/shard_map/all_to_all | solution.py:306
  43.8 4.5 %collective-permute-start = (bf16[32,8,256]{2,1,0:T(8,128)(2,1)S(1)}, bf16[32,8,256]{2,1,0:T(8,128)(2,1)S(1)}, u32[]{:S(2)}, u32[]{:S(2)}) collective-permute-start(bf16[32,8,256]{2,1,0:T(8,128)(2,1)S(1)} %all-to-all-done), channel_id=1, source_target_pairs={{0,64},{64,0},{128,192},{192,128},{1,65},{65,1},{129,193},{193,129... | collective-permute-start | bytes 393224 | tf_op jit(solution)/shard_map/ppermute | solution.py:344
  48.3 4.0 %collective-permute-done = bf16[32,8,256]{2,1,0:T(8,128)(2,1)S(1)} collective-permute-done((bf16[32,8,256]{2,1,0:T(8,128)(2,1)S(1)}, bf16[32,8,256]{2,1,0:T(8,128)(2,1)S(1)}, u32[]{:S(2)}, u32[]{:S(2)}) %collective-permute-start) | collective-permute-done | bytes 131104 | tf_op jit(solution)/shard_map/ppermute | solution.py:344
  52.4 4.7 %collective-permute-start.3 = (bf16[32,16,256]{2,1,0:T(8,128)(2,1)S(1)}, bf16[32,16,256]{2,1,0:T(8,128)(2,1)S(1)}, u32[]{:S(2)}, u32[]{:S(2)}) collective-permute-start(bf16[32,16,256]{2,1,0:T(8,128)(2,1)S(1)} %pad_maximum_fusion.1), channel_id=1, source_target_pairs={{0,768},{256,0},{512,256},{768,512},{1,769},{257,1},{513,257},{769... | collective-permute-start | bytes 786440 | tf_op jit(solution)/shard_map/ppermute | solution.py:314
  57.0 2.7 %collective-permute-start.2 = (bf16[32,16,256]{2,1,0:T(8,128)(2,1)S(1)}, bf16[32,16,256]{2,1,0:T(8,128)(2,1)S(1)}, u32[]{:S(2)}, u32[]{:S(2)}) collective-permute-start(bf16[32,16,256]{2,1,0:T(8,128)(2,1)S(1)} %pad_maximum_fusion.1), channel_id=1, source_target_pairs={{0,512},{256,768},{512,0},{768,256},{1,513},{257,769},{513,1},{769... | collective-permute-start | bytes 786440 | tf_op jit(solution)/shard_map/ppermute | solution.py:314
  59.8 2.8 %collective-permute-start.1 = (bf16[32,16,256]{2,1,0:T(8,128)(2,1)S(1)}, bf16[32,16,256]{2,1,0:T(8,128)(2,1)S(1)}, u32[]{:S(2)}, u32[]{:S(2)}) collective-permute-start(bf16[32,16,256]{2,1,0:T(8,128)(2,1)S(1)} %pad_maximum_fusion.1), channel_id=1, source_target_pairs={{0,256},{256,512},{512,768},{768,0},{1,257},{257,513},{513,769},{7... | collective-permute-start | bytes 786440 | tf_op jit(solution)/shard_map/ppermute | solution.py:314
  62.6 3.7 %collective-permute-done.3 = bf16[32,16,256]{2,1,0:T(8,128)(2,1)S(1)} collective-permute-done((bf16[32,16,256]{2,1,0:T(8,128)(2,1)S(1)}, bf16[32,16,256]{2,1,0:T(8,128)(2,1)S(1)}, u32[]{:S(2)}, u32[]{:S(2)}) %collective-permute-start.3) | collective-permute-done | bytes 262176 | tf_op jit(solution)/shard_map/ppermute | solution.py:314
  66.3 2.7 %collective-permute-done.2 = bf16[32,16,256]{2,1,0:T(8,128)(2,1)S(1)} collective-permute-done((bf16[32,16,256]{2,1,0:T(8,128)(2,1)S(1)}, bf16[32,16,256]{2,1,0:T(8,128)(2,1)S(1)}, u32[]{:S(2)}, u32[]{:S(2)}) %collective-permute-start.2) | collective-permute-done | bytes 262176 | tf_op jit(solution)/shard_map/ppermute | solution.py:314
  69.0 2.7 %collective-permute-done.1 = bf16[32,16,256]{2,1,0:T(8,128)(2,1)S(1)} collective-permute-done((bf16[32,16,256]{2,1,0:T(8,128)(2,1)S(1)}, bf16[32,16,256]{2,1,0:T(8,128)(2,1)S(1)}, u32[]{:S(2)}, u32[]{:S(2)}) %collective-permute-start.1) | collective-permute-done | bytes 262176 | tf_op jit(solution)/shard_map/ppermute | solution.py:314
  71.7 0.1 pad_maximum_fusion.own
  71.9 1.9 %collective-permute-start.4 = (bf16[4,32,16,256]{3,2,1,0:T(8,128)(2,1)S(1)}, bf16[4,32,16,256]{3,2,1,0:T(8,128)(2,1)}, u32[]{:S(2)}, u32[]{:S(2)}) collective-permute-start(bf16[4,32,16,256]{3,2,1,0:T(8,128)(2,1)S(1)} %pad_maximum_fusion.own), channel_id=1, source_target_pairs={{0,32},{32,0},{1,33},{33,1},{2,34},{34,2},{3,35},{35,3},{4,36},{36... | collective-permute-start | bytes 3145736 | tf_op jit(solution)/shard_map/ppermute | solution.py:314
  73.8 0.1 copy.15.labels
  73.9 1.0 fusion.3.bottom
  75.0 4.9 %shard_map.141.packed_hbm = bf16[10240,256]{1,0:T(8,128)(2,1)} custom-call(bf16[2304,256]{1,0:T(8,128)(2,1)} %down, bf16[256,2304]{1,0:T(8,128)(2,1)} %up, bf16[2304,512]{1,0:T(8,128)(2,1)} %top1, bf16[512,512]{1,0:T(8,128)(2,1)} %top2), custom_call_target="tpu_custom_call" | custom-call | bytes 10485760 | tf_op jit(solution)/shard_map/pallas_call | solution.py:225
  79.9 17.5 %all-to-all-done.1.counts = bf16[32,128,128]{2,1,0:T(8,128)(2,1)S(1)} async-done(((bf16[32,128,128]{2,1,0:T(8,128)(2,1)}), bf16[32,128,128]{2,1,0:T(8,128)(2,1)S(1)}, u32[]{:S(2)}, u32[]{:S(2)}) %all-to-all-start.1) | async-done | bytes 1048608 | tf_op jit(solution)/shard_map/all_to_all | solution.py:306
  97.5 10.7 %shard_map.142 = (bf16[2,4,2,16,16,256]{5,4,3,2,1,0:T(8,128)(2,1)S(1)}, f32[1,128]{1,0:T(1,128)}) custom-call(s32[3]{0:T(128)S(1)} %copy-done.1, s32[32]{0:T(128)S(1)} %copy-done.3, bf16[128,256]{1,0:T(8,128)(2,1)S(1)} %fusion.3.bottom, s32[128,1]{1,0:T(8,128)S(1)} %copy.15.labels, f32[1,512]{1,0:T(1,128)S(1)} %bitcast.22, ...), custom_call_target="tpu_custom_call" | custom-call | flops 4000000000 | bytes 12582912 | tf_op jit(solution)/shard_map/pallas_call | solution.py:181
  108.2 5.4 %all_to_all.25.halves = bf16[2,2048,256]{2,1,0:T(8,128)(2,1)S(1)} all-to-all(bf16[2,2048,256]{2,1,0:T(8,128)(2,1)S(1)} %bitcast.21), channel_id=1, replica_groups=mesh['x'=4,'yh'=4,'c'=2,'z'=16,'yl'=2] {'c'}, dimensions={0} | all-to-all | bytes 4194304 | tf_op jit(solution)/shard_map/all_to_all | solution.py:306
  113.6 0.8 shard_map.143
  114.4 20.4 %all_to_all.26.parts = bf16[8,256,256]{2,1,0:T(8,128)(2,1)S(1)} all-to-all(bf16[8,256,256]{2,1,0:T(8,128)(2,1)S(1)} %bitcast.20), channel_id=1, replica_groups=mesh['x'=4,'yh'=4,'c'=2,'z'=16,'yl'=2] {'x','yl'}, dimensions={0} | all-to-all | bytes 2097152 | tf_op jit(solution)/shard_map/all_to_all | solution.py:306
  134.8 0.9 shard_map.144
  135.7 25.7 %all_to_all.27 = bf16[64,4,256]{2,1,0:T(4,128)(2,1)S(1)} all-to-all(bf16[64,4,256]{2,1,0:T(4,128)(2,1)S(1)} %reshape.32), channel_id=1, replica_groups=mesh['x'=4,'yh'=4,'c'=2,'z'=16,'yl'=2] {'yh','z'}, dimensions={0} | all-to-all | bytes 262144 | tf_op jit(solution)/shard_map/all_to_all | solution.py:306
  161.4 0.7 convert_reduce_fusion
  (17 shorter events, 0.1 us)
Async XLA Ops:
  0.6 1.2 copy-start
  3.1 36.4 %all-to-all-start = ((bf16[32,8,256]{2,1,0:T(8,128)(2,1)}), bf16[32,8,256]{2,1,0:T(8,128)(2,1)S(1)}, u32[]{:S(2)}, u32[]{:S(2)}) async-start(bf16[32,8,256]{2,1,0:T(8,128)(2,1)} %broadcast_in_dim.8), calls=%async_computation | async-start | bytes 262144 | tf_op jit(solution)/shard_map/all_to_all | solution.py:306
  39.5 34.3 %copy-start.6 = (s32[128]{0:T(128)S(1)}, s32[128]{0:T(128)}, u32[]{:S(2)}) copy-start(s32[128]{0:T(128)} %param.18) | copy-start | bytes 1540
  39.5 34.4 %copy-start.4 = (bf16[512,256]{1,0:T(8,128)(2,1)S(1)}, bf16[512,256]{1,0:T(8,128)(2,1)}, u32[]{:S(2)}) copy-start(bf16[512,256]{1,0:T(8,128)(2,1)} %param.20) | copy-start | bytes 786436
  39.5 34.4 %copy-start.5 = (bf16[13,512]{1,0:T(8,128)(2,1)S(1)}, bf16[13,512]{1,0:T(8,128)(2,1)}, u32[]{:S(2)}) copy-start(bf16[13,512]{1,0:T(8,128)(2,1)} %param.19) | copy-start | bytes 39940
  39.5 58.0 %all-to-all-start.1 = ((bf16[32,128,128]{2,1,0:T(8,128)(2,1)}), bf16[32,128,128]{2,1,0:T(8,128)(2,1)S(1)}, u32[]{:S(2)}, u32[]{:S(2)}) async-start(bf16[32,128,128]{2,1,0:T(8,128)(2,1)} %bitcast.23), calls=%async_computation.1 | async-start | bytes 2097152 | tf_op jit(solution)/shard_map/all_to_all | solution.py:306
  43.8 8.6 %collective-permute-start = (bf16[32,8,256]{2,1,0:T(8,128)(2,1)S(1)}, bf16[32,8,256]{2,1,0:T(8,128)(2,1)S(1)}, u32[]{:S(2)}, u32[]{:S(2)}) collective-permute-start(bf16[32,8,256]{2,1,0:T(8,128)(2,1)S(1)} %all-to-all-done), channel_id=1, source_target_pairs={{0,64},{64,0},{128,192},{192,128},{1,65},{65,1},{129,193},{193,129... | collective-permute-start | bytes 393224 | tf_op jit(solution)/shard_map/ppermute | solution.py:344
  52.4 13.9 %collective-permute-start.3 = (bf16[32,16,256]{2,1,0:T(8,128)(2,1)S(1)}, bf16[32,16,256]{2,1,0:T(8,128)(2,1)S(1)}, u32[]{:S(2)}, u32[]{:S(2)}) collective-permute-start(bf16[32,16,256]{2,1,0:T(8,128)(2,1)S(1)} %pad_maximum_fusion.1), channel_id=1, source_target_pairs={{0,768},{256,0},{512,256},{768,512},{1,769},{257,1},{513,257},{769... | collective-permute-start | bytes 786440 | tf_op jit(solution)/shard_map/ppermute | solution.py:314
  57.0 11.9 %collective-permute-start.2 = (bf16[32,16,256]{2,1,0:T(8,128)(2,1)S(1)}, bf16[32,16,256]{2,1,0:T(8,128)(2,1)S(1)}, u32[]{:S(2)}, u32[]{:S(2)}) collective-permute-start(bf16[32,16,256]{2,1,0:T(8,128)(2,1)S(1)} %pad_maximum_fusion.1), channel_id=1, source_target_pairs={{0,512},{256,768},{512,0},{768,256},{1,513},{257,769},{513,1},{769... | collective-permute-start | bytes 786440 | tf_op jit(solution)/shard_map/ppermute | solution.py:314
  59.8 12.0 %collective-permute-start.1 = (bf16[32,16,256]{2,1,0:T(8,128)(2,1)S(1)}, bf16[32,16,256]{2,1,0:T(8,128)(2,1)S(1)}, u32[]{:S(2)}, u32[]{:S(2)}) collective-permute-start(bf16[32,16,256]{2,1,0:T(8,128)(2,1)S(1)} %pad_maximum_fusion.1), channel_id=1, source_target_pairs={{0,256},{256,512},{512,768},{768,0},{1,257},{257,513},{513,769},{7... | collective-permute-start | bytes 786440 | tf_op jit(solution)/shard_map/ppermute | solution.py:314
  71.9 8.1 %collective-permute-start.4 = (bf16[4,32,16,256]{3,2,1,0:T(8,128)(2,1)S(1)}, bf16[4,32,16,256]{3,2,1,0:T(8,128)(2,1)}, u32[]{:S(2)}, u32[]{:S(2)}) collective-permute-start(bf16[4,32,16,256]{3,2,1,0:T(8,128)(2,1)S(1)} %pad_maximum_fusion.own), channel_id=1, source_target_pairs={{0,32},{32,0},{1,33},{33,1},{2,34},{34,2},{3,35},{35,3},{4,36},{36... | collective-permute-start | bytes 3145736 | tf_op jit(solution)/shard_map/ppermute | solution.py:314
  75.0 22.5 %copy-start.1 = (s32[3]{0:T(128)S(1)}, s32[3]{0:T(128)}, u32[]{:S(2)}) copy-start(s32[3]{0:T(128)} %pad_add_fusion.place._) | copy-start | bytes 40
  75.0 22.5 %copy-start.2 = (f32[512]{0:T(512)S(1)}, f32[512]{0:T(512)}, u32[]{:S(2)}) copy-start(f32[512]{0:T(512)} %param.25) | copy-start | bytes 6148
  75.0 22.5 %copy-start.3 = (s32[32]{0:T(128)S(1)}, s32[32]{0:T(128)}, u32[]{:S(2)}) copy-start(s32[32]{0:T(128)} %table_of.1) | copy-start | bytes 388

commit v8 on v7

--- a/solution.py
+++ b/solution.py
@@ -81,7 +81,7 @@
     ]
     for copy in copies:
         copy.start()
-    my_x, my_c = place[0], place[2]
+    my_x, my_c, my_yl = place[0], place[2], place[3]
 
     def down(k):
         return packed[cols(k), :]
@@ -109,8 +109,9 @@
         for k in range(PER):
             m = order[t * PER + k]
             turns = [lax.rem(my_x + X - x, X) for x in range(X)]
-            near = [own[k_x, m] for k_x in turns]
-            far = [other[k_x, m] for k_x in turns]
+            at = lax.bitwise_xor(m, my_yl)
+            near = [own[k_x, at] for k_x in turns]
+            far = [other[k_x, at] for k_x in turns]
             rows = jnp.concatenate(
                 [jnp.where(my_c == 0, a, b) for a, b in zip(near, far)]
                 + [jnp.where(my_c == 0, b, a) for a, b in zip(near, far)],
@@ -330,17 +331,18 @@
     w_out,
 ):
     my_x, my_yh, my_c = lax.axis_index("x"), lax.axis_index("yh"), lax.axis_index("c")
-    place = jnp.stack([my_x, my_yh, my_c]).astype(jnp.int32)
+    place = jnp.stack([my_x, my_yh, my_c, lax.axis_index("yl")]).astype(jnp.int32)
     first = my_x * 32 + jnp.bitwise_and(my_yh, 1) * 8 + my_c * 4
     span = lax.dynamic_slice(row_ids, (0, first), (1, 20))[0]
     ids = jnp.concatenate([span[:4], span[16:]])
     mine = jnp.take(table, ids, axis=0, mode="clip").astype(BF)
-    mine = jnp.broadcast_to(mine, (SHARDS, 8, E))
+    mine = jnp.broadcast_to(mine, (Z, 8, E))
     mine, pool_counts = lax.optimization_barrier((mine, pool_counts))
-    looked = swap(mine, MP)
+    looked = swap(mine, "z")
     counts = turn_lanes(place, pool_counts).reshape(SHARDS, N, LOOK)
     looked, counts = lax.optimization_barrier((looked, counts))
     counts = swap(counts, MP)
+    looked = jnp.stack([looked, turn(looked, "yl", YL, 1)], axis=1).reshape(SHARDS, 8, E)
     exchanged = lax.ppermute(looked, "yh", [(i, i ^ 1) for i in range(YH)])
     looked = jnp.concatenate([looked, exchanged], axis=1)
     looked, *weights = lax.optimization_barrier((looked, cross_down, cross_up, w_top1, w_top2))

time: 163 us -> 159 us (0.975)
  waiting for transfers between devices: 43.4 us -> 38.1 us
    all_to_all x2, waiting for transfers between devices: 30.2 us -> 22 us  [swap(): return lax.all_to_all(value, axes, split_axis=0, concat_axis=0, tiled=True)]
    ppermute x4 -> x5, waiting for transfers between devices: 9.15 us -> 12.3 us  [turn(): lax.ppermute(value, axis, [(i, (i + shift) % size) for i in range(size)])]
    ppermute x4 -> x5, starting transfers between devices: 12.1 us -> 14.2 us  [turn(): lax.ppermute(value, axis, [(i, (i + shift) % size) for i in range(size)])]
  transfers between devices with their start and end apart: 7 -> 8, of which waited for: 6 -> 7; matrix products, arithmetic and copies ran while one was open for 1% -> 1% of each run, Pallas kernels for 5% -> 5%
where the time goes in v8:
time: 159 us; the launch traced here: 158 us
  blocking collectives  51.8 us (33%)
  starting transfers between devices  42.3 us (27%)
  waiting for transfers between devices  38.1 us (24%)
  Pallas kernels  20 us (13%)
  local copies, waits for them, and re-layouts  2.51 us (2%)
    all_to_all x3, blocking collectives, swap(): return lax.all_to_all(value, axes, split_axis=0, concat_axis=0, tiled=True)  51.8 us
    all_to_all x2, starting transfers between devices, swap(): return lax.all_to_all(value, axes, split_axis=0, concat_axis=0, tiled=True)  23.5 us
    all_to_all x2, waiting for transfers between devices, swap(): return lax.all_to_all(value, axes, split_axis=0, concat_axis=0, tiled=True)  22 us
    ppermute x5, starting transfers between devices, turn(): lax.ppermute(value, axis, [(i, (i + shift) % size) for i in range(size)])  14.2 us
    ppermute x5, waiting for transfers between devices, turn(): lax.ppermute(value, axis, [(i, (i + shift) % size) for i in range(size)])  12.3 us
    pallas_call x1, Pallas kernels, run_step(): pl.pallas_call(step_kernel, out_shape=(jax.ShapeDtypeStruct((CORES, X, YL...  10.7 us
    pallas_call x1, Pallas kernels, pack(): pl.pallas_call(pack_kernel, out_shape=jax.ShapeDtypeStruct((PACKED, E), B...  4.91 us
    ppermute x1, starting transfers between devices, shards(): exchanged = lax.ppermute(looked, 'yh', [(i, i ^ 1) for i in range(YH)])  4.5 us
  transfers between devices with their start and end apart: 8, of which 7 were waited for; matrix products, arithmetic and copies ran while one was open for 1% of the time, Pallas kernels for 5%

profile of v8, /device:TPU:8, one launch (start us, length us, event | category | flops | bytes accessed | tf_op | source)
XLA Modules:
  0.0 158.0 jit_solution(9651997654357146634)
XLA Ops:
  0.7 0.8 constant_dynamic-slice_fusion
  1.6 0.2 copy-done
  1.9 0.6 gather_fusion
  2.4 0.6 broadcast_in_dim.8
  3.1 18.9 %all-to-all-start = ((bf16[16,8,256]{2,1,0:T(8,128)(2,1)}), bf16[16,8,256]{2,1,0:T(8,128)(2,1)S(1)}, u32[]{:S(2)}, u32[]{:S(2)}) async-start(bf16[16,8,256]{2,1,0:T(8,128)(2,1)} %broadcast_in_dim.8), calls=%async_computation | async-start | bytes 131072 | tf_op jit(solution)/shard_map/all_to_all | solution.py:307
  21.9 0.6 pad_add_fusion.place._
  22.6 2.7 %shard_map.140 = bf16[4096,128]{1,0:T(8,128)(2,1)} custom-call(s32[4]{0:T(128)} %pad_add_fusion.place._, s32[4096,128]{1,0:T(8,128)} %counts), custom_call_target="tpu_custom_call" | custom-call | flops 200000000 | bytes 3145728 | tf_op jit(solution)/shard_map/pallas_call | solution.py:252
  25.3 9.4 %all-to-all-done = bf16[16,8,256]{2,1,0:T(8,128)(2,1)S(1)} async-done(((bf16[16,8,256]{2,1,0:T(8,128)(2,1)}), bf16[16,8,256]{2,1,0:T(8,128)(2,1)S(1)}, u32[]{:S(2)}, u32[]{:S(2)}) %all-to-all-start) | async-done | bytes 65568 | tf_op jit(solution)/shard_map/all_to_all | solution.py:307
  34.7 4.7 %all-to-all-start.1 = ((bf16[32,128,128]{2,1,0:T(8,128)(2,1)}), bf16[32,128,128]{2,1,0:T(8,128)(2,1)S(1)}, u32[]{:S(2)}, u32[]{:S(2)}) async-start(bf16[32,128,128]{2,1,0:T(8,128)(2,1)} %bitcast.29), calls=%async_computation.1 | async-start | bytes 2097152 | tf_op jit(solution)/shard_map/all_to_all | solution.py:307
  39.3 2.1 %collective-permute-start = (bf16[16,8,256]{2,1,0:T(8,128)(2,1)S(1)}, bf16[16,8,256]{2,1,0:T(8,128)(2,1)S(1)}, u32[]{:S(2)}, u32[]{:S(2)}) collective-permute-start(bf16[16,8,256]{2,1,0:T(8,128)(2,1)S(1)} %all-to-all-done), channel_id=1, source_target_pairs={{0,1},{1,0},{2,3},{3,2},{4,5},{5,4},{6,7},{7,6},{8,9},{9,8},{10,11... | collective-permute-start | bytes 196616 | tf_op jit(solution)/shard_map/ppermute | solution.py:315
  41.5 4.4 %collective-permute-done = bf16[16,8,256]{2,1,0:T(8,128)(2,1)S(1)} collective-permute-done((bf16[16,8,256]{2,1,0:T(8,128)(2,1)S(1)}, bf16[16,8,256]{2,1,0:T(8,128)(2,1)S(1)}, u32[]{:S(2)}, u32[]{:S(2)}) %collective-permute-start) | collective-permute-done | bytes 65568 | tf_op jit(solution)/shard_map/ppermute | solution.py:315
  45.9 4.5 %collective-permute-start.1 = (bf16[32,8,256]{2,1,0:T(8,128)(2,1)S(1)}, bf16[32,8,256]{2,1,0:T(8,128)(2,1)S(1)}, u32[]{:S(2)}, u32[]{:S(2)}) collective-permute-start(bf16[32,8,256]{2,1,0:T(8,128)(2,1)S(1)} %bitcast.31), channel_id=1, source_target_pairs={{0,64},{64,0},{128,192},{192,128},{1,65},{65,1},{129,193},{193,129... | collective-permute-start | bytes 393224 | tf_op jit(solution)/shard_map/ppermute | solution.py:346
  50.4 3.8 %collective-permute-done.1 = bf16[32,8,256]{2,1,0:T(8,128)(2,1)S(1)} collective-permute-done((bf16[32,8,256]{2,1,0:T(8,128)(2,1)S(1)}, bf16[32,8,256]{2,1,0:T(8,128)(2,1)S(1)}, u32[]{:S(2)}, u32[]{:S(2)}) %collective-permute-start.1) | collective-permute-done | bytes 131104 | tf_op jit(solution)/shard_map/ppermute | solution.py:346
  54.2 4.7 %collective-permute-start.4 = (bf16[32,16,256]{2,1,0:T(8,128)(2,1)S(1)}, bf16[32,16,256]{2,1,0:T(8,128)(2,1)S(1)}, u32[]{:S(2)}, u32[]{:S(2)}) collective-permute-start(bf16[32,16,256]{2,1,0:T(8,128)(2,1)S(1)} %pad_maximum_fusion.1), channel_id=1, source_target_pairs={{0,768},{256,0},{512,256},{768,512},{1,769},{257,1},{513,257},{769... | collective-permute-start | bytes 786440 | tf_op jit(solution)/shard_map/ppermute | solution.py:315
  58.9 2.7 %collective-permute-start.3 = (bf16[32,16,256]{2,1,0:T(8,128)(2,1)S(1)}, bf16[32,16,256]{2,1,0:T(8,128)(2,1)S(1)}, u32[]{:S(2)}, u32[]{:S(2)}) collective-permute-start(bf16[32,16,256]{2,1,0:T(8,128)(2,1)S(1)} %pad_maximum_fusion.1), channel_id=1, source_target_pairs={{0,512},{256,768},{512,0},{768,256},{1,513},{257,769},{513,1},{769... | collective-permute-start | bytes 786440 | tf_op jit(solution)/shard_map/ppermute | solution.py:315
  61.6 2.8 %collective-permute-start.2 = (bf16[32,16,256]{2,1,0:T(8,128)(2,1)S(1)}, bf16[32,16,256]{2,1,0:T(8,128)(2,1)S(1)}, u32[]{:S(2)}, u32[]{:S(2)}) collective-permute-start(bf16[32,16,256]{2,1,0:T(8,128)(2,1)S(1)} %pad_maximum_fusion.1), channel_id=1, source_target_pairs={{0,256},{256,512},{512,768},{768,0},{1,257},{257,513},{513,769},{7... | collective-permute-start | bytes 786440 | tf_op jit(solution)/shard_map/ppermute | solution.py:315
  64.4 2.8 %collective-permute-done.4 = bf16[32,16,256]{2,1,0:T(8,128)(2,1)S(1)} collective-permute-done((bf16[32,16,256]{2,1,0:T(8,128)(2,1)S(1)}, bf16[32,16,256]{2,1,0:T(8,128)(2,1)S(1)}, u32[]{:S(2)}, u32[]{:S(2)}) %collective-permute-start.4) | collective-permute-done | bytes 262176 | tf_op jit(solution)/shard_map/ppermute | solution.py:315
  67.3 2.3 %collective-permute-done.3 = bf16[32,16,256]{2,1,0:T(8,128)(2,1)S(1)} collective-permute-done((bf16[32,16,256]{2,1,0:T(8,128)(2,1)S(1)}, bf16[32,16,256]{2,1,0:T(8,128)(2,1)S(1)}, u32[]{:S(2)}, u32[]{:S(2)}) %collective-permute-start.3) | collective-permute-done | bytes 262176 | tf_op jit(solution)/shard_map/ppermute | solution.py:315
  69.5 2.7 %collective-permute-done.2 = bf16[32,16,256]{2,1,0:T(8,128)(2,1)S(1)} collective-permute-done((bf16[32,16,256]{2,1,0:T(8,128)(2,1)S(1)}, bf16[32,16,256]{2,1,0:T(8,128)(2,1)S(1)}, u32[]{:S(2)}, u32[]{:S(2)}) %collective-permute-start.2) | collective-permute-done | bytes 262176 | tf_op jit(solution)/shard_map/ppermute | solution.py:315
  72.2 0.1 pad_maximum_fusion.own
  72.4 1.9 %collective-permute-start.5 = (bf16[4,32,16,256]{3,2,1,0:T(8,128)(2,1)S(1)}, bf16[4,32,16,256]{3,2,1,0:T(8,128)(2,1)}, u32[]{:S(2)}, u32[]{:S(2)}) collective-permute-start(bf16[4,32,16,256]{3,2,1,0:T(8,128)(2,1)S(1)} %pad_maximum_fusion.own), channel_id=1, source_target_pairs={{0,32},{32,0},{1,33},{33,1},{2,34},{34,2},{3,35},{35,3},{4,36},{36... | collective-permute-start | bytes 3145736 | tf_op jit(solution)/shard_map/ppermute | solution.py:315
  74.3 0.1 copy.16.labels
  74.4 1.0 fusion.3.bottom
  75.5 4.9 %shard_map.141.packed_hbm = bf16[10240,256]{1,0:T(8,128)(2,1)} custom-call(bf16[2304,256]{1,0:T(8,128)(2,1)} %down, bf16[256,2304]{1,0:T(8,128)(2,1)} %up, bf16[2304,512]{1,0:T(8,128)(2,1)} %top1, bf16[512,512]{1,0:T(8,128)(2,1)} %top2), custom_call_target="tpu_custom_call" | custom-call | bytes 10485760 | tf_op jit(solution)/shard_map/pallas_call | solution.py:226
  80.4 12.7 %all-to-all-done.1.counts = bf16[32,128,128]{2,1,0:T(8,128)(2,1)S(1)} async-done(((bf16[32,128,128]{2,1,0:T(8,128)(2,1)}), bf16[32,128,128]{2,1,0:T(8,128)(2,1)S(1)}, u32[]{:S(2)}, u32[]{:S(2)}) %all-to-all-start.1) | async-done | bytes 1048608 | tf_op jit(solution)/shard_map/all_to_all | solution.py:307
  93.1 10.7 %shard_map.142 = (bf16[2,4,2,16,16,256]{5,4,3,2,1,0:T(8,128)(2,1)S(1)}, f32[1,128]{1,0:T(1,128)}) custom-call(s32[4]{0:T(128)S(1)} %copy-done.1, s32[32]{0:T(128)S(1)} %copy-done.3, bf16[128,256]{1,0:T(8,128)(2,1)S(1)} %fusion.3.bottom, s32[128,1]{1,0:T(8,128)S(1)} %copy.16.labels, f32[1,512]{1,0:T(1,128)S(1)} %bitcast.28, ...), custom_call_target="tpu_custom_call" | custom-call | flops 4000000000 | bytes 12582912 | tf_op jit(solution)/shard_map/pallas_call | solution.py:182
  103.8 5.4 %all_to_all.25.halves = bf16[2,2048,256]{2,1,0:T(8,128)(2,1)S(1)} all-to-all(bf16[2,2048,256]{2,1,0:T(8,128)(2,1)S(1)} %bitcast.27), channel_id=1, replica_groups=mesh['x'=4,'yh'=4,'c'=2,'z'=16,'yl'=2] {'c'}, dimensions={0} | all-to-all | bytes 4194304 | tf_op jit(solution)/shard_map/all_to_all | solution.py:307
  109.2 0.8 shard_map.143
  110.0 20.4 %all_to_all.26.parts = bf16[8,256,256]{2,1,0:T(8,128)(2,1)S(1)} all-to-all(bf16[8,256,256]{2,1,0:T(8,128)(2,1)S(1)} %bitcast.26), channel_id=1, replica_groups=mesh['x'=4,'yh'=4,'c'=2,'z'=16,'yl'=2] {'x','yl'}, dimensions={0} | all-to-all | bytes 2097152 | tf_op jit(solution)/shard_map/all_to_all | solution.py:307
  130.5 0.9 shard_map.144
  131.4 26.0 %all_to_all.27 = bf16[64,4,256]{2,1,0:T(4,128)(2,1)S(1)} all-to-all(bf16[64,4,256]{2,1,0:T(4,128)(2,1)S(1)} %reshape.36), channel_id=1, replica_groups=mesh['x'=4,'yh'=4,'c'=2,'z'=16,'yl'=2] {'yh','z'}, dimensions={0} | all-to-all | bytes 262144 | tf_op jit(solution)/shard_map/all_to_all | solution.py:307
  157.4 0.7 convert_reduce_fusion
  (20 shorter events, 0.3 us)
Async XLA Ops:
  0.6 1.2 copy-start
  3.1 31.6 %all-to-all-start = ((bf16[16,8,256]{2,1,0:T(8,128)(2,1)}), bf16[16,8,256]{2,1,0:T(8,128)(2,1)S(1)}, u32[]{:S(2)}, u32[]{:S(2)}) async-start(bf16[16,8,256]{2,1,0:T(8,128)(2,1)} %broadcast_in_dim.8), calls=%async_computation | async-start | bytes 131072 | tf_op jit(solution)/shard_map/all_to_all | solution.py:307
  34.7 39.6 %copy-start.6 = (s32[128]{0:T(128)S(1)}, s32[128]{0:T(128)}, u32[]{:S(2)}) copy-start(s32[128]{0:T(128)} %param.18) | copy-start | bytes 1540
  34.7 39.8 %copy-start.4 = (bf16[512,256]{1,0:T(8,128)(2,1)S(1)}, bf16[512,256]{1,0:T(8,128)(2,1)}, u32[]{:S(2)}) copy-start(bf16[512,256]{1,0:T(8,128)(2,1)} %param.20) | copy-start | bytes 786436
  34.7 39.8 %copy-start.5 = (bf16[13,512]{1,0:T(8,128)(2,1)S(1)}, bf16[13,512]{1,0:T(8,128)(2,1)}, u32[]{:S(2)}) copy-start(bf16[13,512]{1,0:T(8,128)(2,1)} %param.19) | copy-start | bytes 39940
  34.7 58.4 %all-to-all-start.1 = ((bf16[32,128,128]{2,1,0:T(8,128)(2,1)}), bf16[32,128,128]{2,1,0:T(8,128)(2,1)S(1)}, u32[]{:S(2)}, u32[]{:S(2)}) async-start(bf16[32,128,128]{2,1,0:T(8,128)(2,1)} %bitcast.29), calls=%async_computation.1 | async-start | bytes 2097152 | tf_op jit(solution)/shard_map/all_to_all | solution.py:307
  39.3 6.6 %collective-permute-start = (bf16[16,8,256]{2,1,0:T(8,128)(2,1)S(1)}, bf16[16,8,256]{2,1,0:T(8,128)(2,1)S(1)}, u32[]{:S(2)}, u32[]{:S(2)}) collective-permute-start(bf16[16,8,256]{2,1,0:T(8,128)(2,1)S(1)} %all-to-all-done), channel_id=1, source_target_pairs={{0,1},{1,0},{2,3},{3,2},{4,5},{5,4},{6,7},{7,6},{8,9},{9,8},{10,11... | collective-permute-start | bytes 196616 | tf_op jit(solution)/shard_map/ppermute | solution.py:315
  45.9 8.3 %collective-permute-start.1 = (bf16[32,8,256]{2,1,0:T(8,128)(2,1)S(1)}, bf16[32,8,256]{2,1,0:T(8,128)(2,1)S(1)}, u32[]{:S(2)}, u32[]{:S(2)}) collective-permute-start(bf16[32,8,256]{2,1,0:T(8,128)(2,1)S(1)} %bitcast.31), channel_id=1, source_target_pairs={{0,64},{64,0},{128,192},{192,128},{1,65},{65,1},{129,193},{193,129... | collective-permute-start | bytes 393224 | tf_op jit(solution)/shard_map/ppermute | solution.py:346
  54.2 13.0 %collective-permute-start.4 = (bf16[32,16,256]{2,1,0:T(8,128)(2,1)S(1)}, bf16[32,16,256]{2,1,0:T(8,128)(2,1)S(1)}, u32[]{:S(2)}, u32[]{:S(2)}) collective-permute-start(bf16[32,16,256]{2,1,0:T(8,128)(2,1)S(1)} %pad_maximum_fusion.1), channel_id=1, source_target_pairs={{0,768},{256,0},{512,256},{768,512},{1,769},{257,1},{513,257},{769... | collective-permute-start | bytes 786440 | tf_op jit(solution)/shard_map/ppermute | solution.py:315
  58.9 10.6 %collective-permute-start.3 = (bf16[32,16,256]{2,1,0:T(8,128)(2,1)S(1)}, bf16[32,16,256]{2,1,0:T(8,128)(2,1)S(1)}, u32[]{:S(2)}, u32[]{:S(2)}) collective-permute-start(bf16[32,16,256]{2,1,0:T(8,128)(2,1)S(1)} %pad_maximum_fusion.1), channel_id=1, source_target_pairs={{0,512},{256,768},{512,0},{768,256},{1,513},{257,769},{513,1},{769... | collective-permute-start | bytes 786440 | tf_op jit(solution)/shard_map/ppermute | solution.py:315
  61.6 10.6 %collective-permute-start.2 = (bf16[32,16,256]{2,1,0:T(8,128)(2,1)S(1)}, bf16[32,16,256]{2,1,0:T(8,128)(2,1)S(1)}, u32[]{:S(2)}, u32[]{:S(2)}) collective-permute-start(bf16[32,16,256]{2,1,0:T(8,128)(2,1)S(1)} %pad_maximum_fusion.1), channel_id=1, source_target_pairs={{0,256},{256,512},{512,768},{768,0},{1,257},{257,513},{513,769},{7... | collective-permute-start | bytes 786440 | tf_op jit(solution)/shard_map/ppermute | solution.py:315
  72.4 8.0 %collective-permute-start.5 = (bf16[4,32,16,256]{3,2,1,0:T(8,128)(2,1)S(1)}, bf16[4,32,16,256]{3,2,1,0:T(8,128)(2,1)}, u32[]{:S(2)}, u32[]{:S(2)}) collective-permute-start(bf16[4,32,16,256]{3,2,1,0:T(8,128)(2,1)S(1)} %pad_maximum_fusion.own), channel_id=1, source_target_pairs={{0,32},{32,0},{1,33},{33,1},{2,34},{34,2},{3,35},{35,3},{4,36},{36... | collective-permute-start | bytes 3145736 | tf_op jit(solution)/shard_map/ppermute | solution.py:315
  75.5 17.6 %copy-start.1 = (s32[4]{0:T(128)S(1)}, s32[4]{0:T(128)}, u32[]{:S(2)}) copy-start(s32[4]{0:T(128)} %pad_add_fusion.place._) | copy-start | bytes 52
  75.5 17.6 %copy-start.2 = (f32[512]{0:T(512)S(1)}, f32[512]{0:T(512)}, u32[]{:S(2)}) copy-start(f32[512]{0:T(512)} %param.25) | copy-start | bytes 6148
  75.5 17.6 %copy-start.3 = (s32[32]{0:T(128)S(1)}, s32[32]{0:T(128)}, u32[]{:S(2)}) copy-start(s32[32]{0:T(128)} %table_of.1) | copy-start | bytes 388

commit v9 on v8

--- a/solution.py
+++ b/solution.py
@@ -172,7 +172,7 @@
                 grads[c, x, m % YL, m // YL] = terms[at : at + 16]
         return carry
 
-    lax.fori_loop(0, SHARDS, one_shard, 0, unroll=8)
+    lax.fori_loop(0, SHARDS, one_shard, 0, unroll=32)
 
 
 def run_step(place, table_of, small, packed):
@@ -275,22 +275,24 @@
 
 
 def sum_kernel(place, parts, out):
-    to = lax.broadcasted_iota(jnp.int32, (E, E), 0)
-    at = lax.broadcasted_iota(jnp.int32, (E, E), 1)
-    yh = to // 64
-    turned = (
-        at == (to // 4 % Z) * 16 + ((place[1] + yh) % 2) * 8 + (yh // 2) * 4 + to % 4
-    ).astype(BF)
+    to = lax.broadcasted_iota(jnp.int32, (2 * E, E), 0)
+    at = lax.broadcasted_iota(jnp.int32, (2 * E, E), 1)
+    half, row = to % 2, to // 2
+    yh = row // 64
+    source = (row // 4 % Z) * 16 + ((place[1] + yh) % 2) * 8 + (yh // 2) * 4 + row % 4
     total = parts[0].astype(F32)
     for i in range(1, parts.shape[0]):
         total = total + parts[i].astype(F32)
-    out[...] = dot(turned, total.astype(BF)).astype(BF)
-
-
-def fold(kernel, place, parts):
+    total = total.astype(BF)
+    left = dot(((at == source) & (half == 0)).astype(BF), total[:, :LOOK])
+    right = dot(((at == source) & (half == 1)).astype(BF), total[:, LOOK:])
+    out[...] = (left + right).astype(BF)
+
+
+def fold(kernel, place, parts, shape):
     return pl.pallas_call(
         kernel,
-        out_shape=jax.ShapeDtypeStruct(parts.shape[1:], BF),
+        out_shape=jax.ShapeDtypeStruct(shape, BF),
         in_specs=[
             pl.BlockSpec(memory_space=pltpu.SMEM),
             pl.BlockSpec(memory_space=pltpu.VMEM),
@@ -363,9 +365,9 @@
         packed,
     )
     grads = swap(grads.reshape(CORES, X * YL * Z * 16, E), "c")
-    grads = fold(pair_kernel, place, grads).reshape(X * YL, Z * 16, E)
-    grads = fold(sum_kernel, place, swap(grads, ("x", "yl"))).reshape(YH * Z, 4, E)
-    grads = add_up(swap(grads, ("yh", "z")))
+    grads = fold(pair_kernel, place, grads, grads.shape[1:]).reshape(X * YL, Z * 16, E)
+    grads = fold(sum_kernel, place, swap(grads, ("x", "yl")), (2 * E, LOOK))
+    grads = add_up(swap(grads.reshape(YH * Z, 8, LOOK), ("yh", "z"))).reshape(4, E)
     return grads, logits.reshape(N)
 
 

time: 159 us -> 158 us (level)
  no operation moved by 1% of the time
where the time goes in v9:
time: 158 us; the launch traced here: 157 us
  blocking collectives  51.8 us (33%)
  starting transfers between devices  42.3 us (27%)
  waiting for transfers between devices  38.1 us (24%)
  Pallas kernels  19.4 us (12%)
  local copies, waits for them, and re-layouts  3.07 us (2%)
    all_to_all x3, blocking collectives, swap(): return lax.all_to_all(value, axes, split_axis=0, concat_axis=0, tiled=True)  51.8 us
    all_to_all x2, starting transfers between devices, swap(): return lax.all_to_all(value, axes, split_axis=0, concat_axis=0, tiled=True)  23.5 us
    all_to_all x2, waiting for transfers between devices, swap(): return lax.all_to_all(value, axes, split_axis=0, concat_axis=0, tiled=True)  22 us
    ppermute x5, starting transfers between devices, turn(): lax.ppermute(value, axis, [(i, (i + shift) % size) for i in range(size)])  14.2 us
    ppermute x5, waiting for transfers between devices, turn(): lax.ppermute(value, axis, [(i, (i + shift) % size) for i in range(size)])  12.3 us
    pallas_call x1, Pallas kernels, run_step(): pl.pallas_call(step_kernel, out_shape=(jax.ShapeDtypeStruct((CORES, X, YL...  9.93 us
    pallas_call x1, Pallas kernels, pack(): pl.pallas_call(pack_kernel, out_shape=jax.ShapeDtypeStruct((PACKED, E), B...  4.91 us
    ppermute x1, starting transfers between devices, shards(): exchanged = lax.ppermute(looked, 'yh', [(i, i ^ 1) for i in range(YH)])  4.5 us
  transfers between devices with their start and end apart: 8, of which 7 were waited for; matrix products, arithmetic and copies ran while one was open for 1% of the time, Pallas kernels for 5%

profile of v9, /device:TPU:8, one launch (start us, length us, event | category | flops | bytes accessed | tf_op | source)
XLA Modules:
  0.0 157.4 jit_solution(7674713221800104940)
XLA Ops:
  0.7 0.8 constant_dynamic-slice_fusion
  1.6 0.2 copy-done
  1.9 0.6 gather_fusion
  2.4 0.6 broadcast_in_dim.8
  3.1 18.9 %all-to-all-start = ((bf16[16,8,256]{2,1,0:T(8,128)(2,1)}), bf16[16,8,256]{2,1,0:T(8,128)(2,1)S(1)}, u32[]{:S(2)}, u32[]{:S(2)}) async-start(bf16[16,8,256]{2,1,0:T(8,128)(2,1)} %broadcast_in_dim.8), calls=%async_computation | async-start | bytes 131072 | tf_op jit(solution)/shard_map/all_to_all | solution.py:309
  21.9 0.6 pad_add_fusion.place._
  22.6 2.7 %shard_map.140 = bf16[4096,128]{1,0:T(8,128)(2,1)} custom-call(s32[4]{0:T(128)} %pad_add_fusion.place._, s32[4096,128]{1,0:T(8,128)} %counts), custom_call_target="tpu_custom_call" | custom-call | flops 200000000 | bytes 3145728 | tf_op jit(solution)/shard_map/pallas_call | solution.py:252
  25.3 9.4 %all-to-all-done = bf16[16,8,256]{2,1,0:T(8,128)(2,1)S(1)} async-done(((bf16[16,8,256]{2,1,0:T(8,128)(2,1)}), bf16[16,8,256]{2,1,0:T(8,128)(2,1)S(1)}, u32[]{:S(2)}, u32[]{:S(2)}) %all-to-all-start) | async-done | bytes 65568 | tf_op jit(solution)/shard_map/all_to_all | solution.py:309
  34.7 4.7 %all-to-all-start.1 = ((bf16[32,128,128]{2,1,0:T(8,128)(2,1)}), bf16[32,128,128]{2,1,0:T(8,128)(2,1)S(1)}, u32[]{:S(2)}, u32[]{:S(2)}) async-start(bf16[32,128,128]{2,1,0:T(8,128)(2,1)} %bitcast.31), calls=%async_computation.1 | async-start | bytes 2097152 | tf_op jit(solution)/shard_map/all_to_all | solution.py:309
  39.3 2.1 %collective-permute-start = (bf16[16,8,256]{2,1,0:T(8,128)(2,1)S(1)}, bf16[16,8,256]{2,1,0:T(8,128)(2,1)S(1)}, u32[]{:S(2)}, u32[]{:S(2)}) collective-permute-start(bf16[16,8,256]{2,1,0:T(8,128)(2,1)S(1)} %all-to-all-done), channel_id=1, source_target_pairs={{0,1},{1,0},{2,3},{3,2},{4,5},{5,4},{6,7},{7,6},{8,9},{9,8},{10,11... | collective-permute-start | bytes 196616 | tf_op jit(solution)/shard_map/ppermute | solution.py:317
  41.5 4.4 %collective-permute-done = bf16[16,8,256]{2,1,0:T(8,128)(2,1)S(1)} collective-permute-done((bf16[16,8,256]{2,1,0:T(8,128)(2,1)S(1)}, bf16[16,8,256]{2,1,0:T(8,128)(2,1)S(1)}, u32[]{:S(2)}, u32[]{:S(2)}) %collective-permute-start) | collective-permute-done | bytes 65568 | tf_op jit(solution)/shard_map/ppermute | solution.py:317
  45.9 4.5 %collective-permute-start.1 = (bf16[32,8,256]{2,1,0:T(8,128)(2,1)S(1)}, bf16[32,8,256]{2,1,0:T(8,128)(2,1)S(1)}, u32[]{:S(2)}, u32[]{:S(2)}) collective-permute-start(bf16[32,8,256]{2,1,0:T(8,128)(2,1)S(1)} %bitcast.33), channel_id=1, source_target_pairs={{0,64},{64,0},{128,192},{192,128},{1,65},{65,1},{129,193},{193,129... | collective-permute-start | bytes 393224 | tf_op jit(solution)/shard_map/ppermute | solution.py:348
  50.4 3.8 %collective-permute-done.1 = bf16[32,8,256]{2,1,0:T(8,128)(2,1)S(1)} collective-permute-done((bf16[32,8,256]{2,1,0:T(8,128)(2,1)S(1)}, bf16[32,8,256]{2,1,0:T(8,128)(2,1)S(1)}, u32[]{:S(2)}, u32[]{:S(2)}) %collective-permute-start.1) | collective-permute-done | bytes 131104 | tf_op jit(solution)/shard_map/ppermute | solution.py:348
  54.2 4.7 %collective-permute-start.4 = (bf16[32,16,256]{2,1,0:T(8,128)(2,1)S(1)}, bf16[32,16,256]{2,1,0:T(8,128)(2,1)S(1)}, u32[]{:S(2)}, u32[]{:S(2)}) collective-permute-start(bf16[32,16,256]{2,1,0:T(8,128)(2,1)S(1)} %pad_maximum_fusion.1), channel_id=1, source_target_pairs={{0,768},{256,0},{512,256},{768,512},{1,769},{257,1},{513,257},{769... | collective-permute-start | bytes 786440 | tf_op jit(solution)/shard_map/ppermute | solution.py:317
  58.9 2.7 %collective-permute-start.3 = (bf16[32,16,256]{2,1,0:T(8,128)(2,1)S(1)}, bf16[32,16,256]{2,1,0:T(8,128)(2,1)S(1)}, u32[]{:S(2)}, u32[]{:S(2)}) collective-permute-start(bf16[32,16,256]{2,1,0:T(8,128)(2,1)S(1)} %pad_maximum_fusion.1), channel_id=1, source_target_pairs={{0,512},{256,768},{512,0},{768,256},{1,513},{257,769},{513,1},{769... | collective-permute-start | bytes 786440 | tf_op jit(solution)/shard_map/ppermute | solution.py:317
  61.6 2.8 %collective-permute-start.2 = (bf16[32,16,256]{2,1,0:T(8,128)(2,1)S(1)}, bf16[32,16,256]{2,1,0:T(8,128)(2,1)S(1)}, u32[]{:S(2)}, u32[]{:S(2)}) collective-permute-start(bf16[32,16,256]{2,1,0:T(8,128)(2,1)S(1)} %pad_maximum_fusion.1), channel_id=1, source_target_pairs={{0,256},{256,512},{512,768},{768,0},{1,257},{257,513},{513,769},{7... | collective-permute-start | bytes 786440 | tf_op jit(solution)/shard_map/ppermute | solution.py:317
  64.4 2.8 %collective-permute-done.4 = bf16[32,16,256]{2,1,0:T(8,128)(2,1)S(1)} collective-permute-done((bf16[32,16,256]{2,1,0:T(8,128)(2,1)S(1)}, bf16[32,16,256]{2,1,0:T(8,128)(2,1)S(1)}, u32[]{:S(2)}, u32[]{:S(2)}) %collective-permute-start.4) | collective-permute-done | bytes 262176 | tf_op jit(solution)/shard_map/ppermute | solution.py:317
  67.3 2.3 %collective-permute-done.3 = bf16[32,16,256]{2,1,0:T(8,128)(2,1)S(1)} collective-permute-done((bf16[32,16,256]{2,1,0:T(8,128)(2,1)S(1)}, bf16[32,16,256]{2,1,0:T(8,128)(2,1)S(1)}, u32[]{:S(2)}, u32[]{:S(2)}) %collective-permute-start.3) | collective-permute-done | bytes 262176 | tf_op jit(solution)/shard_map/ppermute | solution.py:317
  69.5 2.7 %collective-permute-done.2 = bf16[32,16,256]{2,1,0:T(8,128)(2,1)S(1)} collective-permute-done((bf16[32,16,256]{2,1,0:T(8,128)(2,1)S(1)}, bf16[32,16,256]{2,1,0:T(8,128)(2,1)S(1)}, u32[]{:S(2)}, u32[]{:S(2)}) %collective-permute-start.2) | collective-permute-done | bytes 262176 | tf_op jit(solution)/shard_map/ppermute | solution.py:317
  72.2 0.1 pad_maximum_fusion.own
  72.4 1.9 %collective-permute-start.5 = (bf16[4,32,16,256]{3,2,1,0:T(8,128)(2,1)S(1)}, bf16[4,32,16,256]{3,2,1,0:T(8,128)(2,1)}, u32[]{:S(2)}, u32[]{:S(2)}) collective-permute-start(bf16[4,32,16,256]{3,2,1,0:T(8,128)(2,1)S(1)} %pad_maximum_fusion.own), channel_id=1, source_target_pairs={{0,32},{32,0},{1,33},{33,1},{2,34},{34,2},{3,35},{35,3},{4,36},{36... | collective-permute-start | bytes 3145736 | tf_op jit(solution)/shard_map/ppermute | solution.py:317
  74.3 0.1 copy.16.labels
  74.4 1.0 fusion.3.bottom
  75.5 4.9 %shard_map.141.packed_hbm = bf16[10240,256]{1,0:T(8,128)(2,1)} custom-call(bf16[2304,256]{1,0:T(8,128)(2,1)} %down, bf16[256,2304]{1,0:T(8,128)(2,1)} %up, bf16[2304,512]{1,0:T(8,128)(2,1)} %top1, bf16[512,512]{1,0:T(8,128)(2,1)} %top2), custom_call_target="tpu_custom_call" | custom-call | bytes 10485760 | tf_op jit(solution)/shard_map/pallas_call | solution.py:226
  80.4 12.7 %all-to-all-done.1.counts = bf16[32,128,128]{2,1,0:T(8,128)(2,1)S(1)} async-done(((bf16[32,128,128]{2,1,0:T(8,128)(2,1)}), bf16[32,128,128]{2,1,0:T(8,128)(2,1)S(1)}, u32[]{:S(2)}, u32[]{:S(2)}) %all-to-all-start.1) | async-done | bytes 1048608 | tf_op jit(solution)/shard_map/all_to_all | solution.py:309
  93.1 9.9 %shard_map.142 = (bf16[2,4,2,16,16,256]{5,4,3,2,1,0:T(8,128)(2,1)S(1)}, f32[1,128]{1,0:T(1,128)}) custom-call(s32[4]{0:T(128)S(1)} %copy-done.1, s32[32]{0:T(128)S(1)} %copy-done.3, bf16[128,256]{1,0:T(8,128)(2,1)S(1)} %fusion.3.bottom, s32[128,1]{1,0:T(8,128)S(1)} %copy.16.labels, f32[1,512]{1,0:T(1,128)S(1)} %bitcast.30, ...), custom_call_target="tpu_custom_call" | custom-call | flops 4000000000 | bytes 12582912 | tf_op jit(solution)/shard_map/pallas_call | solution.py:182
  103.0 5.4 %all_to_all.25.halves = bf16[2,2048,256]{2,1,0:T(8,128)(2,1)S(1)} all-to-all(bf16[2,2048,256]{2,1,0:T(8,128)(2,1)S(1)} %bitcast.28), channel_id=1, replica_groups=mesh['x'=4,'yh'=4,'c'=2,'z'=16,'yl'=2] {'c'}, dimensions={0} | all-to-all | bytes 4194304 | tf_op jit(solution)/shard_map/all_to_all | solution.py:309
  108.4 0.8 shard_map.143
  109.2 20.4 %all_to_all.26.parts = bf16[8,256,256]{2,1,0:T(8,128)(2,1)S(1)} all-to-all(bf16[8,256,256]{2,1,0:T(8,128)(2,1)S(1)} %bitcast.27), channel_id=1, replica_groups=mesh['x'=4,'yh'=4,'c'=2,'z'=16,'yl'=2] {'x','yl'}, dimensions={0} | all-to-all | bytes 2097152 | tf_op jit(solution)/shard_map/all_to_all | solution.py:309
  129.7 1.1 shard_map.144
  130.8 26.0 %all_to_all.27 = bf16[64,8,128]{2,1,0:T(8,128)(2,1)S(1)} all-to-all(bf16[64,8,128]{2,1,0:T(8,128)(2,1)S(1)} %bitcast.29), channel_id=1, replica_groups=mesh['x'=4,'yh'=4,'c'=2,'z'=16,'yl'=2] {'yh','z'}, dimensions={0} | all-to-all | bytes 262144 | tf_op jit(solution)/shard_map/all_to_all | solution.py:309
  156.8 0.6 reshape.40
  (20 shorter events, 0.3 us)
Async XLA Ops:
  0.6 1.2 copy-start
  3.1 31.6 %all-to-all-start = ((bf16[16,8,256]{2,1,0:T(8,128)(2,1)}), bf16[16,8,256]{2,1,0:T(8,128)(2,1)S(1)}, u32[]{:S(2)}, u32[]{:S(2)}) async-start(bf16[16,8,256]{2,1,0:T(8,128)(2,1)} %broadcast_in_dim.8), calls=%async_computation | async-start | bytes 131072 | tf_op jit(solution)/shard_map/all_to_all | solution.py:309
  34.7 39.6 %copy-start.6 = (s32[128]{0:T(128)S(1)}, s32[128]{0:T(128)}, u32[]{:S(2)}) copy-start(s32[128]{0:T(128)} %param.18) | copy-start | bytes 1540
  34.7 39.8 %copy-start.4 = (bf16[512,256]{1,0:T(8,128)(2,1)S(1)}, bf16[512,256]{1,0:T(8,128)(2,1)}, u32[]{:S(2)}) copy-start(bf16[512,256]{1,0:T(8,128)(2,1)} %param.20) | copy-start | bytes 786436
  34.7 39.8 %copy-start.5 = (bf16[13,512]{1,0:T(8,128)(2,1)S(1)}, bf16[13,512]{1,0:T(8,128)(2,1)}, u32[]{:S(2)}) copy-start(bf16[13,512]{1,0:T(8,128)(2,1)} %param.19) | copy-start | bytes 39940
  34.7 58.4 %all-to-all-start.1 = ((bf16[32,128,128]{2,1,0:T(8,128)(2,1)}), bf16[32,128,128]{2,1,0:T(8,128)(2,1)S(1)}, u32[]{:S(2)}, u32[]{:S(2)}) async-start(bf16[32,128,128]{2,1,0:T(8,128)(2,1)} %bitcast.31), calls=%async_computation.1 | async-start | bytes 2097152 | tf_op jit(solution)/shard_map/all_to_all | solution.py:309
  39.3 6.6 %collective-permute-start = (bf16[16,8,256]{2,1,0:T(8,128)(2,1)S(1)}, bf16[16,8,256]{2,1,0:T(8,128)(2,1)S(1)}, u32[]{:S(2)}, u32[]{:S(2)}) collective-permute-start(bf16[16,8,256]{2,1,0:T(8,128)(2,1)S(1)} %all-to-all-done), channel_id=1, source_target_pairs={{0,1},{1,0},{2,3},{3,2},{4,5},{5,4},{6,7},{7,6},{8,9},{9,8},{10,11... | collective-permute-start | bytes 196616 | tf_op jit(solution)/shard_map/ppermute | solution.py:317
  45.9 8.3 %collective-permute-start.1 = (bf16[32,8,256]{2,1,0:T(8,128)(2,1)S(1)}, bf16[32,8,256]{2,1,0:T(8,128)(2,1)S(1)}, u32[]{:S(2)}, u32[]{:S(2)}) collective-permute-start(bf16[32,8,256]{2,1,0:T(8,128)(2,1)S(1)} %bitcast.33), channel_id=1, source_target_pairs={{0,64},{64,0},{128,192},{192,128},{1,65},{65,1},{129,193},{193,129... | collective-permute-start | bytes 393224 | tf_op jit(solution)/shard_map/ppermute | solution.py:348
  54.2 13.0 %collective-permute-start.4 = (bf16[32,16,256]{2,1,0:T(8,128)(2,1)S(1)}, bf16[32,16,256]{2,1,0:T(8,128)(2,1)S(1)}, u32[]{:S(2)}, u32[]{:S(2)}) collective-permute-start(bf16[32,16,256]{2,1,0:T(8,128)(2,1)S(1)} %pad_maximum_fusion.1), channel_id=1, source_target_pairs={{0,768},{256,0},{512,256},{768,512},{1,769},{257,1},{513,257},{769... | collective-permute-start | bytes 786440 | tf_op jit(solution)/shard_map/ppermute | solution.py:317
  58.9 10.6 %collective-permute-start.3 = (bf16[32,16,256]{2,1,0:T(8,128)(2,1)S(1)}, bf16[32,16,256]{2,1,0:T(8,128)(2,1)S(1)}, u32[]{:S(2)}, u32[]{:S(2)}) collective-permute-start(bf16[32,16,256]{2,1,0:T(8,128)(2,1)S(1)} %pad_maximum_fusion.1), channel_id=1, source_target_pairs={{0,512},{256,768},{512,0},{768,256},{1,513},{257,769},{513,1},{769... | collective-permute-start | bytes 786440 | tf_op jit(solution)/shard_map/ppermute | solution.py:317
  61.6 10.6 %collective-permute-start.2 = (bf16[32,16,256]{2,1,0:T(8,128)(2,1)S(1)}, bf16[32,16,256]{2,1,0:T(8,128)(2,1)S(1)}, u32[]{:S(2)}, u32[]{:S(2)}) collective-permute-start(bf16[32,16,256]{2,1,0:T(8,128)(2,1)S(1)} %pad_maximum_fusion.1), channel_id=1, source_target_pairs={{0,256},{256,512},{512,768},{768,0},{1,257},{257,513},{513,769},{7... | collective-permute-start | bytes 786440 | tf_op jit(solution)/shard_map/ppermute | solution.py:317
  72.4 8.0 %collective-permute-start.5 = (bf16[4,32,16,256]{3,2,1,0:T(8,128)(2,1)S(1)}, bf16[4,32,16,256]{3,2,1,0:T(8,128)(2,1)}, u32[]{:S(2)}, u32[]{:S(2)}) collective-permute-start(bf16[4,32,16,256]{3,2,1,0:T(8,128)(2,1)S(1)} %pad_maximum_fusion.own), channel_id=1, source_target_pairs={{0,32},{32,0},{1,33},{33,1},{2,34},{34,2},{3,35},{35,3},{4,36},{36... | collective-permute-start | bytes 3145736 | tf_op jit(solution)/shard_map/ppermute | solution.py:317
  75.5 17.6 %copy-start.1 = (s32[4]{0:T(128)S(1)}, s32[4]{0:T(128)}, u32[]{:S(2)}) copy-start(s32[4]{0:T(128)} %pad_add_fusion.place._) | copy-start | bytes 52
  75.5 17.6 %copy-start.2 = (f32[512]{0:T(512)S(1)}, f32[512]{0:T(512)}, u32[]{:S(2)}) copy-start(f32[512]{0:T(512)} %param.25) | copy-start | bytes 6148
  75.5 17.6 %copy-start.3 = (s32[32]{0:T(128)S(1)}, s32[32]{0:T(128)}, u32[]{:S(2)}) copy-start(s32[32]{0:T(128)} %table_of.1) | copy-start | bytes 388
